TPU v7x, 32 devices: a whole 2x2x4 slice. The times are simulated.
32 devices in a mesh: gy: 4 (over z), gx: 8 (over y, x, core).
Axes of the slice: x: 2, y: 2, z: 4, core: 2. Of those that a mesh axis runs over, the one named last changes fastest.
Arguments:
- mask: float32 [160, 1024], P('gy', 'gx'), may hold values from 0 to 1
- target: int32 [160, 1024], P('gy', 'gx'), may hold values 0 or 1
- kernels: bfloat16 [24, 35, 35], replicated, may hold values from -0.15625 to 0.15625
- offsets: int32 [8, 2], replicated, may hold values from -8 to 8, as said below
- load_weights: float32 [8], replicated, may hold values from 0.2 to 1
Outputs:
- update: float32 [160, 1024], P('gy', 'gx')
- loss: float32 [], replicated
Inputs may be any that keep to these rules, and one draw needn't show every extreme that they name: `offsets`: some offset has row component 8 and some has column component -8.
All inputs are finite; a program needn't handle non-finite values. No bound on the sum of `target` on one device may be relied on, other than what follows from the above.
Results may differ from a plain program's by a relative error of at most 0.002.
Values may be sent and summed in bfloat16 or wider, within the bound.
No kernel may reach another device: no remote copies, remote signals or barrier semaphores. Data moves between devices by JAX's collectives and lax.ppermute only.
A program may use at most 64 MiB of HBM per device.

v0:
```python
import jax
import jax.numpy as jnp
from jax import lax
from jax.sharding import PartitionSpec as P

KERNELS = 12
REACH = 8
LOAD_TAPS = 8


SMOOTH_TAPS = (0.0625, 0.25, 0.375, 0.25, 0.0625)
SHARPNESS = 4.0
THRESHOLD = 0.65
LOADING_GAIN = 0.5
ROW_BLOCK = 8


def with_halo(block, sides, width):
    for axis, dim in sides:
        count = lax.axis_size(axis)
        forward = [(i, i + 1) for i in range(count - 1)]
        backward = [(target, source) for source, target in forward]
        low = lax.ppermute(
            lax.slice_in_dim(block, block.shape[dim] - width, None, axis=dim), axis, forward
        )
        high = lax.ppermute(lax.slice_in_dim(block, 0, width, axis=dim), axis, backward)
        block = jnp.concatenate([low, block, high], axis=dim)
    return block


def smooth_valid(padded, out_rows, out_cols):
    partial_rows = sum((SMOOTH_TAPS[a] * padded[a : a + out_rows, :] for a in range(5)))
    return sum((SMOOTH_TAPS[b] * partial_rows[:, b : b + out_cols] for b in range(5)))


def forward_field(extended, kernels, out_rows, out_cols):
    channels, taps = (kernels.shape[0], kernels.shape[1])
    blocks = -(-out_rows // ROW_BLOCK)
    flat_kernels = kernels.reshape(channels, taps * taps)

    def one_block(block_index, total):
        start = block_index * ROW_BLOCK
        band = lax.dynamic_slice_in_dim(extended, start, ROW_BLOCK + taps - 1, 0)
        across = jnp.stack([band[:, b : b + out_cols] for b in range(taps)])
        patches = jnp.stack([across[:, a : a + ROW_BLOCK, :] for a in range(taps)])
        patches = patches.reshape(taps * taps, ROW_BLOCK, out_cols)
        piece = jnp.einsum("ck,kyx->cyx", flat_kernels, patches, preferred_element_type=jnp.float32)
        return lax.dynamic_update_slice_in_dim(total, piece, start, 1)

    empty = jnp.zeros((channels, blocks * ROW_BLOCK, out_cols), jnp.float32)
    result = lax.fori_loop(0, blocks, one_block, empty)
    return result


def adjoint_field(products, kernels, out_rows, out_cols):
    taps = kernels.shape[1]
    reach = 2 * (taps // 2)

    def one_row(tap_row, total):
        band = lax.dynamic_slice_in_dim(products, reach - tap_row, out_rows, 1)
        row_weights = lax.dynamic_index_in_dim(kernels, tap_row, 1, keepdims=False)
        mixed = jnp.einsum("cb,cyx->byx", row_weights, band, preferred_element_type=jnp.float32)
        return total + sum((mixed[b, :, reach - b : reach - b + out_cols] for b in range(taps)))

    empty = jnp.zeros((out_rows, out_cols), jnp.float32)
    return lax.fori_loop(0, taps, one_row, empty)


def inside_window(first, count, total):
    position = first + jnp.arange(count, dtype=jnp.int32)
    return (position >= 0) & (position < total)


def body(mask, target, kernels, offsets, load_weights):
    tile_rows, tile_cols = mask.shape
    radius = kernels.shape[-1] // 2
    margin = REACH + 2
    total_rows = tile_rows * lax.axis_size("gy")
    total_cols = tile_cols * lax.axis_size("gx")
    first_row = lax.axis_index("gy") * tile_rows
    first_col = lax.axis_index("gx") * tile_cols
    plane = mask.astype(jnp.bfloat16)
    extended = with_halo(plane, (("gy", 0), ("gx", 1)), radius)
    field = forward_field(extended, kernels, tile_rows, tile_cols)
    intensity = jnp.sum(field * field, axis=0) / KERNELS
    inten_ext = with_halo(intensity, (("gy", 0), ("gx", 1)), margin)
    dense = smooth_valid(inten_ext, tile_rows + 2 * REACH, tile_cols + 2 * REACH)
    inside = (
        inside_window(first_row - REACH, tile_rows + 2 * REACH, total_rows)[:, None]
        & inside_window(first_col - REACH, tile_cols + 2 * REACH, total_cols)[None, :]
    )
    develop = jnp.where(inside, jax.nn.sigmoid(SHARPNESS * (dense - THRESHOLD)), 0.0)
    loading = jnp.zeros((tile_rows, tile_cols), jnp.float32)
    for index in range(LOAD_TAPS):
        shifted = lax.dynamic_slice(
            develop, (REACH + offsets[index, 0], REACH + offsets[index, 1]), (tile_rows, tile_cols)
        )
        loading = loading + load_weights[index] * shifted
    center = develop[REACH : REACH + tile_rows, REACH : REACH + tile_cols]
    printed = center - LOADING_GAIN / LOAD_TAPS * loading
    row_pos = (first_row + jnp.arange(tile_rows, dtype=jnp.int32)).astype(jnp.float32)
    col_pos = (first_col + jnp.arange(tile_cols, dtype=jnp.int32)).astype(jnp.float32)
    weight = (1.0 + 2.0 * row_pos / total_rows)[:, None] * (1.0 + 2.0 * col_pos / total_cols)[
        None, :
    ]
    diff = printed - target.astype(jnp.float32)
    part_loss = jnp.sum(weight * diff * diff)
    resid = 2.0 * weight * diff
    resid_ext = with_halo(resid, (("gy", 0), ("gx", 1)), margin)
    back = jnp.zeros((tile_rows + 4, tile_cols + 4), jnp.float32)
    for index in range(LOAD_TAPS):
        shifted = lax.dynamic_slice(
            resid_ext,
            (REACH - offsets[index, 0], REACH - offsets[index, 1]),
            (tile_rows + 4, tile_cols + 4),
        )
        back = back + load_weights[index] * shifted
    slope = (
        resid_ext[REACH : REACH + tile_rows + 4, REACH : REACH + tile_cols + 4]
        - LOADING_GAIN / LOAD_TAPS * back
    )
    nearby = develop[REACH - 2 : REACH + tile_rows + 2, REACH - 2 : REACH + tile_cols + 2]
    inside_near = (
        inside_window(first_row - 2, tile_rows + 4, total_rows)[:, None]
        & inside_window(first_col - 2, tile_cols + 4, total_cols)[None, :]
    )
    dense_grad = jnp.where(inside_near, slope * SHARPNESS * nearby * (1.0 - nearby), 0.0)
    inten_grad = smooth_valid(dense_grad, tile_rows, tile_cols)
    products = (2.0 * field * inten_grad / KERNELS).astype(jnp.bfloat16)
    products = with_halo(products, (("gy", 1), ("gx", 2)), radius)
    gradient = adjoint_field(products, kernels, tile_rows, tile_cols)
    totals = lax.psum((part_loss, jnp.sum(gradient * gradient)), ("gy", "gx"))
    scale = jnp.sqrt(totals[1] / (total_rows * total_cols) + 1e-06)
    update = mask - gradient / scale
    return (update, totals[0])


def solution(mesh):
    return jax.shard_map(
        body,
        mesh=mesh,
        in_specs=(P("gy", "gx"), P("gy", "gx"), P(), P(), P()),
        out_specs=(P("gy", "gx"), P()),
        check_vma=False,
    )
```

profile of v0, /device:TPU:0, one launch (start us, length us, event | category | flops | bytes accessed | tf_op | source)
XLA Modules:
  0.0 294.9 jit_solution(6756470346671824055)
XLA Ops:
  1.4 4.9 %collective-permute-start = (bf16[17,128]{1,0:T(8,128)(2,1)S(1)}, bf16[17,128]{1,0:T(8,128)(2,1)S(1)}, u32[]{:S(2)}, u32[]{:S(2)}) collective-permute-start(bf16[17,128]{1,0:T(8,128)(2,1)S(1)} %get-tuple-element.277), channel_id=1, source_target_pairs={{0,8},{8,16},{16,24},{1,9},{9,17},{17,25},{2,10},{10,18},{18,26},{... | collective-permute-start | bytes 13064 | tf_op jit(solution)/shard_map/ppermute | solution.py:23
  6.3 1.3 collective-permute-start.1
  8.7 1.9 fusion.74
  10.6 1.6 fusion.75
  12.9 1.4 collective-permute-start.2
  14.3 1.3 collective-permute-start.3
  16.1 1.0 copy.78
  17.3 1.7 collective-permute-done.3
  19.1 24.7 %while.29 = (s32[]{:T(128)}, f32[24,40,128]{2,0,1:T(8,128)S(1)}, bf16[74,162]{1,0:T(8,128)(2,1)S(1)}, bf16[24,1225]{1,0:T(8,128)(2,1)S(1)}, s32[]{:T(128)}, /*in...) while((s32[]{:T(128)}, f32[24,40,128]{2,0,1:T(8,128)S(1)}, ...), condition=%wide.region_1.0_spmd, body=%wide.region_0.0_spmd.sunk | while | flops 60211240 | bytes 8545892 | solution.py:51
  44.0 4.5 %collective-permute-start.4 = (f32[10,128]{1,0:T(8,128)S(1)}, f32[10,128]{1,0:T(8,128)S(1)}, u32[]{:S(2)}, u32[]{:S(2)}) collective-permute-start(f32[10,128]{1,0:T(8,128)S(1)} %get-tuple-element.273), channel_id=1, source_target_pairs={{0,8},{8,16},{16,24},{1,9},{9,17},{17,25},{2,10},{10,18},{18,26},{... | collective-permute-start | bytes 15368 | tf_op jit(solution)/shard_map/ppermute | solution.py:23
  48.5 1.3 collective-permute-start.5
  69.8 4.1 %collective-permute-start.6 = (f32[60,10]{1,0:T(8,128)S(1)}, f32[60,10]{1,0:T(8,128)S(1)}, u32[]{:S(2)}, u32[]{:S(2)}) collective-permute-start(f32[60,10]{1,0:T(8,128)S(1)} %get-tuple-element.269), channel_id=1, source_target_pairs={{0,1},{1,2},{2,3},{3,4},{4,5},{5,6},{6,7},{8,9},{9,10},{10,11},{11... | collective-permute-start | bytes 7208 | tf_op jit(solution)/shard_map/ppermute | solution.py:23
  74.0 1.3 collective-permute-start.7
  75.4 1.7 collective-permute-done.7
  78.1 6.6 %fusion.56 = (f32[]{:T(128)}, f32[40,128]{1,0:T(8,128)S(1)}) fusion(f32[128]{0:T(128)} %multiply_add_fusion, f32[40]{0:T(128)} %multiply_add_fusion.1, s32[40,128]{1,0:T(8,128)S(1)} %copy-done.1, f32[56,144]{1,0:T(8,128)S(1)} %fusion.39, s32[]{:T(128)S(6)} %select_n.152, s32[]{:T(128)S(6)} %select_n.153, f32[]{:T(128)} %bitcast.108, s32[]{:T(128)S(6)} %select_n.150, ...), kind=kLoop, calls=%fused_computation.220 | loop fusion | flops 117759 | bytes 226052 | tf_op jit(solution)/shard_map/reduce_sum | solution.py:107
  85.5 4.5 %collective-permute-start.8 = (f32[10,128]{1,0:T(8,128)S(1)}, f32[10,128]{1,0:T(8,128)S(1)}, u32[]{:S(2)}, u32[]{:S(2)}) collective-permute-start(f32[10,128]{1,0:T(8,128)S(1)} %get-tuple-element.271), channel_id=1, source_target_pairs={{0,8},{8,16},{16,24},{1,9},{9,17},{17,25},{2,10},{10,18},{18,26},{... | collective-permute-start | bytes 15368 | tf_op jit(solution)/shard_map/ppermute | solution.py:23
  90.0 1.3 collective-permute-start.9
  111.4 4.2 %collective-permute-start.10 = (f32[60,10]{1,0:T(8,128)S(1)}, f32[60,10]{1,0:T(8,128)S(1)}, u32[]{:S(2)}, u32[]{:S(2)}) collective-permute-start(f32[60,10]{1,0:T(8,128)S(1)} %get-tuple-element.267), channel_id=1, source_target_pairs={{0,1},{1,2},{2,3},{3,4},{4,5},{5,6},{6,7},{8,9},{9,10},{10,11},{11... | collective-permute-start | bytes 7208 | tf_op jit(solution)/shard_map/ppermute | solution.py:23
  115.6 1.3 collective-permute-start.11
  117.1 1.7 collective-permute-done.11
  118.8 5.4 %fusion.50 = f32[44,132]{1,0:T(8,128)S(1)} fusion(f32[60,148]{1,0:T(8,128)S(1)} %pad_maximum_fusion.3, f32[56,144]{1,0:T(8,128)S(1)} %fusion.39, s32[]{:T(128)S(6)} %select_n.168, s32[]{:T(128)S(6)} %select_n.169, s32[]{:T(128)S(6)} %select_n.166, s32[]{:T(128)S(6)} %select_n.167, s32[]{:T(128)S(6)} %select_n.164, s32[]{:T(128)S(6)} %select_n.165, ...), kind=kLoop, calls=%fused_computation.204 | loop fusion | flops 133584 | bytes 255824 | tf_op jit(solution)/shard_map/jit(_where)/select_n | solution.py:127
  124.4 4.3 %collective-permute-start.12 = (bf16[24,17,128]{2,0,1:T(8,128)(2,1)S(1)}, bf16[24,17,128]{2,0,1:T(8,128)(2,1)S(1)}, u32[]{:S(2)}, u32[]{:S(2)}) collective-permute-start(bf16[24,17,128]{2,0,1:T(8,128)(2,1)S(1)} %get-tuple-element.265), channel_id=1, source_target_pairs={{0,8},{8,16},{16,24},{1,9},{9,17},{17,25},{2,10},{10,18},{18,26},{... | collective-permute-start | bytes 313352 | tf_op jit(solution)/shard_map/ppermute | solution.py:23
  128.8 1.3 collective-permute-start.13
  131.0 4.3 %collective-permute-done.13 = bf16[24,17,128]{2,0,1:T(8,128)(2,1)S(1)} collective-permute-done((bf16[24,17,128]{2,0,1:T(8,128)(2,1)S(1)}, bf16[24,17,128]{2,0,1:T(8,128)(2,1)S(1)}, u32[]{:S(2)}, u32[]{:S(2)}) %collective-permute-start.13) | collective-permute-done | bytes 104480 | tf_op jit(solution)/shard_map/ppermute | solution.py:26
  135.6 4.2 %collective-permute-start.14 = (bf16[24,74,17]{2,0,1:T(8,128)(2,1)S(1)}, bf16[24,74,17]{2,0,1:T(8,128)(2,1)S(1)}, u32[]{:S(2)}, u32[]{:S(2)}) collective-permute-start(bf16[24,74,17]{2,0,1:T(8,128)(2,1)S(1)} %get-tuple-element.263), channel_id=1, source_target_pairs={{0,1},{1,2},{2,3},{3,4},{4,5},{5,6},{6,7},{8,9},{9,10},{10,11},{11... | collective-permute-start | bytes 181160 | tf_op jit(solution)/shard_map/ppermute | solution.py:23
  139.9 1.3 collective-permute-start.15
  141.3 3.2 %collective-permute-done.15 = bf16[24,74,17]{2,0,1:T(8,128)(2,1)S(1)} collective-permute-done((bf16[24,74,17]{2,0,1:T(8,128)(2,1)S(1)}, bf16[24,74,17]{2,0,1:T(8,128)(2,1)S(1)}, u32[]{:S(2)}, u32[]{:S(2)}) %collective-permute-start.15) | collective-permute-done | bytes 60416 | tf_op jit(solution)/shard_map/ppermute | solution.py:26
  145.0 99.4 %while.30 = (s32[]{:T(128)}, f32[40,128]{1,0:T(8,128)S(1)}, bf16[24,35,35]{2,0,1:T(8,128)(2,1)}, bf16[24,74,162]{2,0,1:T(8,128)(2,1)S(1)}, s32[]{:T(128)}, /*index=5*/s32[]{:T(128)}, s32[]{:T(128)}, s32[]{:T(128)}) while((s32[]{:T(128)}, f32[40,128]{1,0:T(8,128)S(1)}, bf16[24,35,35]{2,0,1:T(8,128)(2,1)}, ...), condition=%wide.region_4.5_spmd.clone, body=%wide.region_3.4_spmd.clone.sunk | while | flops 11070727 | bytes 3596881 | solution.py:66
  145.1 1.1 fusion.90
  147.9 1.1 fusion.90
  150.7 1.1 fusion.90
  153.6 1.1 fusion.90
  156.4 1.1 fusion.90
  159.2 1.1 fusion.90
  162.1 1.1 fusion.90
  164.9 1.1 fusion.90
  167.8 1.1 fusion.90
  170.6 1.1 fusion.90
  173.4 1.1 fusion.90
  176.3 1.1 fusion.90
  179.1 1.1 fusion.90
  182.0 1.1 fusion.90
  184.8 1.1 fusion.90
  187.6 1.1 fusion.90
  190.5 1.1 fusion.90
  193.3 1.1 fusion.90
  196.1 1.1 fusion.90
  199.0 1.1 fusion.90
  201.8 1.1 fusion.90
  204.7 1.1 fusion.90
  207.5 1.1 fusion.90
  210.3 1.1 fusion.90
  213.2 1.1 fusion.90
  216.0 1.1 fusion.90
  218.9 1.1 fusion.90
  221.7 1.1 fusion.90
  224.6 1.1 fusion.90
  227.4 1.1 fusion.90
  230.2 1.1 fusion.90
  233.1 1.1 fusion.90
  235.9 1.1 fusion.90
  238.8 1.1 fusion.90
  241.6 1.1 fusion.90
  245.0 48.5 %all-reduce = (f32[]{:T(128)}, f32[]{:T(128)}) all-reduce(f32[]{:T(128)} %multiply_reduce_fusion.1, f32[]{:T(128)} %get-tuple-element.226), channel_id=1, replica_groups=mesh['gy'=4,'gx'=8] {'gy','gx'}, use_global_device_ids=true, to_apply=%region_6.7 | all-reduce | flops 2 | bytes 16 | tf_op jit(solution)/shard_map/psum | solution.py:132
  (511 shorter events, 91.9 us)
Async XLA Ops:
  1.4 11.4 %collective-permute-start = (bf16[17,128]{1,0:T(8,128)(2,1)S(1)}, bf16[17,128]{1,0:T(8,128)(2,1)S(1)}, u32[]{:S(2)}, u32[]{:S(2)}) collective-permute-start(bf16[17,128]{1,0:T(8,128)(2,1)S(1)} %get-tuple-element.277), channel_id=1, source_target_pairs={{0,8},{8,16},{16,24},{1,9},{9,17},{17,25},{2,10},{10,18},{18,26},{... | collective-permute-start | bytes 13064 | tf_op jit(solution)/shard_map/ppermute | solution.py:23
  6.3 6.5 %collective-permute-start.1 = (bf16[17,128]{1,0:T(8,128)(2,1)S(1)}, bf16[17,128]{1,0:T(8,128)(2,1)S(1)}, u32[]{:S(2)}, u32[]{:S(2)}) collective-permute-start(bf16[17,128]{1,0:T(8,128)(2,1)S(1)} %get-tuple-element.278), channel_id=1, source_target_pairs={{8,0},{16,8},{24,16},{9,1},{17,9},{25,17},{10,2},{18,10},{26,18},{... | collective-permute-start | bytes 13064 | tf_op jit(solution)/shard_map/ppermute | solution.py:26
  12.9 4.4 %collective-permute-start.2 = (bf16[74,17]{1,0:T(8,128)(2,1)S(1)}, bf16[74,17]{1,0:T(8,128)(2,1)S(1)}, u32[]{:S(2)}, u32[]{:S(2)}) collective-permute-start(bf16[74,17]{1,0:T(8,128)(2,1)S(1)} %get-tuple-element.275), channel_id=1, source_target_pairs={{0,1},{1,2},{2,3},{3,4},{4,5},{5,6},{6,7},{8,9},{9,10},{10,11},{11... | collective-permute-start | bytes 7556 | tf_op jit(solution)/shard_map/ppermute | solution.py:23
  14.3 4.6 %collective-permute-start.3 = (bf16[74,17]{1,0:T(8,128)(2,1)S(1)}, bf16[74,17]{1,0:T(8,128)(2,1)S(1)}, u32[]{:S(2)}, u32[]{:S(2)}) collective-permute-start(bf16[74,17]{1,0:T(8,128)(2,1)S(1)} %get-tuple-element.276), channel_id=1, source_target_pairs={{1,0},{2,1},{3,2},{4,3},{5,4},{6,5},{7,6},{9,8},{10,9},{11,10},{12... | collective-permute-start | bytes 7556 | tf_op jit(solution)/shard_map/ppermute | solution.py:26
  19.1 59.0 %copy-start.1 = (s32[40,128]{1,0:T(8,128)S(1)}, s32[40,128]{1,0:T(8,128)}, u32[]{:S(2)}) copy-start(s32[40,128]{1,0:T(8,128)} %param.10) | copy-start | bytes 61444
  44.0 25.8 %collective-permute-start.4 = (f32[10,128]{1,0:T(8,128)S(1)}, f32[10,128]{1,0:T(8,128)S(1)}, u32[]{:S(2)}, u32[]{:S(2)}) collective-permute-start(f32[10,128]{1,0:T(8,128)S(1)} %get-tuple-element.273), channel_id=1, source_target_pairs={{0,8},{8,16},{16,24},{1,9},{9,17},{17,25},{2,10},{10,18},{18,26},{... | collective-permute-start | bytes 15368 | tf_op jit(solution)/shard_map/ppermute | solution.py:23
  48.5 21.2 %collective-permute-start.5 = (f32[10,128]{1,0:T(8,128)S(1)}, f32[10,128]{1,0:T(8,128)S(1)}, u32[]{:S(2)}, u32[]{:S(2)}) collective-permute-start(f32[10,128]{1,0:T(8,128)S(1)} %get-tuple-element.274), channel_id=1, source_target_pairs={{8,0},{16,8},{24,16},{9,1},{17,9},{25,17},{10,2},{18,10},{26,18},{... | collective-permute-start | bytes 15368 | tf_op jit(solution)/shard_map/ppermute | solution.py:26
  69.8 5.6 %collective-permute-start.6 = (f32[60,10]{1,0:T(8,128)S(1)}, f32[60,10]{1,0:T(8,128)S(1)}, u32[]{:S(2)}, u32[]{:S(2)}) collective-permute-start(f32[60,10]{1,0:T(8,128)S(1)} %get-tuple-element.269), channel_id=1, source_target_pairs={{0,1},{1,2},{2,3},{3,4},{4,5},{5,6},{6,7},{8,9},{9,10},{10,11},{11... | collective-permute-start | bytes 7208 | tf_op jit(solution)/shard_map/ppermute | solution.py:23
  74.0 3.1 %collective-permute-start.7 = (f32[60,10]{1,0:T(8,128)S(1)}, f32[60,10]{1,0:T(8,128)S(1)}, u32[]{:S(2)}, u32[]{:S(2)}) collective-permute-start(f32[60,10]{1,0:T(8,128)S(1)} %get-tuple-element.270), channel_id=1, source_target_pairs={{1,0},{2,1},{3,2},{4,3},{5,4},{6,5},{7,6},{9,8},{10,9},{11,10},{12... | collective-permute-start | bytes 7208 | tf_op jit(solution)/shard_map/ppermute | solution.py:26
  85.5 25.8 %collective-permute-start.8 = (f32[10,128]{1,0:T(8,128)S(1)}, f32[10,128]{1,0:T(8,128)S(1)}, u32[]{:S(2)}, u32[]{:S(2)}) collective-permute-start(f32[10,128]{1,0:T(8,128)S(1)} %get-tuple-element.271), channel_id=1, source_target_pairs={{0,8},{8,16},{16,24},{1,9},{9,17},{17,25},{2,10},{10,18},{18,26},{... | collective-permute-start | bytes 15368 | tf_op jit(solution)/shard_map/ppermute | solution.py:23
  90.0 21.2 %collective-permute-start.9 = (f32[10,128]{1,0:T(8,128)S(1)}, f32[10,128]{1,0:T(8,128)S(1)}, u32[]{:S(2)}, u32[]{:S(2)}) collective-permute-start(f32[10,128]{1,0:T(8,128)S(1)} %get-tuple-element.272), channel_id=1, source_target_pairs={{8,0},{16,8},{24,16},{9,1},{17,9},{25,17},{10,2},{18,10},{26,18},{... | collective-permute-start | bytes 15368 | tf_op jit(solution)/shard_map/ppermute | solution.py:26
  111.4 5.7 %collective-permute-start.10 = (f32[60,10]{1,0:T(8,128)S(1)}, f32[60,10]{1,0:T(8,128)S(1)}, u32[]{:S(2)}, u32[]{:S(2)}) collective-permute-start(f32[60,10]{1,0:T(8,128)S(1)} %get-tuple-element.267), channel_id=1, source_target_pairs={{0,1},{1,2},{2,3},{3,4},{4,5},{5,6},{6,7},{8,9},{9,10},{10,11},{11... | collective-permute-start | bytes 7208 | tf_op jit(solution)/shard_map/ppermute | solution.py:23
  115.6 3.1 %collective-permute-start.11 = (f32[60,10]{1,0:T(8,128)S(1)}, f32[60,10]{1,0:T(8,128)S(1)}, u32[]{:S(2)}, u32[]{:S(2)}) collective-permute-start(f32[60,10]{1,0:T(8,128)S(1)} %get-tuple-element.268), channel_id=1, source_target_pairs={{1,0},{2,1},{3,2},{4,3},{5,4},{6,5},{7,6},{9,8},{10,9},{11,10},{12... | collective-permute-start | bytes 7208 | tf_op jit(solution)/shard_map/ppermute | solution.py:26
  124.4 6.6 %collective-permute-start.12 = (bf16[24,17,128]{2,0,1:T(8,128)(2,1)S(1)}, bf16[24,17,128]{2,0,1:T(8,128)(2,1)S(1)}, u32[]{:S(2)}, u32[]{:S(2)}) collective-permute-start(bf16[24,17,128]{2,0,1:T(8,128)(2,1)S(1)} %get-tuple-element.265), channel_id=1, source_target_pairs={{0,8},{8,16},{16,24},{1,9},{9,17},{17,25},{2,10},{10,18},{18,26},{... | collective-permute-start | bytes 313352 | tf_op jit(solution)/shard_map/ppermute | solution.py:23
  128.8 6.6 %collective-permute-start.13 = (bf16[24,17,128]{2,0,1:T(8,128)(2,1)S(1)}, bf16[24,17,128]{2,0,1:T(8,128)(2,1)S(1)}, u32[]{:S(2)}, u32[]{:S(2)}) collective-permute-start(bf16[24,17,128]{2,0,1:T(8,128)(2,1)S(1)} %get-tuple-element.266), channel_id=1, source_target_pairs={{8,0},{16,8},{24,16},{9,1},{17,9},{25,17},{10,2},{18,10},{26,18},{... | collective-permute-start | bytes 313352 | tf_op jit(solution)/shard_map/ppermute | solution.py:26
  135.6 5.6 %collective-permute-start.14 = (bf16[24,74,17]{2,0,1:T(8,128)(2,1)S(1)}, bf16[24,74,17]{2,0,1:T(8,128)(2,1)S(1)}, u32[]{:S(2)}, u32[]{:S(2)}) collective-permute-start(bf16[24,74,17]{2,0,1:T(8,128)(2,1)S(1)} %get-tuple-element.263), channel_id=1, source_target_pairs={{0,1},{1,2},{2,3},{3,4},{4,5},{5,6},{6,7},{8,9},{9,10},{10,11},{11... | collective-permute-start | bytes 181160 | tf_op jit(solution)/shard_map/ppermute | solution.py:23
  139.9 4.6 %collective-permute-start.15 = (bf16[24,74,17]{2,0,1:T(8,128)(2,1)S(1)}, bf16[24,74,17]{2,0,1:T(8,128)(2,1)S(1)}, u32[]{:S(2)}, u32[]{:S(2)}) collective-permute-start(bf16[24,74,17]{2,0,1:T(8,128)(2,1)S(1)} %get-tuple-element.264), channel_id=1, source_target_pairs={{1,0},{2,1},{3,2},{4,3},{5,4},{6,5},{7,6},{9,8},{10,9},{11,10},{12... | collective-permute-start | bytes 181160 | tf_op jit(solution)/shard_map/ppermute | solution.py:26
  145.0 149.2 %copy-start = (f32[40,128]{1,0:T(8,128)S(1)}, f32[40,128]{1,0:T(8,128)}, u32[]{:S(2)}) copy-start(f32[40,128]{1,0:T(8,128)} %param.9) | copy-start | bytes 61444
where the time goes:
time: 298 us; the launch traced here: 295 us
  local copies, waits for them, and re-layouts  82.5 us (28%)
  blocking collectives  48.5 us (16%)
  starting transfers between devices  42.8 us (14%)
  between operations  41.8 us (14%)
  matrix products  41.3 us (14%)
  other arithmetic  22.8 us (8%)
  waiting for transfers between devices  13.6 us (5%)
    slice x70, local copies, waits for them, and re-layouts, one_row(): mixed[b, :, reach - b:reach - b + out_cols]  55.1 us
    psum x1, blocking collectives, body(): totals = lax.psum((part_loss, jnp.sum(gradient * gradient)), ('gy', 'gx'))  48.5 us
    dot_general x35, matrix products, one_row(): jnp.einsum('cb,cyx->byx', row_weights, band, preferred_element_type=jnp.f...  39.1 us
    ppermute x8, starting transfers between devices, with_halo(): lax.ppermute(lax.slice_in_dim(block, block.shape[dim] - width, None, axis...  32.4 us
    while x340, local copies, waits for them, and re-layouts  21.5 us
    ppermute x8, waiting for transfers between devices, with_halo(): lax.ppermute(lax.slice_in_dim(block, 0, width, axis=dim), axis, backward)  12.6 us
    ppermute x8, starting transfers between devices, with_halo(): lax.ppermute(lax.slice_in_dim(block, 0, width, axis=dim), axis, backward)  10.3 us
    reduce_sum x1, other arithmetic, body(): part_loss = jnp.sum(weight * diff * diff)  6.63 us
  transfers between devices with their start and end apart: 16, of which 7 were waited for; matrix products, arithmetic and copies ran while one was open for 2% of the time, Pallas kernels for 0%

commit v1 on v0

v1 whole, which is shorter than its diff:
```python
import functools

import jax
import jax.numpy as jnp
from jax import lax
from jax.experimental import pallas as pl
from jax.experimental.pallas import tpu as pltpu
from jax.sharding import PartitionSpec as P

REACH = 8
LOAD_TAPS = 8
SMOOTH = 2
SMOOTH_TAPS = (0.0625, 0.25, 0.375, 0.25, 0.0625)
SHARPNESS = 4.0
THRESHOLD = 0.65
LOADING_GAIN = 0.5

LANES = 128
WINDOW = 64
SLOT = 32
WIDE = 256
TOP = 24
PAD = 8

NT = (((1,), (1,)), ((), ()))
NN = (((1,), (0,)), ((), ()))
VMEM = pl.BlockSpec(memory_space=pltpu.VMEM)
SMEM = pl.BlockSpec(memory_space=pltpu.SMEM)


class Plan:
    def __init__(self, tile_rows, tile_cols, ny, nx, channels, taps):
        self.tile_rows, self.tile_cols, self.ny, self.nx = tile_rows, tile_cols, ny, nx
        self.rows, self.cols = tile_rows * ny, tile_cols * nx
        self.channels, self.taps, self.radius = channels, taps, taps // 2
        self.step = WINDOW - taps + 1
        self.field_halo = self.radius + 2 * (REACH + SMOOTH)
        self.halo = self.field_halo + self.radius
        self.blocks = -(-(tile_cols + 2 * self.field_halo) // self.step)
        self.pairs = -(-taps // 2)
        self.pairs += self.pairs % 2
        self.depth = self.pairs * LANES
        self.wide = channels * SLOT
        self.lo = self.field_halo - self.radius
        self.hi = self.field_halo + tile_cols + self.radius
        first, last = self.lo // self.step, (self.hi - 1) // self.step
        shift = self.field_halo + self.radius
        pieces = []
        for block in range(first, last + 1):
            low = max(0, shift - block * self.step)
            high = min(WINDOW, shift + tile_cols - block * self.step)
            pieces.append([block, block - first, block * self.step - shift, low, high])
        start = self.lo - first * self.step
        end = self.hi - last * self.step
        self.merged = (
            last > first
            and end <= start
            and end - 1 + taps - 1 < pieces[0][3]
            and start >= pieces[-1][4]
        )
        if self.merged:
            pieces[-1][1] = 0
        self.pieces = pieces
        self.operand_blocks = max(p[1] for p in pieces) + 1
        self.acc_rows = self.rows + 8 * ((self.pairs // 2 + 1) // 2) + 8


def roll_lanes(value, shift):
    return pltpu.roll(value, shift % value.shape[1], 1)


def lane_index(rows, lanes):
    return lax.broadcasted_iota(jnp.int32, (rows, lanes), 1)


def shifted_image(ref, rows, down, right):
    start = PAD + down
    rest = lax.rem(start, 8)
    base = pl.multiple_of(start - rest, 8)
    tiles = ref[pl.ds(base, rows + 8), :].reshape(rows // 8 + 1, 8, WIDE)
    tiles = pltpu.roll(tiles, lax.rem(8 - rest, 8), 1)
    row = lax.broadcasted_iota(jnp.int32, (rows // 8, 8, WIDE), 1)
    value = jnp.where(row < 8 - rest, tiles[:-1], tiles[1:]).reshape(rows, WIDE)
    return pltpu.roll(value, lax.rem(WIDE - right, WIDE), 1)


def strip_kernel(plan, *refs):
    pieces, out, hold = refs[: plan.ny], refs[plan.ny], refs[plan.ny + 1]
    here = lax.axis_index("gy")
    tile_rows, rows = plan.tile_rows, plan.rows
    for index, piece in enumerate(pieces):
        source = partner(here, index, plan.ny)
        value = piece[...].astype(jnp.float32)
        start = pl.multiple_of(source * tile_rows, 8)
        hold[0, pl.ds(start, tile_rows), :] = value[:tile_rows]
        hold[1, pl.ds(start, tile_rows), :] = value[tile_rows:]
    out[0:rows, :] = hold[0].astype(jnp.bfloat16)
    out[rows : 2 * rows, :] = hold[1].astype(jnp.bfloat16)


def build_bands(plan, taps_ref, bands):
    def channel(c, _):
        for q in range(plan.pairs):
            row = taps_ref[pl.ds(c * plan.pairs + q, 1), :]
            wide = jnp.broadcast_to(row, (SLOT, LANES))
            rolled = pltpu.roll(wide, 0, 1, stride=1, stride_axis=0)
            bands[pl.ds(pl.multiple_of(c * SLOT, SLOT), SLOT), q * LANES : (q + 1) * LANES] = (
                rolled.astype(jnp.bfloat16)
            )
        return 0

    lax.fori_loop(0, plan.channels, channel, 0)


def smooth_rows(ref, rows):
    total = None
    for a in range(5):
        term = SMOOTH_TAPS[a] * ref[pl.ds(PAD + a - 2, rows), :]
        total = term if total is None else total + term
    return total


def smooth_cols(value):
    total = None
    for b in range(5):
        term = SMOOTH_TAPS[b] * (value if b == 2 else roll_lanes(value, 2 - b))
        total = term if total is None else total + term
    return total


def main_kernel(
    plan,
    offsets,
    load_weights,
    own,
    near,
    far,
    taps_ref,
    grad_out,
    sums_out,
    bands,
    extended,
    turned,
    pairs_ref,
    patches,
    field,
    image,
    products,
    even,
    odd,
    tall,
):
    rows, tile_cols, step = plan.rows, plan.tile_cols, plan.step
    here = lax.axis_index("gx")
    first_col = here * tile_cols
    build_bands(plan, taps_ref, bands)

    is_even = here % 2 == 0
    lane = lane_index(rows, WIDE)
    blank = jnp.zeros((rows, LANES), jnp.float32)
    spread = []
    for part in range(2):
        mine, close, remote = (
            ref[part * rows : (part + 1) * rows, :].astype(jnp.float32)
            for ref in (own, near, far)
        )
        left = jnp.where(is_even, remote, close)
        right = jnp.where(is_even, close, remote)
        left, mid, right = (jnp.concatenate([v, blank], axis=1) for v in (left, mine, right))
        halo = plan.halo
        left = roll_lanes(left, halo - tile_cols)
        mid = roll_lanes(mid, halo)
        right = roll_lanes(right, halo + tile_cols)
        joined = jnp.where(lane < halo, left, jnp.where(lane < halo + tile_cols, mid, right))
        spread.append(jnp.where(lane < tile_cols + 2 * halo, joined, 0.0))
    tall_rows = extended.shape[0]
    extended[0:TOP, :] = jnp.zeros((TOP, WIDE), jnp.float32)
    extended[TOP : TOP + rows, :] = spread[0]
    extended[TOP + rows : tall_rows, :] = jnp.zeros((tall_rows - TOP - rows, WIDE), jnp.float32)
    target = roll_lanes(spread[1], -plan.radius)

    body_rows = tall_rows - 8
    half = lane_index(body_rows, LANES) < WINDOW
    for block in range(plan.blocks):
        window = roll_lanes(extended[...], -block * step)[:, :LANES]
        turned[...] = roll_lanes(window, WINDOW)
        pairs_ref[0:body_rows, :] = jnp.where(half, window[0:body_rows], turned[1 : body_rows + 1, :])
        for q in range(plan.pairs):
            start = TOP - plan.radius + 2 * q
            patches[block * rows : (block + 1) * rows, q * LANES : (q + 1) * LANES] = pairs_ref[
                start : start + rows, :
            ].astype(jnp.bfloat16)

    field[...] = lax.dot_general(patches[...], bands[...], NT, preferred_element_type=jnp.float32)

    col = lane + (first_col - plan.field_halo)
    inside = (col >= 0) & (col < plan.cols)
    total = jnp.zeros((rows, WIDE), jnp.float32)
    for block in range(plan.blocks):
        power = None
        for t in range(plan.wide // LANES):
            piece = field[block * rows : (block + 1) * rows, t * LANES : (t + 1) * LANES]
            power = piece * piece if power is None else power + piece * piece
        power = power + roll_lanes(power, 2 * SLOT)
        power = power + roll_lanes(power, SLOT)
        power = roll_lanes(jnp.concatenate([power, power], axis=1), block * step)
        total = jnp.where((lane >= block * step) & (lane < (block + 1) * step), power, total)
    kernels_count = plan.channels // 2
    intensity = jnp.where(inside, total / kernels_count, 0.0)
    zeros = jnp.zeros((PAD, WIDE), jnp.float32)
    image[0:PAD, :] = zeros
    image[PAD + rows : 3 * PAD + rows, :] = jnp.concatenate([zeros, zeros], axis=0)
    image[PAD : PAD + rows, :] = intensity
    dense = smooth_cols(smooth_rows(image, rows))
    develop = jnp.where(inside, jax.nn.sigmoid(SHARPNESS * (dense - THRESHOLD)), 0.0)

    image[PAD : PAD + rows, :] = develop
    loading = jnp.zeros((rows, WIDE), jnp.float32)
    for index in range(LOAD_TAPS):
        shifted = shifted_image(image, rows, offsets[index, 0], offsets[index, 1])
        loading = loading + load_weights[index] * shifted
    printed = develop - LOADING_GAIN / LOAD_TAPS * loading
    row_pos = lax.broadcasted_iota(jnp.int32, (rows, WIDE), 0).astype(jnp.float32)
    weight = (1.0 + 2.0 * row_pos / rows) * (1.0 + 2.0 * col.astype(jnp.float32) / plan.cols)
    diff = printed - target
    weighted = weight * diff
    mine = (lane >= plan.field_halo) & (lane < plan.field_halo + tile_cols)
    loss = jnp.sum(jnp.where(mine, weighted * diff, 0.0))
    resid = jnp.where(inside, 2.0 * weighted, 0.0)

    image[PAD : PAD + rows, :] = resid
    back = jnp.zeros((rows, WIDE), jnp.float32)
    for index in range(LOAD_TAPS):
        shifted = shifted_image(image, rows, -offsets[index, 0], -offsets[index, 1])
        back = back + load_weights[index] * shifted
    slope = resid - LOADING_GAIN / LOAD_TAPS * back
    image[PAD : PAD + rows, :] = slope * SHARPNESS * develop * (1.0 - develop)
    inten_grad = smooth_cols(smooth_rows(image, rows)) * (2.0 / kernels_count)
    used = inside & (lane >= plan.lo) & (lane < plan.hi)
    inten_grad = jnp.where(used, inten_grad, 0.0)

    narrow = lane_index(rows, LANES) < step
    gains = {}
    for block, operand, _, _, _ in plan.pieces:
        part = jnp.where(narrow, roll_lanes(inten_grad, -block * step)[:, :LANES], 0.0)
        part = part + roll_lanes(part, SLOT)
        gains[block] = part + roll_lanes(part, 2 * SLOT)
    for operand in range(plan.operand_blocks):
        blocks = [p[0] for p in plan.pieces if p[1] == operand]
        for t in range(plan.wide // LANES):
            value = None
            for block in blocks:
                piece = field[block * rows : (block + 1) * rows, t * LANES : (t + 1) * LANES]
                piece = piece * gains[block]
                value = piece if value is None else value + piece
            products[operand * rows : (operand + 1) * rows, t * LANES : (t + 1) * LANES] = (
                value.astype(jnp.bfloat16)
            )

    even[...] = jnp.zeros_like(even)
    odd[...] = jnp.zeros_like(odd)
    for group in range(plan.pairs // 2):
        out = lax.dot_general(
            products[...],
            bands[:, group * 2 * LANES : (group + 1) * 2 * LANES],
            NN,
            preferred_element_type=jnp.float32,
        )
        held = odd if group % 2 else even
        start = 8 * (group // 2)
        for operand in range(plan.operand_blocks):
            base = operand * plan.acc_rows + start
            held[base : base + rows, :] += out[operand * rows : (operand + 1) * rows, :]

    lane = lane_index(plan.acc_rows, LANES)
    total = [None, None]
    for operand in range(plan.operand_blocks):
        base = operand * plan.acc_rows
        tall[8 : 8 + plan.acc_rows, :] = odd[base : base + plan.acc_rows, :]
        both = even[base : base + plan.acc_rows, :] + tall[4 : 4 + plan.acc_rows, :]
        tall[8 : 8 + plan.acc_rows, :] = both
        pair = both[:, :LANES] + tall[6 : 6 + plan.acc_rows, LANES:]
        for _, index, shift, low, high in plan.pieces:
            if index != operand:
                continue
            keep = (lane >= low + shift) & (lane < high + shift)
            for a in range(2):
                piece = jnp.where(keep, roll_lanes(pair, shift - a * WINDOW), 0.0)
                total[a] = piece if total[a] is None else total[a] + piece
    tall[8 : 8 + plan.acc_rows, 0:LANES] = total[0]
    tall[8 : 8 + plan.acc_rows, LANES:] = total[1]
    gradient = (
        tall[8 + plan.radius : 8 + plan.radius + rows, 0:LANES]
        + tall[7 + plan.radius : 7 + plan.radius + rows, LANES:]
    )
    square = jnp.sum(gradient * gradient)
    tall[0:rows, 0:LANES] = gradient
    start = pl.multiple_of(lax.axis_index("gy") * plan.tile_rows, 8)
    grad_out[...] = tall[pl.ds(start, plan.tile_rows), 0:LANES]
    sums_out[0:8, :] = jnp.broadcast_to(loss, (8, LANES))
    sums_out[8:16, :] = jnp.broadcast_to(square, (8, LANES))


def update_kernel(plan, mask, grad, *refs):
    *sums, update, loss = refs
    total = sums[0][...]
    for other in sums[1:]:
        total = total + other[...]
    scale = jnp.sqrt(total[8:9, :] / (plan.rows * plan.cols) + 1e-06)
    update[...] = mask[...] - (grad[...] / scale)[:, : plan.tile_cols]
    loss[...] = total[0:1, 0:1]


def partner(here, step, count):
    if count & (count - 1) == 0:
        return jnp.bitwise_xor(here, step)
    return lax.rem(here + step, count)


def fetch(value, axis, step, count):
    if count & (count - 1) == 0:
        pairs = [(i, i ^ step) for i in range(count)]
    else:
        pairs = [((i + step) % count, i) for i in range(count)]
    return lax.ppermute(value, axis, pairs)


def swap_neighbours(value, axis, count, first):
    pairs = []
    for i in range(first, count - 1, 2):
        pairs += [(i, i + 1), (i + 1, i)]
    return lax.ppermute(value, axis, pairs)


def sum_terms(value, axis, count):
    if count & (count - 1):
        return [lax.psum(value, axis)]
    terms, bit = [value], 1
    while bit < count:
        value = functools.reduce(jnp.add, terms)
        steps = (bit, 2 * bit, 3 * bit) if 2 * bit < count else (bit,)
        terms = [value] + [fetch(value, axis, s, count) for s in steps]
        bit *= 4 if len(steps) == 3 else 2
    return terms


def body(mask, target, kernels, offsets, load_weights):
    tile_rows, tile_cols = mask.shape
    ny, nx = lax.axis_size("gy"), lax.axis_size("gx")
    channels, taps = kernels.shape[0], kernels.shape[1]
    plan = Plan(tile_rows, tile_cols, ny, nx, channels, taps)
    rows = plan.rows

    def params(megabytes):
        return pltpu.CompilerParams(vmem_limit_bytes=megabytes * 1024 * 1024)

    both = jnp.concatenate([mask.astype(jnp.bfloat16), target.astype(jnp.bfloat16)], axis=0)
    both = jnp.pad(both, ((0, 0), (0, LANES - tile_cols)))
    pieces = [both] + [fetch(both, "gy", s, ny) for s in range(1, ny)]
    strip = pl.pallas_call(
        functools.partial(strip_kernel, plan),
        out_shape=jax.ShapeDtypeStruct((2 * rows, LANES), jnp.bfloat16),
        in_specs=[VMEM] * ny,
        out_specs=VMEM,
        scratch_shapes=[pltpu.VMEM((2, rows, LANES), jnp.float32)],
        name="strip",
    )(*pieces)
    near = swap_neighbours(strip, "gx", nx, 0)
    far = swap_neighbours(strip, "gx", nx, 1)

    tap_rows = jnp.pad(
        kernels.astype(jnp.float32), ((0, 0), (0, 2 * plan.pairs - taps), (0, WINDOW - taps))
    ).reshape(channels * plan.pairs, LANES)

    tall_rows = TOP + rows + 32
    grad, sums = pl.pallas_call(
        functools.partial(main_kernel, plan),
        out_shape=(
            jax.ShapeDtypeStruct((tile_rows, LANES), jnp.float32),
            jax.ShapeDtypeStruct((16, LANES), jnp.float32),
        ),
        in_specs=[SMEM, SMEM, VMEM, VMEM, VMEM, VMEM],
        out_specs=(VMEM, VMEM),
        scratch_shapes=[
            pltpu.VMEM((plan.wide, plan.depth), jnp.bfloat16),
            pltpu.VMEM((tall_rows, WIDE), jnp.float32),
            pltpu.VMEM((tall_rows, LANES), jnp.float32),
            pltpu.VMEM((tall_rows, LANES), jnp.float32),
            pltpu.VMEM((plan.blocks * rows, plan.depth), jnp.bfloat16),
            pltpu.VMEM((plan.blocks * rows, plan.wide), jnp.float32),
            pltpu.VMEM((rows + 3 * PAD, WIDE), jnp.float32),
            pltpu.VMEM((plan.operand_blocks * rows, plan.wide), jnp.bfloat16),
            pltpu.VMEM((plan.operand_blocks * plan.acc_rows, 2 * LANES), jnp.float32),
            pltpu.VMEM((plan.operand_blocks * plan.acc_rows, 2 * LANES), jnp.float32),
            pltpu.VMEM((plan.acc_rows + 16, 2 * LANES), jnp.float32),
        ],
        compiler_params=params(56),
        name="step",
    )(offsets, load_weights, strip, near, far, tap_rows)

    terms = sum_terms(sums, "gx", nx)
    update, loss = pl.pallas_call(
        functools.partial(update_kernel, plan),
        out_shape=(
            jax.ShapeDtypeStruct((tile_rows, tile_cols), jnp.float32),
            jax.ShapeDtypeStruct((1, 1), jnp.float32),
        ),
        in_specs=[VMEM] * (2 + len(terms)),
        out_specs=(VMEM, VMEM),
        name="update",
    )(mask, grad, *terms)
    return update, loss.reshape(())


def solution(mesh):
    return jax.shard_map(
        body,
        mesh=mesh,
        in_specs=(P("gy", "gx"), P("gy", "gx"), P(), P(), P()),
        out_specs=(P("gy", "gx"), P()),
        check_vma=False,
    )
```

time: 298 us -> 52 us (0.17)
  local copies, waits for them, and re-layouts: 82.5 us -> 4.04 us
  blocking collectives: 48.5 us -> 0 us
  matrix products: 41.3 us -> 0 us
  between operations: 41.8 us -> 0.74 us
  starting transfers between devices: 42.8 us -> 13 us
  other arithmetic: 22.8 us -> 1.51 us
  Pallas kernels: 0 us -> 20.4 us
    slice x80 -> x0, local copies, waits for them, and re-layouts: 59.1 us -> none  [the longest x70 55.1 us: one_row(): mixed[b, :, reach - b:reach - b + out_cols]]
    psum x1 -> x0, blocking collectives: 48.5 us -> none  [body(): totals = lax.psum((part_loss, jnp.sum(gradient * gradient)), ('gy', 'gx'))]
    dot_general x40 -> x0, matrix products: 41.3 us -> none  [the longest x35 39.1 us: one_row(): jnp.einsum('cb,cyx->byx', row_weights, band, preferred_element_type=jnp.f...]
    ppermute x16 -> x9, starting transfers between devices: 42.8 us -> 13 us  [the longest x7 12.3 us: fetch(): return lax.ppermute(value, axis, pairs)]
    while x340 -> x0, local copies, waits for them, and re-layouts: 21.5 us -> none
    pallas_call x0 -> x3, Pallas kernels: none -> 20.4 us  [the longest x1 17.6 us: body(): pl.pallas_call(functools.partial(main_kernel, plan), out_shape=(jax.Shape...]
    reduce_sum x3 -> x0, other arithmetic: 7.31 us -> none  [the longest x1 6.63 us: body(): part_loss = jnp.sum(weight * diff * diff)]
    select_n x2 -> x0, other arithmetic: 6.19 us -> none  [the longest x1 5.37 us: body(): jnp.where(inside_near, slope * SHARPNESS * nearby * (1.0 - nearby), 0.0)]
  transfers between devices with their start and end apart: 16 -> 9, of which waited for: 7 -> 5; matrix products, arithmetic and copies ran while one was open for 2% -> 3% of each run, Pallas kernels for 0% -> 0%
where the time goes in v1:
time: 52 us; the launch traced here: 51.7 us
  Pallas kernels  20.4 us (39%)
  starting transfers between devices  13 us (25%)
  waiting for transfers between devices  12 us (23%)
  local copies, waits for them, and re-layouts  4.04 us (8%)
  other arithmetic  1.51 us (3%)
  between operations  0.74 us (1%)
    pallas_call x1, Pallas kernels, body(): pl.pallas_call(functools.partial(main_kernel, plan), out_shape=(jax.Shape...  17.6 us
    ppermute x7, starting transfers between devices, fetch(): return lax.ppermute(value, axis, pairs)  12.3 us
    ppermute x7, waiting for transfers between devices, fetch(): return lax.ppermute(value, axis, pairs)  12 us
    unnamed x23, local copies, waits for them, and re-layouts  3.15 us
    pallas_call x1, Pallas kernels, body(): pl.pallas_call(functools.partial(strip_kernel, plan), out_shape=jax.Shape...  1.44 us
    pallas_call x1, Pallas kernels, body(): pl.pallas_call(functools.partial(update_kernel, plan), out_shape=(jax.Sha...  1.38 us
  transfers between devices with their start and end apart: 9, of which 5 were waited for; matrix products, arithmetic and copies ran while one was open for 3% of the time, Pallas kernels for 0%

profile of v1, /device:TPU:0, one launch (start us, length us, event | category | flops | bytes accessed | tf_op | source)
XLA Modules:
  0.0 51.7 jit_solution(18115785525987985768)
XLA Ops:
  0.6 0.0 copy-start.2
  0.6 0.0 copy-start
  0.7 0.8 %convert_element_type.10 = bf16[40,128]{1,0:T(8,128)(2,1)S(1)} convert(s32[40,128]{1,0:T(8,128)} %param.6) | non-fusion elementwise | flops 5120 | bytes 30720 | tf_op jit(solution)/shard_map/convert_element_type | solution.py:357
  1.4 0.0 copy-done.2
  1.4 0.0 copy-start.1
  1.5 3.1 %collective-permute-start = (bf16[80,128]{1,0:T(8,128)(2,1)S(1)}, bf16[80,128]{1,0:T(8,128)(2,1)S(1)}, u32[]{:S(2)}, u32[]{:S(2)}) collective-permute-start(bf16[80,128]{1,0:T(8,128)(2,1)S(1)} %pad_maximum_fusion.refs_0_), channel_id=1, source_target_pairs={{0,8},{8,0},{16,24},{24,16},{1,9},{9,1},{17,25},{25,17},{2,10},{10... | collective-permute-start | bytes 61448 | tf_op jit(solution)/shard_map/ppermute | solution.py:325
  4.5 2.6 %collective-permute-start.1 = (bf16[80,128]{1,0:T(8,128)(2,1)S(1)}, bf16[80,128]{1,0:T(8,128)(2,1)S(1)}, u32[]{:S(2)}, u32[]{:S(2)}) collective-permute-start(bf16[80,128]{1,0:T(8,128)(2,1)S(1)} %pad_maximum_fusion.refs_0_), channel_id=1, source_target_pairs={{0,16},{8,24},{16,0},{24,8},{1,17},{9,25},{17,1},{25,9},{2,18},{10... | collective-permute-start | bytes 61448 | tf_op jit(solution)/shard_map/ppermute | solution.py:325
  7.1 0.0 collective-permute-start.2
  7.1 0.0 collective-permute-done.refs_1_
  7.1 0.0 copy-start.6
  7.1 2.3 %collective-permute-done.1.refs_2_ = bf16[80,128]{1,0:T(8,128)(2,1)S(1)} collective-permute-done((bf16[80,128]{1,0:T(8,128)(2,1)S(1)}, bf16[80,128]{1,0:T(8,128)(2,1)S(1)}, u32[]{:S(2)}, u32[]{:S(2)}) %collective-permute-start.1) | collective-permute-done | bytes 20512 | tf_op jit(solution)/shard_map/ppermute | solution.py:325
  9.4 0.0 copy-start.7
  9.4 3.3 %collective-permute-done.2.refs_3_ = bf16[80,128]{1,0:T(8,128)(2,1)S(1)} collective-permute-done((bf16[80,128]{1,0:T(8,128)(2,1)S(1)}, bf16[80,128]{1,0:T(8,128)(2,1)S(1)}, u32[]{:S(2)}, u32[]{:S(2)}) %collective-permute-start.2) | collective-permute-done | bytes 20512 | tf_op jit(solution)/shard_map/ppermute | solution.py:325
  12.7 0.0 copy-done.1
  12.7 0.0 copy-done.6
  12.7 0.0 copy-done.7
  12.7 0.0 copy-start.8
  12.7 0.6 %copy-done.8 = bf16[80,128]{1,0:T(8,128)(2,1)} copy-done((bf16[80,128]{1,0:T(8,128)(2,1)}, bf16[80,128]{1,0:T(8,128)(2,1)S(1)}, u32[]{:S(2)}) %copy-start.8) | copy-done | bytes 20504
  13.3 1.4 %strip.1.own = bf16[320,128]{1,0:T(8,128)(2,1)} custom-call(bf16[80,128]{1,0:T(8,128)(2,1)} %copy-done.1, bf16[80,128]{1,0:T(8,128)(2,1)} %copy-done.6, bf16[80,128]{1,0:T(8,128)(2,1)} %copy-done.7, bf16[80,128]{1,0:T(8,128)(2,1)} %copy-done.8), custom_call_target="tpu_custom_call" | custom-call | tf_op jit(solution)/shard_map/strip/pallas_call | solution.py:360
  14.8 0.0 collective-permute-start.3
  14.8 0.7 %collective-permute-start.4 = (bf16[320,128]{1,0:T(8,128)(2,1)}, bf16[320,128]{1,0:T(8,128)(2,1)S(1)}, u32[]{:S(2)}, u32[]{:S(2)}) collective-permute-start(bf16[320,128]{1,0:T(8,128)(2,1)} %strip.1.own), channel_id=1, source_target_pairs={{1,2},{2,1},{3,4},{4,3},{5,6},{6,5},{9,10},{10,9},{11,12},{12,11},... | collective-permute-start | bytes 245768 | tf_op jit(solution)/shard_map/ppermute | solution.py:332
  15.4 0.0 copy-done
  15.5 0.1 copy.9
  15.6 0.0 copy-start.10
  15.6 0.8 %reshape.16.taps_ref = f32[432,128]{1,0:T(8,128)} reshape(f32[24,36,64]{2,1,0:T(8,128)S(1)} %copy.9) | data formatting | bytes 442368 | tf_op jit(solution)/shard_map/reshape | solution.py:373
  16.4 0.0 copy-done.10
  16.4 0.7 %copy.10.offsets = s32[8,2]{1,0:T(8,128)} copy(s32[8,2]{0,1:T(2,128)S(1)} %copy-done.10) | data formatting | bytes 128 | tf_op args[3]
  17.1 0.0 collective-permute-done.3.near
  17.1 0.0 copy-start.3
  17.1 0.0 collective-permute-done.4.far
  17.1 0.6 %copy-done.3 = bf16[320,128]{1,0:T(8,128)(2,1)} copy-done((bf16[320,128]{1,0:T(8,128)(2,1)}, bf16[320,128]{1,0:T(8,128)(2,1)S(1)}, u32[]{:S(2)}) %copy-start.3) | copy-done | bytes 81944
  17.7 0.0 copy-start.4
  17.7 0.6 %copy-done.4 = bf16[320,128]{1,0:T(8,128)(2,1)} copy-done((bf16[320,128]{1,0:T(8,128)(2,1)}, bf16[320,128]{1,0:T(8,128)(2,1)S(1)}, u32[]{:S(2)}) %copy-start.4) | copy-done | bytes 81944
  18.3 17.6 %step.1 = (f32[40,128]{1,0:T(8,128)}, f32[16,128]{1,0:T(8,128)}) custom-call(s32[8,2]{1,0:T(8,128)} %copy.10.offsets, f32[8]{0:T(128)} %load_weights.1, bf16[320,128]{1,0:T(8,128)(2,1)} %strip.1.own, bf16[320,128]{1,0:T(8,128)(2,1)} %copy-done.3, bf16[320,128]{1,0:T(8,128)(2,1)} %copy-done.4, f32[432,128]{1,0:T(8,128)} %reshape.16.taps_ref), custom_call_target="tpu_custom_call" | custom-call | tf_op jit(solution)/shard_map/step/pallas_call | solution.py:376
  35.9 4.1 %collective-permute-start.5 = (f32[16,128]{1,0:T(8,128)}, f32[16,128]{1,0:T(8,128)S(1)}, u32[]{:S(2)}, u32[]{:S(2)}) collective-permute-start(f32[16,128]{1,0:T(8,128)} %get-tuple-element.7), channel_id=1, source_target_pairs={{0,1},{1,0},{2,3},{3,2},{4,5},{5,4},{6,7},{7,6},{8,9},{9,8},{10,11... | collective-permute-start | bytes 24584 | tf_op jit(solution)/shard_map/ppermute | solution.py:325
  40.1 2.0 %collective-permute-start.6 = (f32[16,128]{1,0:T(8,128)}, f32[16,128]{1,0:T(8,128)S(1)}, u32[]{:S(2)}, u32[]{:S(2)}) collective-permute-start(f32[16,128]{1,0:T(8,128)} %get-tuple-element.7), channel_id=1, source_target_pairs={{0,2},{1,3},{2,0},{3,1},{4,6},{5,7},{6,4},{7,5},{8,10},{9,11},{10,... | collective-permute-start | bytes 24584 | tf_op jit(solution)/shard_map/ppermute | solution.py:325
  42.1 0.0 collective-permute-start.7
  42.1 0.0 collective-permute-done.5
  42.1 1.8 %collective-permute-done.6 = f32[16,128]{1,0:T(8,128)S(1)} collective-permute-done((f32[16,128]{1,0:T(8,128)}, f32[16,128]{1,0:T(8,128)S(1)}, u32[]{:S(2)}, u32[]{:S(2)}) %collective-permute-start.6) | collective-permute-done | bytes 8224 | tf_op jit(solution)/shard_map/ppermute | solution.py:325
  43.9 1.4 %collective-permute-done.7 = f32[16,128]{1,0:T(8,128)S(1)} collective-permute-done((f32[16,128]{1,0:T(8,128)}, f32[16,128]{1,0:T(8,128)S(1)}, u32[]{:S(2)}, u32[]{:S(2)}) %collective-permute-start.7) | collective-permute-done | bytes 8224 | tf_op jit(solution)/shard_map/ppermute | solution.py:325
  45.4 0.7 %add_add_fusion.refs_0_ = f32[16,128]{1,0:T(8,128)S(1)} fusion(f32[16,128]{1,0:T(8,128)S(1)} %collective-permute-done.7, f32[16,128]{1,0:T(8,128)S(1)} %collective-permute-done.6, f32[16,128]{1,0:T(8,128)} %get-tuple-element.7, f32[16,128]{1,0:T(8,128)S(1)} %collective-permute-done.5), kind=kLoop, calls=%fused_computation.2 | loop fusion | flops 6144 | bytes 40960 | tf_op jit(solution)/shard_map/add | solution.py:340
  46.1 0.0 copy-start.5
  46.1 0.5 collective-permute-start.8
  46.5 3.2 %collective-permute-done.8.refs_1_ = f32[16,128]{1,0:T(8,128)S(1)} collective-permute-done((f32[16,128]{1,0:T(8,128)S(1)}, f32[16,128]{1,0:T(8,128)S(1)}, u32[]{:S(2)}, u32[]{:S(2)}) %collective-permute-start.8) | collective-permute-done | bytes 8224 | tf_op jit(solution)/shard_map/ppermute | solution.py:325
  49.7 0.0 copy-start.9
  49.7 0.0 copy-done.5
  49.7 0.6 %copy-done.9 = f32[16,128]{1,0:T(8,128)} copy-done((f32[16,128]{1,0:T(8,128)}, f32[16,128]{1,0:T(8,128)S(1)}, u32[]{:S(2)}) %copy-start.9) | copy-done | bytes 8216
  50.3 1.4 %update.1 = (f32[40,128]{1,0:T(8,128)}, f32[1,1]{1,0:T(1,128)}) custom-call(f32[40,128]{1,0:T(8,128)} %mask.1, f32[40,128]{1,0:T(8,128)} %get-tuple-element.6.grad, f32[16,128]{1,0:T(8,128)} %copy-done.5, f32[16,128]{1,0:T(8,128)} %copy-done.9), custom_call_target="tpu_custom_call" | custom-call | tf_op jit(solution)/shard_map/update/pallas_call | solution.py:402
  (3 shorter events, 0.0 us)
Async XLA Ops:
  0.6 0.8 %copy-start.2 = (f32[40,128]{1,0:T(8,128)S(1)}, f32[40,128]{1,0:T(8,128)}, u32[]{:S(2)}) copy-start(f32[40,128]{1,0:T(8,128)} %mask.1) | copy-start | bytes 61444
  0.6 14.8 %copy-start = (bf16[24,35,35]{2,0,1:T(8,128)(2,1)S(1)}, bf16[24,35,35]{2,0,1:T(8,128)(2,1)}, u32[]{:S(2)}) copy-start(bf16[24,35,35]{2,0,1:T(8,128)(2,1)} %param.7) | copy-start | bytes 176404
  1.4 11.3 %copy-start.1 = (bf16[80,128]{1,0:T(8,128)(2,1)}, bf16[80,128]{1,0:T(8,128)(2,1)S(1)}, u32[]{:S(2)}) copy-start(bf16[80,128]{1,0:T(8,128)(2,1)S(1)} %pad_maximum_fusion.refs_0_) | copy-start | bytes 61444
  1.5 5.7 %collective-permute-start = (bf16[80,128]{1,0:T(8,128)(2,1)S(1)}, bf16[80,128]{1,0:T(8,128)(2,1)S(1)}, u32[]{:S(2)}, u32[]{:S(2)}) collective-permute-start(bf16[80,128]{1,0:T(8,128)(2,1)S(1)} %pad_maximum_fusion.refs_0_), channel_id=1, source_target_pairs={{0,8},{8,0},{16,24},{24,16},{1,9},{9,1},{17,25},{25,17},{2,10},{10... | collective-permute-start | bytes 61448 | tf_op jit(solution)/shard_map/ppermute | solution.py:325
  4.5 4.9 %collective-permute-start.1 = (bf16[80,128]{1,0:T(8,128)(2,1)S(1)}, bf16[80,128]{1,0:T(8,128)(2,1)S(1)}, u32[]{:S(2)}, u32[]{:S(2)}) collective-permute-start(bf16[80,128]{1,0:T(8,128)(2,1)S(1)} %pad_maximum_fusion.refs_0_), channel_id=1, source_target_pairs={{0,16},{8,24},{16,0},{24,8},{1,17},{9,25},{17,1},{25,9},{2,18},{10... | collective-permute-start | bytes 61448 | tf_op jit(solution)/shard_map/ppermute | solution.py:325
  7.1 5.6 %collective-permute-start.2 = (bf16[80,128]{1,0:T(8,128)(2,1)S(1)}, bf16[80,128]{1,0:T(8,128)(2,1)S(1)}, u32[]{:S(2)}, u32[]{:S(2)}) collective-permute-start(bf16[80,128]{1,0:T(8,128)(2,1)S(1)} %pad_maximum_fusion.refs_0_), channel_id=1, source_target_pairs={{0,24},{8,16},{16,8},{24,0},{1,25},{9,17},{17,9},{25,1},{2,26},{10... | collective-permute-start | bytes 61448 | tf_op jit(solution)/shard_map/ppermute | solution.py:325
  7.1 5.6 %copy-start.6 = (bf16[80,128]{1,0:T(8,128)(2,1)}, bf16[80,128]{1,0:T(8,128)(2,1)S(1)}, u32[]{:S(2)}) copy-start(bf16[80,128]{1,0:T(8,128)(2,1)S(1)} %collective-permute-done.refs_1_) | copy-start | bytes 61444
  9.4 3.3 %copy-start.7 = (bf16[80,128]{1,0:T(8,128)(2,1)}, bf16[80,128]{1,0:T(8,128)(2,1)S(1)}, u32[]{:S(2)}) copy-start(bf16[80,128]{1,0:T(8,128)(2,1)S(1)} %collective-permute-done.1.refs_2_) | copy-start | bytes 61444
  12.7 0.6 %copy-start.8 = (bf16[80,128]{1,0:T(8,128)(2,1)}, bf16[80,128]{1,0:T(8,128)(2,1)S(1)}, u32[]{:S(2)}) copy-start(bf16[80,128]{1,0:T(8,128)(2,1)S(1)} %collective-permute-done.2.refs_3_) | copy-start | bytes 61444
  14.8 2.3 %collective-permute-start.3 = (bf16[320,128]{1,0:T(8,128)(2,1)}, bf16[320,128]{1,0:T(8,128)(2,1)S(1)}, u32[]{:S(2)}, u32[]{:S(2)}) collective-permute-start(bf16[320,128]{1,0:T(8,128)(2,1)} %strip.1.own), channel_id=1, source_target_pairs={{0,1},{1,0},{2,3},{3,2},{4,5},{5,4},{6,7},{7,6},{8,9},{9,8},{10,11... | collective-permute-start | bytes 245768 | tf_op jit(solution)/shard_map/ppermute | solution.py:332
  14.8 2.3 %collective-permute-start.4 = (bf16[320,128]{1,0:T(8,128)(2,1)}, bf16[320,128]{1,0:T(8,128)(2,1)S(1)}, u32[]{:S(2)}, u32[]{:S(2)}) collective-permute-start(bf16[320,128]{1,0:T(8,128)(2,1)} %strip.1.own), channel_id=1, source_target_pairs={{1,2},{2,1},{3,4},{4,3},{5,6},{6,5},{9,10},{10,9},{11,12},{12,11},... | collective-permute-start | bytes 245768 | tf_op jit(solution)/shard_map/ppermute | solution.py:332
  15.6 0.8 %copy-start.10 = (s32[8,2]{0,1:T(2,128)S(1)}, s32[8,2]{0,1:T(2,128)}, u32[]{:S(2)}) copy-start(s32[8,2]{0,1:T(2,128)} %param.8) | copy-start | bytes 196
  17.1 0.6 %copy-start.3 = (bf16[320,128]{1,0:T(8,128)(2,1)}, bf16[320,128]{1,0:T(8,128)(2,1)S(1)}, u32[]{:S(2)}) copy-start(bf16[320,128]{1,0:T(8,128)(2,1)S(1)} %collective-permute-done.3.near) | copy-start | bytes 245764
  17.7 0.6 %copy-start.4 = (bf16[320,128]{1,0:T(8,128)(2,1)}, bf16[320,128]{1,0:T(8,128)(2,1)S(1)}, u32[]{:S(2)}) copy-start(bf16[320,128]{1,0:T(8,128)(2,1)S(1)} %collective-permute-done.4.far) | copy-start | bytes 245764
  35.9 6.2 %collective-permute-start.5 = (f32[16,128]{1,0:T(8,128)}, f32[16,128]{1,0:T(8,128)S(1)}, u32[]{:S(2)}, u32[]{:S(2)}) collective-permute-start(f32[16,128]{1,0:T(8,128)} %get-tuple-element.7), channel_id=1, source_target_pairs={{0,1},{1,0},{2,3},{3,2},{4,5},{5,4},{6,7},{7,6},{8,9},{9,8},{10,11... | collective-permute-start | bytes 24584 | tf_op jit(solution)/shard_map/ppermute | solution.py:325
  40.1 3.9 %collective-permute-start.6 = (f32[16,128]{1,0:T(8,128)}, f32[16,128]{1,0:T(8,128)S(1)}, u32[]{:S(2)}, u32[]{:S(2)}) collective-permute-start(f32[16,128]{1,0:T(8,128)} %get-tuple-element.7), channel_id=1, source_target_pairs={{0,2},{1,3},{2,0},{3,1},{4,6},{5,7},{6,4},{7,5},{8,10},{9,11},{10,... | collective-permute-start | bytes 24584 | tf_op jit(solution)/shard_map/ppermute | solution.py:325
  42.1 3.3 %collective-permute-start.7 = (f32[16,128]{1,0:T(8,128)}, f32[16,128]{1,0:T(8,128)S(1)}, u32[]{:S(2)}, u32[]{:S(2)}) collective-permute-start(f32[16,128]{1,0:T(8,128)} %get-tuple-element.7), channel_id=1, source_target_pairs={{0,3},{1,2},{2,1},{3,0},{4,7},{5,6},{6,5},{7,4},{8,11},{9,10},{10,... | collective-permute-start | bytes 24584 | tf_op jit(solution)/shard_map/ppermute | solution.py:325
  46.1 3.7 %copy-start.5 = (f32[16,128]{1,0:T(8,128)}, f32[16,128]{1,0:T(8,128)S(1)}, u32[]{:S(2)}) copy-start(f32[16,128]{1,0:T(8,128)S(1)} %add_add_fusion.refs_0_) | copy-start | bytes 24580
  46.1 3.7 %collective-permute-start.8 = (f32[16,128]{1,0:T(8,128)S(1)}, f32[16,128]{1,0:T(8,128)S(1)}, u32[]{:S(2)}, u32[]{:S(2)}) collective-permute-start(f32[16,128]{1,0:T(8,128)S(1)} %add_add_fusion.refs_0_), channel_id=1, source_target_pairs={{0,4},{1,5},{2,6},{3,7},{4,0},{5,1},{6,2},{7,3},{8,12},{9,13},{10,... | collective-permute-start | bytes 24584 | tf_op jit(solution)/shard_map/ppermute | solution.py:325
  49.7 0.6 %copy-start.9 = (f32[16,128]{1,0:T(8,128)}, f32[16,128]{1,0:T(8,128)S(1)}, u32[]{:S(2)}) copy-start(f32[16,128]{1,0:T(8,128)S(1)} %collective-permute-done.8.refs_1_) | copy-start | bytes 24580

commit v2 on v1

--- a/solution.py
+++ b/solution.py
@@ -62,6 +62,10 @@
             pieces[-1][1] = 0
         self.pieces = pieces
         self.operand_blocks = max(p[1] for p in pieces) + 1
+        low = sum(b * self.step < self.halo for b in range(self.blocks))
+        end = self.halo + tile_cols
+        high = sum(b * self.step + WINDOW > end for b in range(self.blocks))
+        self.late = max(low, high)
         self.acc_rows = self.rows + 8 * ((self.pairs // 2 + 1) // 2) + 8
 
 
@@ -84,8 +88,24 @@
     return pltpu.roll(value, lax.rem(WIDE - right, WIDE), 1)
 
 
+def pack_kernel(plan, mask, target, both, mask_out, target_in, sems):
+    rows, cols = plan.tile_rows, plan.tile_cols
+    copies = [
+        pltpu.make_async_copy(source, held, sems.at[i])
+        for i, (source, held) in enumerate(((mask, mask_out), (target, target_in)))
+    ]
+    for copy in copies:
+        copy.start()
+    if cols < LANES:
+        both[...] = jnp.zeros_like(both)
+    copies[0].wait()
+    both[0:rows, 0:cols] = mask_out[...].astype(jnp.bfloat16)
+    copies[1].wait()
+    both[rows : 2 * rows, 0:cols] = target_in[...].astype(jnp.float32).astype(jnp.bfloat16)
+
+
 def strip_kernel(plan, *refs):
-    pieces, out, hold = refs[: plan.ny], refs[plan.ny], refs[plan.ny + 1]
+    pieces, out, hold = refs[: plan.ny], refs[plan.ny + 1], refs[plan.ny + 2]
     here = lax.axis_index("gy")
     tile_rows, rows = plan.tile_rows, plan.rows
     for index, piece in enumerate(pieces):
@@ -98,10 +118,20 @@
     out[rows : 2 * rows, :] = hold[1].astype(jnp.bfloat16)
 
 
-def build_bands(plan, taps_ref, bands):
+def bands_kernel(plan, kernels_ref, bands, row_ref, pairs_ref):
+    channels, taps = plan.channels, plan.taps
+    row_ref[...] = jnp.zeros_like(row_ref)
+    for q in range(plan.pairs):
+        for a in range(2):
+            if 2 * q + a < taps:
+                row_ref[a, :, 0:taps] = kernels_ref[2 * q + a].astype(jnp.float32)
+            else:
+                row_ref[a] = jnp.zeros((channels, LANES), jnp.float32)
+        pairs_ref[q * channels : (q + 1) * channels, :] = row_ref[0] + roll_lanes(row_ref[1], WINDOW)
+
     def channel(c, _):
         for q in range(plan.pairs):
-            row = taps_ref[pl.ds(c * plan.pairs + q, 1), :]
+            row = pairs_ref[pl.ds(q * channels + c, 1), :]
             wide = jnp.broadcast_to(row, (SLOT, LANES))
             rolled = pltpu.roll(wide, 0, 1, stride=1, stride_axis=0)
             bands[pl.ds(pl.multiple_of(c * SLOT, SLOT), SLOT), q * LANES : (q + 1) * LANES] = (
@@ -109,7 +139,7 @@
             )
         return 0
 
-    lax.fori_loop(0, plan.channels, channel, 0)
+    lax.fori_loop(0, channels, channel, 0)
 
 
 def smooth_rows(ref, rows):
@@ -128,70 +158,97 @@
     return total
 
 
-def main_kernel(
+def read_part(ref, part, rows):
+    value = ref[part * rows : (part + 1) * rows, :].astype(jnp.float32)
+    return jnp.concatenate([value, jnp.zeros((rows, LANES), jnp.float32)], axis=1)
+
+
+def join_columns(plan, own, near, far, part):
+    rows, tile_cols, halo = plan.rows, plan.tile_cols, plan.halo
+    is_even = lax.axis_index("gx") % 2 == 0
+    lane = lane_index(rows, WIDE)
+    mid = roll_lanes(read_part(own, part, rows), halo)
+    close = read_part(near, part, rows)
+    remote = jnp.zeros_like(close) if far is None else read_part(far, part, rows)
+    left = roll_lanes(jnp.where(is_even, remote, close), halo - tile_cols)
+    right = roll_lanes(jnp.where(is_even, close, remote), halo + tile_cols)
+    joined = jnp.where(lane < halo, left, jnp.where(lane < halo + tile_cols, mid, right))
+    return jnp.where(lane < tile_cols + 2 * halo, joined, 0.0)
+
+
+def fill_extended(plan, value, extended):
+    rows, tall_rows = plan.rows, extended.shape[0]
+    extended[0:TOP, :] = jnp.zeros((TOP, WIDE), jnp.float32)
+    extended[TOP : TOP + rows, :] = value
+    extended[TOP + rows : tall_rows, :] = jnp.zeros((tall_rows - TOP - rows, WIDE), jnp.float32)
+
+
+def fill_patches(plan, block, index, extended, turned, pairs_ref, patches):
+    rows, body_rows = plan.rows, extended.shape[0] - 8
+    half = lane_index(body_rows, LANES) < WINDOW
+    window = pltpu.roll(extended[...], lax.rem(WIDE - block * plan.step, WIDE), 1)[:, :LANES]
+    turned[...] = roll_lanes(window, WINDOW)
+    pairs_ref[0:body_rows, :] = jnp.where(half, window[0:body_rows], turned[1 : body_rows + 1, :])
+    for q in range(plan.pairs):
+        start = TOP - plan.radius + 2 * q
+        patches[index * rows : (index + 1) * rows, q * LANES : (q + 1) * LANES] = pairs_ref[
+            start : start + rows, :
+        ].astype(jnp.bfloat16)
+
+
+def early_kernel(plan, own, near, bands, field, extended, turned, pairs_ref, patches):
+    rows, late, blocks = plan.rows, plan.late, plan.blocks
+    fill_extended(plan, join_columns(plan, own, near, None, 0), extended)
+    first = jnp.where(lax.axis_index("gx") % 2 == 0, late, 0)
+    for index in range(blocks - late):
+        fill_patches(plan, first + index, index, extended, turned, pairs_ref, patches)
+    field[late * rows : blocks * rows, :] = lax.dot_general(
+        patches[...], bands[...], NT, preferred_element_type=jnp.float32
+    )
+
+
+def late_kernel(
     plan,
     offsets,
     load_weights,
     own,
     near,
     far,
-    taps_ref,
+    bands,
+    field_in,
     grad_out,
     sums_out,
-    bands,
+    field,
     extended,
     turned,
     pairs_ref,
     patches,
-    field,
     image,
     products,
     even,
     odd,
     tall,
 ):
+    del field_in
     rows, tile_cols, step = plan.rows, plan.tile_cols, plan.step
+    late, blocks = plan.late, plan.blocks
     here = lax.axis_index("gx")
+    is_even = here % 2 == 0
     first_col = here * tile_cols
-    build_bands(plan, taps_ref, bands)
-
-    is_even = here % 2 == 0
     lane = lane_index(rows, WIDE)
-    blank = jnp.zeros((rows, LANES), jnp.float32)
-    spread = []
-    for part in range(2):
-        mine, close, remote = (
-            ref[part * rows : (part + 1) * rows, :].astype(jnp.float32)
-            for ref in (own, near, far)
-        )
-        left = jnp.where(is_even, remote, close)
-        right = jnp.where(is_even, close, remote)
-        left, mid, right = (jnp.concatenate([v, blank], axis=1) for v in (left, mine, right))
-        halo = plan.halo
-        left = roll_lanes(left, halo - tile_cols)
-        mid = roll_lanes(mid, halo)
-        right = roll_lanes(right, halo + tile_cols)
-        joined = jnp.where(lane < halo, left, jnp.where(lane < halo + tile_cols, mid, right))
-        spread.append(jnp.where(lane < tile_cols + 2 * halo, joined, 0.0))
-    tall_rows = extended.shape[0]
-    extended[0:TOP, :] = jnp.zeros((TOP, WIDE), jnp.float32)
-    extended[TOP : TOP + rows, :] = spread[0]
-    extended[TOP + rows : tall_rows, :] = jnp.zeros((tall_rows - TOP - rows, WIDE), jnp.float32)
-    target = roll_lanes(spread[1], -plan.radius)
-
-    body_rows = tall_rows - 8
-    half = lane_index(body_rows, LANES) < WINDOW
-    for block in range(plan.blocks):
-        window = roll_lanes(extended[...], -block * step)[:, :LANES]
-        turned[...] = roll_lanes(window, WINDOW)
-        pairs_ref[0:body_rows, :] = jnp.where(half, window[0:body_rows], turned[1 : body_rows + 1, :])
-        for q in range(plan.pairs):
-            start = TOP - plan.radius + 2 * q
-            patches[block * rows : (block + 1) * rows, q * LANES : (q + 1) * LANES] = pairs_ref[
-                start : start + rows, :
-            ].astype(jnp.bfloat16)
-
-    field[...] = lax.dot_general(patches[...], bands[...], NT, preferred_element_type=jnp.float32)
+    fill_extended(plan, join_columns(plan, own, near, far, 0), extended)
+    target = roll_lanes(join_columns(plan, own, near, far, 1), -plan.radius)
+    first = jnp.where(is_even, 0, blocks - late)
+    for index in range(late):
+        fill_patches(plan, first + index, index, extended, turned, pairs_ref, patches)
+    field[0 : late * rows, :] = lax.dot_general(
+        patches[...], bands[...], NT, preferred_element_type=jnp.float32
+    )
+
+    def field_piece(block, t):
+        slot = jnp.where(is_even, block, (block + late) % blocks)
+        start = pl.multiple_of(slot * rows, 8)
+        return field[pl.ds(start, rows), t * LANES : (t + 1) * LANES]
 
     col = lane + (first_col - plan.field_halo)
     inside = (col >= 0) & (col < plan.cols)
@@ -199,7 +256,7 @@
     for block in range(plan.blocks):
         power = None
         for t in range(plan.wide // LANES):
-            piece = field[block * rows : (block + 1) * rows, t * LANES : (t + 1) * LANES]
+            piece = field_piece(block, t)
             power = piece * piece if power is None else power + piece * piece
         power = power + roll_lanes(power, 2 * SLOT)
         power = power + roll_lanes(power, SLOT)
@@ -217,7 +274,7 @@
     image[PAD : PAD + rows, :] = develop
     loading = jnp.zeros((rows, WIDE), jnp.float32)
     for index in range(LOAD_TAPS):
-        shifted = shifted_image(image, rows, offsets[index, 0], offsets[index, 1])
+        shifted = shifted_image(image, rows, offsets[0, index], offsets[1, index])
         loading = loading + load_weights[index] * shifted
     printed = develop - LOADING_GAIN / LOAD_TAPS * loading
     row_pos = lax.broadcasted_iota(jnp.int32, (rows, WIDE), 0).astype(jnp.float32)
@@ -231,7 +288,7 @@
     image[PAD : PAD + rows, :] = resid
     back = jnp.zeros((rows, WIDE), jnp.float32)
     for index in range(LOAD_TAPS):
-        shifted = shifted_image(image, rows, -offsets[index, 0], -offsets[index, 1])
+        shifted = shifted_image(image, rows, -offsets[0, index], -offsets[1, index])
         back = back + load_weights[index] * shifted
     slope = resid - LOADING_GAIN / LOAD_TAPS * back
     image[PAD : PAD + rows, :] = slope * SHARPNESS * develop * (1.0 - develop)
@@ -246,12 +303,11 @@
         part = part + roll_lanes(part, SLOT)
         gains[block] = part + roll_lanes(part, 2 * SLOT)
     for operand in range(plan.operand_blocks):
-        blocks = [p[0] for p in plan.pieces if p[1] == operand]
+        sources = [p[0] for p in plan.pieces if p[1] == operand]
         for t in range(plan.wide // LANES):
             value = None
-            for block in blocks:
-                piece = field[block * rows : (block + 1) * rows, t * LANES : (t + 1) * LANES]
-                piece = piece * gains[block]
+            for block in sources:
+                piece = field_piece(block, t) * gains[block]
                 value = piece if value is None else value + piece
             products[operand * rows : (operand + 1) * rows, t * LANES : (t + 1) * LANES] = (
                 value.astype(jnp.bfloat16)
@@ -351,54 +407,110 @@
     plan = Plan(tile_rows, tile_cols, ny, nx, channels, taps)
     rows = plan.rows
 
-    def params(megabytes):
-        return pltpu.CompilerParams(vmem_limit_bytes=megabytes * 1024 * 1024)
-
-    both = jnp.concatenate([mask.astype(jnp.bfloat16), target.astype(jnp.bfloat16)], axis=0)
-    both = jnp.pad(both, ((0, 0), (0, LANES - tile_cols)))
+    def in_vmem(value):
+        return pltpu.with_memory_space_constraint(value, pltpu.VMEM)
+
+    def cost(nanoseconds):
+        return pl.CostEstimate(flops=nanoseconds * 1000000, bytes_accessed=0, transcendentals=0)
+
+    def params(scratch):
+        return pltpu.CompilerParams(vmem_limit_bytes=scratch + 12 * 1024 * 1024)
+
+    both, mask = pl.pallas_call(
+        functools.partial(pack_kernel, plan),
+        out_shape=(
+            pltpu.VMEM((2 * tile_rows, LANES), jnp.bfloat16),
+            pltpu.VMEM((tile_rows, tile_cols), jnp.float32),
+        ),
+        in_specs=[pl.BlockSpec(memory_space=pltpu.HBM)] * 2,
+        out_specs=(VMEM,) * 2,
+        scratch_shapes=[
+            pltpu.VMEM((tile_rows, tile_cols), jnp.int32),
+            pltpu.SemaphoreType.DMA((2,)),
+        ],
+        compiler_params=params(0),
+        name="pack",
+    )(*[pltpu.with_memory_space_constraint(v, pltpu.HBM) for v in (mask, target)])
     pieces = [both] + [fetch(both, "gy", s, ny) for s in range(1, ny)]
+
+    bands = pl.pallas_call(
+        functools.partial(bands_kernel, plan),
+        out_shape=pltpu.VMEM((plan.wide, plan.depth), jnp.bfloat16),
+        in_specs=[VMEM],
+        out_specs=VMEM,
+        scratch_shapes=[
+            pltpu.VMEM((2, channels, LANES), jnp.float32),
+            pltpu.VMEM((plan.pairs * channels, LANES), jnp.float32),
+        ],
+        compiler_params=params(0),
+        cost_estimate=cost(2000),
+        name="bands",
+    )(in_vmem(jnp.transpose(kernels, (1, 0, 2))))
+    bands = in_vmem(bands)
     strip = pl.pallas_call(
         functools.partial(strip_kernel, plan),
-        out_shape=jax.ShapeDtypeStruct((2 * rows, LANES), jnp.bfloat16),
-        in_specs=[VMEM] * ny,
+        out_shape=pltpu.VMEM((2 * rows, LANES), jnp.bfloat16),
+        in_specs=[VMEM] * ny + [pl.BlockSpec(memory_space=pl.ANY)],
         out_specs=VMEM,
         scratch_shapes=[pltpu.VMEM((2, rows, LANES), jnp.float32)],
+        compiler_params=params(0),
+        cost_estimate=cost(300),
         name="strip",
-    )(*pieces)
-    near = swap_neighbours(strip, "gx", nx, 0)
-    far = swap_neighbours(strip, "gx", nx, 1)
-
-    tap_rows = jnp.pad(
-        kernels.astype(jnp.float32), ((0, 0), (0, 2 * plan.pairs - taps), (0, WINDOW - taps))
-    ).reshape(channels * plan.pairs, LANES)
+    )(*[in_vmem(p) for p in pieces], bands)
+    near = in_vmem(swap_neighbours(strip, "gx", nx, 0))
+    far = in_vmem(swap_neighbours(strip, "gx", nx, 1))
+    own = in_vmem(strip)
 
     tall_rows = TOP + rows + 32
-    grad, sums = pl.pallas_call(
-        functools.partial(main_kernel, plan),
+    early = plan.blocks - plan.late
+    patch_scratch = [
+        pltpu.VMEM((tall_rows, WIDE), jnp.float32),
+        pltpu.VMEM((tall_rows, LANES), jnp.float32),
+        pltpu.VMEM((tall_rows, LANES), jnp.float32),
+    ]
+    field_type = pltpu.VMEM((plan.blocks * rows, plan.wide), jnp.float32)
+    field = pl.pallas_call(
+        functools.partial(early_kernel, plan),
+        out_shape=field_type,
+        in_specs=[VMEM] * 3,
+        out_specs=VMEM,
+        scratch_shapes=[
+            *patch_scratch,
+            pltpu.VMEM((early * rows, plan.depth), jnp.bfloat16),
+        ],
+        compiler_params=params(early * rows * plan.depth * 2),
+        cost_estimate=cost(3500),
+        name="early",
+    )(own, near, bands)
+
+    grad, sums, _ = pl.pallas_call(
+        functools.partial(late_kernel, plan),
         out_shape=(
-            jax.ShapeDtypeStruct((tile_rows, LANES), jnp.float32),
-            jax.ShapeDtypeStruct((16, LANES), jnp.float32),
+            pltpu.VMEM((tile_rows, LANES), jnp.float32),
+            pltpu.VMEM((16, LANES), jnp.float32),
+            field_type,
         ),
-        in_specs=[SMEM, SMEM, VMEM, VMEM, VMEM, VMEM],
-        out_specs=(VMEM, VMEM),
+        in_specs=[SMEM, SMEM] + [VMEM] * 5,
+        out_specs=(VMEM,) * 3,
         scratch_shapes=[
-            pltpu.VMEM((plan.wide, plan.depth), jnp.bfloat16),
-            pltpu.VMEM((tall_rows, WIDE), jnp.float32),
-            pltpu.VMEM((tall_rows, LANES), jnp.float32),
-            pltpu.VMEM((tall_rows, LANES), jnp.float32),
-            pltpu.VMEM((plan.blocks * rows, plan.depth), jnp.bfloat16),
-            pltpu.VMEM((plan.blocks * rows, plan.wide), jnp.float32),
+            *patch_scratch,
+            pltpu.VMEM((plan.late * rows, plan.depth), jnp.bfloat16),
             pltpu.VMEM((rows + 3 * PAD, WIDE), jnp.float32),
             pltpu.VMEM((plan.operand_blocks * rows, plan.wide), jnp.bfloat16),
             pltpu.VMEM((plan.operand_blocks * plan.acc_rows, 2 * LANES), jnp.float32),
             pltpu.VMEM((plan.operand_blocks * plan.acc_rows, 2 * LANES), jnp.float32),
             pltpu.VMEM((plan.acc_rows + 16, 2 * LANES), jnp.float32),
         ],
-        compiler_params=params(56),
-        name="step",
-    )(offsets, load_weights, strip, near, far, tap_rows)
-
-    terms = sum_terms(sums, "gx", nx)
+        input_output_aliases={6: 2},
+        compiler_params=params(
+            plan.late * rows * plan.depth * 2
+            + plan.operand_blocks * (rows * plan.wide * 2 + plan.acc_rows * 16 * LANES)
+        ),
+        cost_estimate=cost(12000),
+        name="late",
+    )(jnp.transpose(offsets), load_weights, own, near, far, bands, in_vmem(field))
+
+    terms = [in_vmem(t) for t in sum_terms(sums, "gx", nx)]
     update, loss = pl.pallas_call(
         functools.partial(update_kernel, plan),
         out_shape=(
@@ -407,8 +519,9 @@
         ),
         in_specs=[VMEM] * (2 + len(terms)),
         out_specs=(VMEM, VMEM),
+        compiler_params=params(0),
         name="update",
-    )(mask, grad, *terms)
+    )(in_vmem(mask), in_vmem(grad), *terms)
     return update, loss.reshape(())
 
 

time: 52 us -> 38.7 us (0.74)
  waiting for transfers between devices: 12 us -> 7.68 us
  local copies, waits for them, and re-layouts: 4.04 us -> 0.95 us
  Pallas kernels: 20.4 us -> 17.8 us
  starting transfers between devices: 13 us -> 11.3 us
  other arithmetic: 1.51 us -> 0.01 us
    ppermute x7, waiting for transfers between devices: 12 us -> 7.09 us  [fetch(): return lax.ppermute(value, axis, pairs)]
    unnamed x23 -> x6, local copies, waits for them, and re-layouts: 3.15 us -> 0.95 us
    pallas_call x2 -> x5, Pallas kernels: 19 us -> 17.2 us  [the longest x1 10.6 us: body(): pl.pallas_call(functools.partial(late_kernel, plan), out_shape=(pltpu.VME...]
    ppermute x7, starting transfers between devices: 12.3 us -> 10.6 us  [fetch(): return lax.ppermute(value, axis, pairs)]
    reshape x2 -> x0, local copies, waits for them, and re-layouts: 0.89 us -> none  [body(): tap_rows = jnp.pad(kernels.astype(jnp.float32), ((0, 0), (0, 2 * plan.pai...]
    convert_element_type x2 -> x0, other arithmetic: 0.78 us -> none  [the longest x1 0.77 us: body(): target.astype(jnp.bfloat16)]
    pallas_call x1, Pallas kernels: 1.38 us -> 0.63 us  [body(): pl.pallas_call(functools.partial(update_kernel, plan), out_shape=(jax.Sha...]
    add x1, other arithmetic: 0.7 us -> 0.01 us  [sum_terms(): value = functools.reduce(jnp.add, terms)]
  transfers between devices with their start and end apart: 9 -> 9, of which waited for: 5 -> 5; matrix products, arithmetic and copies ran while one was open for 3% -> 0% of each run, Pallas kernels for 0% -> 15%
where the time goes in v2:
time: 38.7 us; the launch traced here: 38.5 us
  Pallas kernels  17.8 us (46%)
  starting transfers between devices  11.3 us (29%)
  waiting for transfers between devices  7.68 us (20%)
  local copies, waits for them, and re-layouts  0.95 us (2%)
  between operations  0.74 us (2%)
    pallas_call x1, Pallas kernels, body(): pl.pallas_call(functools.partial(late_kernel, plan), out_shape=(pltpu.VME...  10.6 us
    ppermute x7, starting transfers between devices, fetch(): return lax.ppermute(value, axis, pairs)  10.6 us
    ppermute x7, waiting for transfers between devices, fetch(): return lax.ppermute(value, axis, pairs)  7.09 us
    pallas_call x1, Pallas kernels, body(): pl.pallas_call(functools.partial(early_kernel, plan), out_shape=field_typ...  3.08 us
    pallas_call x1, Pallas kernels, body(): pl.pallas_call(functools.partial(bands_kernel, plan), out_shape=pltpu.VME...  2.76 us
    unnamed x6, local copies, waits for them, and re-layouts  0.95 us
  transfers between devices with their start and end apart: 9, of which 5 were waited for; matrix products, arithmetic and copies ran while one was open for 0% of the time, Pallas kernels for 15%

profile of v2, /device:TPU:0, one launch (start us, length us, event | category | flops | bytes accessed | tf_op | source)
XLA Modules:
  0.0 38.5 jit_solution(15723734105917575864)
XLA Ops:
  0.6 0.8 %pack.1 = (bf16[80,128]{1,0:T(8,128)(2,1)S(1)}, f32[40,128]{1,0:T(8,128)S(1)}) custom-call(f32[40,128]{1,0:T(8,128)} %mask.1, s32[40,128]{1,0:T(8,128)} %target.1), custom_call_target="tpu_custom_call" | custom-call | tf_op jit(solution)/shard_map/pack/pallas_call | solution.py:419
  1.4 5.1 %collective-permute-start.2 = (bf16[80,128]{1,0:T(8,128)(2,1)S(1)}, bf16[80,128]{1,0:T(8,128)(2,1)S(1)}, u32[]{:S(2)}, u32[]{:S(2)}) collective-permute-start(bf16[80,128]{1,0:T(8,128)(2,1)S(1)} %get-tuple-element.9.refs_0_), channel_id=1, source_target_pairs={{0,24},{8,16},{16,8},{24,0},{1,25},{9,17},{17,9},{25,1},{2,26},{10... | collective-permute-start | bytes 61448 | tf_op jit(solution)/shard_map/ppermute | solution.py:381
  6.5 0.0 collective-permute-start.1
  6.5 0.6 %collective-permute-start = (bf16[80,128]{1,0:T(8,128)(2,1)S(1)}, bf16[80,128]{1,0:T(8,128)(2,1)S(1)}, u32[]{:S(2)}, u32[]{:S(2)}) collective-permute-start(bf16[80,128]{1,0:T(8,128)(2,1)S(1)} %get-tuple-element.9.refs_0_), channel_id=1, source_target_pairs={{0,8},{8,0},{16,24},{24,16},{1,9},{9,1},{17,25},{25,17},{2,10},{10... | collective-permute-start | bytes 61448 | tf_op jit(solution)/shard_map/ppermute | solution.py:381
  7.2 0.0 copy-start
  7.2 0.9 %copy-done = bf16[24,35,35]{2,0,1:T(8,128)(2,1)S(1)} copy-done((bf16[24,35,35]{2,0,1:T(8,128)(2,1)S(1)}, bf16[24,35,35]{2,0,1:T(8,128)(2,1)}, u32[]{:S(2)}) %copy-start) | copy-done | bytes 58824
  8.1 2.8 %bands.1.refs_4_ = bf16[768,2304]{1,0:T(8,128)(2,1)S(1)} custom-call(bf16[35,24,35]{2,1,0:T(8,128)(2,1)S(1)} %bitcast.3), custom_call_target="tpu_custom_call" | custom-call | flops 2000000000 | tf_op jit(solution)/shard_map/bands/pallas_call | solution.py:436
  10.9 0.0 collective-permute-done.2.refs_3_
  10.9 0.3 collective-permute-done.1.refs_2_
  11.2 0.0 collective-permute-done.refs_1_
  11.2 0.0 copy-start.1
  11.2 0.0 copy-start.2
  11.3 0.1 collective-permute-start.3
  11.3 0.7 %collective-permute-start.4 = (bf16[320,128]{1,0:T(8,128)(2,1)S(1)}, bf16[320,128]{1,0:T(8,128)(2,1)S(1)}, u32[]{:S(2)}, u32[]{:S(2)}) collective-permute-start(bf16[320,128]{1,0:T(8,128)(2,1)S(1)} %strip.1.own), channel_id=1, source_target_pairs={{1,2},{2,1},{3,4},{4,3},{5,6},{6,5},{9,10},{10,9},{11,12},{12,11},... | collective-permute-start | bytes 245768 | tf_op jit(solution)/shard_map/ppermute | solution.py:388
  12.0 0.6 %collective-permute-done.3.near = bf16[320,128]{1,0:T(8,128)(2,1)S(1)} collective-permute-done((bf16[320,128]{1,0:T(8,128)(2,1)S(1)}, bf16[320,128]{1,0:T(8,128)(2,1)S(1)}, u32[]{:S(2)}, u32[]{:S(2)}) %collective-permute-start.3) | collective-permute-done | bytes 81952 | tf_op jit(solution)/shard_map/ppermute | solution.py:388
  12.6 3.1 %early.1.field_in = f32[1120,768]{1,0:T(8,128)S(1)} custom-call(bf16[320,128]{1,0:T(8,128)(2,1)S(1)} %strip.1.own, bf16[320,128]{1,0:T(8,128)(2,1)S(1)} %collective-permute-done.3.near, bf16[768,2304]{1,0:T(8,128)(2,1)S(1)} %bands.1.refs_4_), custom_call_target="tpu_custom_call" | custom-call | flops 3500000000 | tf_op jit(solution)/shard_map/early/pallas_call | solution.py:472
  15.7 0.0 collective-permute-done.4.far
  15.7 0.0 copy-done.1
  15.7 0.0 copy-done.2
  15.7 10.6 %late.1 = (f32[40,128]{1,0:T(8,128)S(1)}, f32[16,128]{1,0:T(8,128)S(1)}, f32[1120,768]{1,0:T(8,128)S(1)}) custom-call(s32[2,8]{1,0:T(2,128)S(1)} %bitcast.4, f32[8]{0:T(128)S(1)} %copy-done.2, bf16[320,128]{1,0:T(8,128)(2,1)S(1)} %strip.1.own, bf16[320,128]{1,0:T(8,128)(2,1)S(1)} %collective-permute-done.3.near, ...), custom_call_target="tpu_custom_call", output_to_operand_aliasing={{2}: (6, {})} | custom-call | flops 12000000000 | tf_op jit(solution)/shard_map/late/pallas_call | solution.py:486
  26.3 4.2 %collective-permute-start.7 = (f32[16,128]{1,0:T(8,128)S(1)}, f32[16,128]{1,0:T(8,128)S(1)}, u32[]{:S(2)}, u32[]{:S(2)}) collective-permute-start(f32[16,128]{1,0:T(8,128)S(1)} %get-tuple-element.11), channel_id=1, source_target_pairs={{0,3},{1,2},{2,1},{3,0},{4,7},{5,6},{6,5},{7,4},{8,11},{9,10},{10,... | collective-permute-start | bytes 24584 | tf_op jit(solution)/shard_map/ppermute | solution.py:381
  30.5 0.0 collective-permute-start.6
  30.5 0.2 collective-permute-start.5
  30.7 1.2 %collective-permute-done.7 = f32[16,128]{1,0:T(8,128)S(1)} collective-permute-done((f32[16,128]{1,0:T(8,128)S(1)}, f32[16,128]{1,0:T(8,128)S(1)}, u32[]{:S(2)}, u32[]{:S(2)}) %collective-permute-start.7) | collective-permute-done | bytes 8224 | tf_op jit(solution)/shard_map/ppermute | solution.py:381
  31.9 2.3 %collective-permute-done.6 = f32[16,128]{1,0:T(8,128)S(1)} collective-permute-done((f32[16,128]{1,0:T(8,128)S(1)}, f32[16,128]{1,0:T(8,128)S(1)}, u32[]{:S(2)}, u32[]{:S(2)}) %collective-permute-start.6) | collective-permute-done | bytes 8224 | tf_op jit(solution)/shard_map/ppermute | solution.py:381
  34.2 0.0 collective-permute-done.5
  34.2 0.4 %collective-permute-start.8 = (f32[16,128]{1,0:T(8,128)S(1)}, f32[16,128]{1,0:T(8,128)S(1)}, u32[]{:S(2)}, u32[]{:S(2)}) collective-permute-start(f32[16,128]{1,0:T(8,128)S(1)} %add_add_fusion.refs_0_), channel_id=1, source_target_pairs={{0,4},{1,5},{2,6},{3,7},{4,0},{5,1},{6,2},{7,3},{8,12},{9,13},{10,... | collective-permute-start | bytes 24584 | tf_op jit(solution)/shard_map/ppermute | solution.py:381
  34.6 3.3 %collective-permute-done.8.refs_1_ = f32[16,128]{1,0:T(8,128)S(1)} collective-permute-done((f32[16,128]{1,0:T(8,128)S(1)}, f32[16,128]{1,0:T(8,128)S(1)}, u32[]{:S(2)}, u32[]{:S(2)}) %collective-permute-start.8) | collective-permute-done | bytes 8224 | tf_op jit(solution)/shard_map/ppermute | solution.py:381
  37.9 0.6 %update.1 = (f32[40,128]{1,0:T(8,128)}, f32[1,1]{1,0:T(1,128)}) custom-call(f32[40,128]{1,0:T(8,128)S(1)} %get-tuple-element.8.mask, f32[40,128]{1,0:T(8,128)S(1)} %get-tuple-element.10.grad, f32[16,128]{1,0:T(8,128)S(1)} %add_add_fusion.refs_0_, f32[16,128]{1,0:T(8,128)S(1)} %collective-permute-done.8.refs_1_), custom_call_target="tpu_custom_call" | custom-call | tf_op jit(solution)/shard_map/update/pallas_call | solution.py:514
  (2 shorter events, 0.0 us)
Async XLA Ops:
  1.4 9.5 %collective-permute-start.2 = (bf16[80,128]{1,0:T(8,128)(2,1)S(1)}, bf16[80,128]{1,0:T(8,128)(2,1)S(1)}, u32[]{:S(2)}, u32[]{:S(2)}) collective-permute-start(bf16[80,128]{1,0:T(8,128)(2,1)S(1)} %get-tuple-element.9.refs_0_), channel_id=1, source_target_pairs={{0,24},{8,16},{16,8},{24,0},{1,25},{9,17},{17,9},{25,1},{2,26},{10... | collective-permute-start | bytes 61448 | tf_op jit(solution)/shard_map/ppermute | solution.py:381
  6.5 4.7 %collective-permute-start.1 = (bf16[80,128]{1,0:T(8,128)(2,1)S(1)}, bf16[80,128]{1,0:T(8,128)(2,1)S(1)}, u32[]{:S(2)}, u32[]{:S(2)}) collective-permute-start(bf16[80,128]{1,0:T(8,128)(2,1)S(1)} %get-tuple-element.9.refs_0_), channel_id=1, source_target_pairs={{0,16},{8,24},{16,0},{24,8},{1,17},{9,25},{17,1},{25,9},{2,18},{10... | collective-permute-start | bytes 61448 | tf_op jit(solution)/shard_map/ppermute | solution.py:381
  6.5 4.7 %collective-permute-start = (bf16[80,128]{1,0:T(8,128)(2,1)S(1)}, bf16[80,128]{1,0:T(8,128)(2,1)S(1)}, u32[]{:S(2)}, u32[]{:S(2)}) collective-permute-start(bf16[80,128]{1,0:T(8,128)(2,1)S(1)} %get-tuple-element.9.refs_0_), channel_id=1, source_target_pairs={{0,8},{8,0},{16,24},{24,16},{1,9},{9,1},{17,25},{25,17},{2,10},{10... | collective-permute-start | bytes 61448 | tf_op jit(solution)/shard_map/ppermute | solution.py:381
  7.2 0.9 %copy-start = (bf16[24,35,35]{2,0,1:T(8,128)(2,1)S(1)}, bf16[24,35,35]{2,0,1:T(8,128)(2,1)}, u32[]{:S(2)}) copy-start(bf16[24,35,35]{2,0,1:T(8,128)(2,1)} %param.7) | copy-start | bytes 176404
  11.2 4.5 %copy-start.1 = (s32[8,2]{0,1:T(2,128)S(1)}, s32[8,2]{0,1:T(2,128)}, u32[]{:S(2)}) copy-start(s32[8,2]{0,1:T(2,128)} %param.8) | copy-start | bytes 196
  11.2 4.5 %copy-start.2 = (f32[8]{0:T(128)S(1)}, f32[8]{0:T(128)}, u32[]{:S(2)}) copy-start(f32[8]{0:T(128)} %load_weights.1) | copy-start | bytes 100
  11.3 1.3 %collective-permute-start.3 = (bf16[320,128]{1,0:T(8,128)(2,1)S(1)}, bf16[320,128]{1,0:T(8,128)(2,1)S(1)}, u32[]{:S(2)}, u32[]{:S(2)}) collective-permute-start(bf16[320,128]{1,0:T(8,128)(2,1)S(1)} %strip.1.own), channel_id=1, source_target_pairs={{0,1},{1,0},{2,3},{3,2},{4,5},{5,4},{6,7},{7,6},{8,9},{9,8},{10,11... | collective-permute-start | bytes 245768 | tf_op jit(solution)/shard_map/ppermute | solution.py:388
  11.3 4.4 %collective-permute-start.4 = (bf16[320,128]{1,0:T(8,128)(2,1)S(1)}, bf16[320,128]{1,0:T(8,128)(2,1)S(1)}, u32[]{:S(2)}, u32[]{:S(2)}) collective-permute-start(bf16[320,128]{1,0:T(8,128)(2,1)S(1)} %strip.1.own), channel_id=1, source_target_pairs={{1,2},{2,1},{3,4},{4,3},{5,6},{6,5},{9,10},{10,9},{11,12},{12,11},... | collective-permute-start | bytes 245768 | tf_op jit(solution)/shard_map/ppermute | solution.py:388
  26.3 5.6 %collective-permute-start.7 = (f32[16,128]{1,0:T(8,128)S(1)}, f32[16,128]{1,0:T(8,128)S(1)}, u32[]{:S(2)}, u32[]{:S(2)}) collective-permute-start(f32[16,128]{1,0:T(8,128)S(1)} %get-tuple-element.11), channel_id=1, source_target_pairs={{0,3},{1,2},{2,1},{3,0},{4,7},{5,6},{6,5},{7,4},{8,11},{9,10},{10,... | collective-permute-start | bytes 24584 | tf_op jit(solution)/shard_map/ppermute | solution.py:381
  30.5 3.7 %collective-permute-start.6 = (f32[16,128]{1,0:T(8,128)S(1)}, f32[16,128]{1,0:T(8,128)S(1)}, u32[]{:S(2)}, u32[]{:S(2)}) collective-permute-start(f32[16,128]{1,0:T(8,128)S(1)} %get-tuple-element.11), channel_id=1, source_target_pairs={{0,2},{1,3},{2,0},{3,1},{4,6},{5,7},{6,4},{7,5},{8,10},{9,11},{10,... | collective-permute-start | bytes 24584 | tf_op jit(solution)/shard_map/ppermute | solution.py:381
  30.5 3.7 %collective-permute-start.5 = (f32[16,128]{1,0:T(8,128)S(1)}, f32[16,128]{1,0:T(8,128)S(1)}, u32[]{:S(2)}, u32[]{:S(2)}) collective-permute-start(f32[16,128]{1,0:T(8,128)S(1)} %get-tuple-element.11), channel_id=1, source_target_pairs={{0,1},{1,0},{2,3},{3,2},{4,5},{5,4},{6,7},{7,6},{8,9},{9,8},{10,11... | collective-permute-start | bytes 24584 | tf_op jit(solution)/shard_map/ppermute | solution.py:381
  34.2 3.7 %collective-permute-start.8 = (f32[16,128]{1,0:T(8,128)S(1)}, f32[16,128]{1,0:T(8,128)S(1)}, u32[]{:S(2)}, u32[]{:S(2)}) collective-permute-start(f32[16,128]{1,0:T(8,128)S(1)} %add_add_fusion.refs_0_), channel_id=1, source_target_pairs={{0,4},{1,5},{2,6},{3,7},{4,0},{5,1},{6,2},{7,3},{8,12},{9,13},{10,... | collective-permute-start | bytes 24584 | tf_op jit(solution)/shard_map/ppermute | solution.py:381

commit v3 on v2

--- a/solution.py
+++ b/solution.py
@@ -66,7 +66,7 @@
         end = self.halo + tile_cols
         high = sum(b * self.step + WINDOW > end for b in range(self.blocks))
         self.late = max(low, high)
-        self.acc_rows = self.rows + 8 * ((self.pairs // 2 + 1) // 2) + 8
+        self.acc_rows = -(-(self.rows + taps) // 8) * 8
 
 
 def roll_lanes(value, shift):
@@ -105,7 +105,7 @@
 
 
 def strip_kernel(plan, *refs):
-    pieces, out, hold = refs[: plan.ny], refs[plan.ny + 1], refs[plan.ny + 2]
+    pieces, (out, facing, hold) = refs[: plan.ny], refs[plan.ny + 1 :]
     here = lax.axis_index("gy")
     tile_rows, rows = plan.tile_rows, plan.rows
     for index, piece in enumerate(pieces):
@@ -116,6 +116,11 @@
         hold[1, pl.ds(start, tile_rows), :] = value[tile_rows:]
     out[0:rows, :] = hold[0].astype(jnp.bfloat16)
     out[rows : 2 * rows, :] = hold[1].astype(jnp.bfloat16)
+    even = lax.axis_index("gx") % 2 == 0
+    cols = plan.tile_cols
+    first = jnp.where(even, hold[0], roll_lanes(hold[0], WINDOW - cols))
+    second = jnp.where(even, roll_lanes(hold[1], WINDOW), roll_lanes(hold[1], LANES - cols))
+    facing[...] = jnp.where(lane_index(rows, LANES) < WINDOW, first, second).astype(jnp.bfloat16)
 
 
 def bands_kernel(plan, kernels_ref, bands, row_ref, pairs_ref):
@@ -158,22 +163,31 @@
     return total
 
 
-def read_part(ref, part, rows):
-    value = ref[part * rows : (part + 1) * rows, :].astype(jnp.float32)
-    return jnp.concatenate([value, jnp.zeros((rows, LANES), jnp.float32)], axis=1)
+def widen(value):
+    return jnp.concatenate([value, jnp.zeros_like(value)], axis=1)
 
 
 def join_columns(plan, own, near, far, part):
     rows, tile_cols, halo = plan.rows, plan.tile_cols, plan.halo
-    is_even = lax.axis_index("gx") % 2 == 0
+    here = lax.axis_index("gx")
+    even = here % 2 == 0
     lane = lane_index(rows, WIDE)
-    mid = roll_lanes(read_part(own, part, rows), halo)
-    close = read_part(near, part, rows)
-    remote = jnp.zeros_like(close) if far is None else read_part(far, part, rows)
-    left = roll_lanes(jnp.where(is_even, remote, close), halo - tile_cols)
-    right = roll_lanes(jnp.where(is_even, close, remote), halo + tile_cols)
-    joined = jnp.where(lane < halo, left, jnp.where(lane < halo + tile_cols, mid, right))
-    return jnp.where(lane < tile_cols + 2 * halo, joined, 0.0)
+    mine, close = (
+        widen(ref[part * rows : (part + 1) * rows, :].astype(jnp.float32)) for ref in (own, near)
+    )
+    mine = roll_lanes(mine, halo)
+    to_right = halo + tile_cols
+    close = pltpu.roll(close, jnp.where(even, to_right, WIDE + halo - tile_cols) % WIDE, 1)
+    on_left, on_right = lane < halo, (lane >= to_right) & (lane < to_right + halo)
+    joined = jnp.where((on_left & ~even) | (on_right & even), close, 0.0)
+    joined = jnp.where((lane >= halo) & (lane < to_right), mine, joined)
+    if far is not None:
+        exists = jnp.where(even, here > 0, here < plan.nx - 1)
+        shift = jnp.where(even, halo - WINDOW, to_right) + (WIDE - part * WINDOW)
+        remote = pltpu.roll(widen(far[...].astype(jnp.float32)), shift % WIDE, 1)
+        there = ((on_left & even) | (on_right & ~even)) & exists
+        joined = jnp.where(there, remote, joined)
+    return joined
 
 
 def fill_extended(plan, value, extended):
@@ -225,8 +239,8 @@
     patches,
     image,
     products,
-    even,
-    odd,
+    low,
+    high,
     tall,
 ):
     del field_in
@@ -299,7 +313,14 @@
     narrow = lane_index(rows, LANES) < step
     gains = {}
     for block, operand, _, _, _ in plan.pieces:
-        part = jnp.where(narrow, roll_lanes(inten_grad, -block * step)[:, :LANES], 0.0)
+        begin, end = block * step // LANES, (block * step + step - 1) // LANES
+        if begin == end:
+            part = roll_lanes(
+                inten_grad[:, begin * LANES : (begin + 1) * LANES], begin * LANES - block * step
+            )
+        else:
+            part = roll_lanes(inten_grad, -block * step)[:, :LANES]
+        part = jnp.where(narrow, part, 0.0)
         part = part + roll_lanes(part, SLOT)
         gains[block] = part + roll_lanes(part, 2 * SLOT)
     for operand in range(plan.operand_blocks):
@@ -309,52 +330,60 @@
             for block in sources:
                 piece = field_piece(block, t) * gains[block]
                 value = piece if value is None else value + piece
-            products[operand * rows : (operand + 1) * rows, t * LANES : (t + 1) * LANES] = (
-                value.astype(jnp.bfloat16)
-            )
-
-    even[...] = jnp.zeros_like(even)
-    odd[...] = jnp.zeros_like(odd)
-    for group in range(plan.pairs // 2):
+            lanes = slice(t * LANES, (t + 1) * LANES)
+            products[operand * rows : (operand + 1) * rows, lanes] = value.astype(jnp.bfloat16)
+
+    acc_rows, group_lanes = plan.acc_rows, 2 * LANES
+    low[...] = jnp.zeros_like(low)
+    high[...] = jnp.zeros_like(high)
+
+    def add_groups(index, count):
+        lanes = pl.ds(pl.multiple_of(index * 2 * group_lanes, LANES), count * group_lanes)
         out = lax.dot_general(
-            products[...],
-            bands[:, group * 2 * LANES : (group + 1) * 2 * LANES],
-            NN,
-            preferred_element_type=jnp.float32,
+            products[...], bands[:, lanes], NN, preferred_element_type=jnp.float32
         )
-        held = odd if group % 2 else even
-        start = 8 * (group // 2)
         for operand in range(plan.operand_blocks):
-            base = operand * plan.acc_rows + start
-            held[base : base + rows, :] += out[operand * rows : (operand + 1) * rows, :]
-
-    lane = lane_index(plan.acc_rows, LANES)
+            held = pl.ds(pl.multiple_of(operand * acc_rows + index * 8, 8), rows)
+            block = slice(operand * rows, (operand + 1) * rows)
+            low[held, :] += out[block, :group_lanes]
+            if count == 2:
+                high[held, :] += out[block, group_lanes:]
+
+    def both_groups(index, carry):
+        add_groups(index, 2)
+        return carry
+
+    groups = plan.pairs // 2
+    lax.fori_loop(0, groups // 2, both_groups, 0)
+    if groups % 2:
+        add_groups(groups // 2, 1)
+
+    start_row = plan.radius - 1
+    count = -(-(rows + 1) // 8) * 8
+    lane = lane_index(count, LANES)
     total = [None, None]
     for operand in range(plan.operand_blocks):
-        base = operand * plan.acc_rows
-        tall[8 : 8 + plan.acc_rows, :] = odd[base : base + plan.acc_rows, :]
-        both = even[base : base + plan.acc_rows, :] + tall[4 : 4 + plan.acc_rows, :]
-        tall[8 : 8 + plan.acc_rows, :] = both
-        pair = both[:, :LANES] + tall[6 : 6 + plan.acc_rows, LANES:]
-        for _, index, shift, low, high in plan.pieces:
+        base = operand * acc_rows + start_row
+        pair = None
+        for out, tap in ((low, 0), (low, 2), (high, 4), (high, 6)):
+            lanes = slice(LANES, 2 * LANES) if tap % 4 else slice(0, LANES)
+            piece = out[base - tap : base - tap + count, lanes]
+            pair = piece if pair is None else pair + piece
+        for _, index, shift, lowest, highest in plan.pieces:
             if index != operand:
                 continue
-            keep = (lane >= low + shift) & (lane < high + shift)
+            keep = (lane >= lowest + shift) & (lane < highest + shift)
             for a in range(2):
                 piece = jnp.where(keep, roll_lanes(pair, shift - a * WINDOW), 0.0)
                 total[a] = piece if total[a] is None else total[a] + piece
-    tall[8 : 8 + plan.acc_rows, 0:LANES] = total[0]
-    tall[8 : 8 + plan.acc_rows, LANES:] = total[1]
-    gradient = (
-        tall[8 + plan.radius : 8 + plan.radius + rows, 0:LANES]
-        + tall[7 + plan.radius : 7 + plan.radius + rows, LANES:]
-    )
+    tall[...] = total[0]
+    gradient = tall[1 : 1 + rows, :] + total[1][:rows]
     square = jnp.sum(gradient * gradient)
-    tall[0:rows, 0:LANES] = gradient
+    tall[0:rows, :] = gradient
     start = pl.multiple_of(lax.axis_index("gy") * plan.tile_rows, 8)
-    grad_out[...] = tall[pl.ds(start, plan.tile_rows), 0:LANES]
-    sums_out[0:8, :] = jnp.broadcast_to(loss, (8, LANES))
-    sums_out[8:16, :] = jnp.broadcast_to(square, (8, LANES))
+    grad_out[...] = tall[pl.ds(start, plan.tile_rows), :]
+    sums_out[0:4, :] = jnp.broadcast_to(loss, (4, LANES))
+    sums_out[4:8, :] = jnp.broadcast_to(square, (4, LANES))
 
 
 def update_kernel(plan, mask, grad, *refs):
@@ -362,7 +391,7 @@
     total = sums[0][...]
     for other in sums[1:]:
         total = total + other[...]
-    scale = jnp.sqrt(total[8:9, :] / (plan.rows * plan.cols) + 1e-06)
+    scale = jnp.sqrt(total[4:5, :] / (plan.rows * plan.cols) + 1e-06)
     update[...] = mask[...] - (grad[...] / scale)[:, : plan.tile_cols]
     loss[...] = total[0:1, 0:1]
 
@@ -385,6 +414,8 @@
     pairs = []
     for i in range(first, count - 1, 2):
         pairs += [(i, i + 1), (i + 1, i)]
+    if first and count % 2 == 0:
+        pairs += [(0, count - 1), (count - 1, 0)]
     return lax.ppermute(value, axis, pairs)
 
 
@@ -447,18 +478,21 @@
         name="bands",
     )(in_vmem(jnp.transpose(kernels, (1, 0, 2))))
     bands = in_vmem(bands)
-    strip = pl.pallas_call(
+    strip, facing = pl.pallas_call(
         functools.partial(strip_kernel, plan),
-        out_shape=pltpu.VMEM((2 * rows, LANES), jnp.bfloat16),
+        out_shape=(
+            pltpu.VMEM((2 * rows, LANES), jnp.bfloat16),
+            pltpu.VMEM((rows, LANES), jnp.bfloat16),
+        ),
         in_specs=[VMEM] * ny + [pl.BlockSpec(memory_space=pl.ANY)],
-        out_specs=VMEM,
+        out_specs=(VMEM,) * 2,
         scratch_shapes=[pltpu.VMEM((2, rows, LANES), jnp.float32)],
         compiler_params=params(0),
         cost_estimate=cost(300),
         name="strip",
     )(*[in_vmem(p) for p in pieces], bands)
     near = in_vmem(swap_neighbours(strip, "gx", nx, 0))
-    far = in_vmem(swap_neighbours(strip, "gx", nx, 1))
+    far = in_vmem(swap_neighbours(facing, "gx", nx, 1))
     own = in_vmem(strip)
 
     tall_rows = TOP + rows + 32
@@ -487,7 +521,7 @@
         functools.partial(late_kernel, plan),
         out_shape=(
             pltpu.VMEM((tile_rows, LANES), jnp.float32),
-            pltpu.VMEM((16, LANES), jnp.float32),
+            pltpu.VMEM((8, LANES), jnp.float32),
             field_type,
         ),
         in_specs=[SMEM, SMEM] + [VMEM] * 5,
@@ -499,7 +533,7 @@
             pltpu.VMEM((plan.operand_blocks * rows, plan.wide), jnp.bfloat16),
             pltpu.VMEM((plan.operand_blocks * plan.acc_rows, 2 * LANES), jnp.float32),
             pltpu.VMEM((plan.operand_blocks * plan.acc_rows, 2 * LANES), jnp.float32),
-            pltpu.VMEM((plan.acc_rows + 16, 2 * LANES), jnp.float32),
+            pltpu.VMEM((-(-(rows + 1) // 8) * 8, LANES), jnp.float32),
         ],
         input_output_aliases={6: 2},
         compiler_params=params(

time: 38.7 us -> 36 us (0.930)
  waiting for transfers between devices: 7.68 us -> 4.43 us
  starting transfers between devices: 11.3 us -> 11.9 us
    ppermute x7, waiting for transfers between devices: 7.09 us -> 4.43 us  [fetch(): return lax.ppermute(value, axis, pairs)]
    ppermute x2, starting transfers between devices: 0.74 us -> 2.6 us  [swap_neighbours(): return lax.ppermute(value, axis, pairs)]
    ppermute x7, starting transfers between devices: 10.6 us -> 9.27 us  [fetch(): return lax.ppermute(value, axis, pairs)]
    ppermute x2, waiting for transfers between devices: 0.59 us -> 0.01 us  [swap_neighbours(): return lax.ppermute(value, axis, pairs)]
  transfers between devices with their start and end apart: 9 -> 9, of which waited for: 5 -> 4; matrix products, arithmetic and copies ran while one was open for 0% -> 0% of each run, Pallas kernels for 15% -> 16%
where the time goes in v3:
time: 36 us; the launch traced here: 35.8 us
  Pallas kernels  17.8 us (49%)
  starting transfers between devices  11.9 us (33%)
  waiting for transfers between devices  4.43 us (12%)
  local copies, waits for them, and re-layouts  0.95 us (3%)
  between operations  0.73 us (2%)
    pallas_call x1, Pallas kernels, body(): pl.pallas_call(functools.partial(late_kernel, plan), out_shape=(pltpu.VME...  10.4 us
    ppermute x7, starting transfers between devices, fetch(): return lax.ppermute(value, axis, pairs)  9.27 us
    ppermute x7, waiting for transfers between devices, fetch(): return lax.ppermute(value, axis, pairs)  4.43 us
    pallas_call x1, Pallas kernels, body(): pl.pallas_call(functools.partial(early_kernel, plan), out_shape=field_typ...  3.08 us
    pallas_call x1, Pallas kernels, body(): pl.pallas_call(functools.partial(bands_kernel, plan), out_shape=pltpu.VME...  2.76 us
    ppermute x2, starting transfers between devices, swap_neighbours(): return lax.ppermute(value, axis, pairs)  2.6 us
    unnamed x6, local copies, waits for them, and re-layouts  0.95 us
    pallas_call x1, Pallas kernels, body(): pl.pallas_call(functools.partial(pack_kernel, plan), out_shape=(pltpu.VME...  0.77 us
  transfers between devices with their start and end apart: 9, of which 4 were waited for; matrix products, arithmetic and copies ran while one was open for 0% of the time, Pallas kernels for 16%

profile of v3, /device:TPU:0, one launch (start us, length us, event | category | flops | bytes accessed | tf_op | source)
XLA Modules:
  0.0 35.8 jit_solution(3413067781923192148)
XLA Ops:
  0.6 0.8 %pack.1 = (bf16[80,128]{1,0:T(8,128)(2,1)S(1)}, f32[40,128]{1,0:T(8,128)S(1)}) custom-call(f32[40,128]{1,0:T(8,128)} %mask.1, s32[40,128]{1,0:T(8,128)} %target.1), custom_call_target="tpu_custom_call" | custom-call | tf_op jit(solution)/shard_map/pack/pallas_call | solution.py:450
  1.4 5.1 %collective-permute-start.2 = (bf16[80,128]{1,0:T(8,128)(2,1)S(1)}, bf16[80,128]{1,0:T(8,128)(2,1)S(1)}, u32[]{:S(2)}, u32[]{:S(2)}) collective-permute-start(bf16[80,128]{1,0:T(8,128)(2,1)S(1)} %get-tuple-element.11.refs_0_), channel_id=1, source_target_pairs={{0,24},{8,16},{16,8},{24,0},{1,25},{9,17},{17,9},{25,1},{2,26},{10... | collective-permute-start | bytes 61448 | tf_op jit(solution)/shard_map/ppermute | solution.py:410
  6.5 0.0 collective-permute-start.1
  6.5 0.6 %collective-permute-start = (bf16[80,128]{1,0:T(8,128)(2,1)S(1)}, bf16[80,128]{1,0:T(8,128)(2,1)S(1)}, u32[]{:S(2)}, u32[]{:S(2)}) collective-permute-start(bf16[80,128]{1,0:T(8,128)(2,1)S(1)} %get-tuple-element.11.refs_0_), channel_id=1, source_target_pairs={{0,8},{8,0},{16,24},{24,16},{1,9},{9,1},{17,25},{25,17},{2,10},{10... | collective-permute-start | bytes 61448 | tf_op jit(solution)/shard_map/ppermute | solution.py:410
  7.2 0.0 copy-start
  7.2 0.9 %copy-done = bf16[24,35,35]{2,0,1:T(8,128)(2,1)S(1)} copy-done((bf16[24,35,35]{2,0,1:T(8,128)(2,1)S(1)}, bf16[24,35,35]{2,0,1:T(8,128)(2,1)}, u32[]{:S(2)}) %copy-start) | copy-done | bytes 58824
  8.1 2.8 %bands.1.refs_4_ = bf16[768,2304]{1,0:T(8,128)(2,1)S(1)} custom-call(bf16[35,24,35]{2,1,0:T(8,128)(2,1)S(1)} %bitcast.3), custom_call_target="tpu_custom_call" | custom-call | flops 2000000000 | tf_op jit(solution)/shard_map/bands/pallas_call | solution.py:467
  10.9 0.0 collective-permute-done.2.refs_3_
  10.9 0.3 collective-permute-done.1.refs_2_
  11.2 0.0 collective-permute-done.refs_1_
  11.2 0.1 strip.1
  11.3 0.1 collective-permute-start.3
  11.4 0.0 copy-start.1
  11.4 0.0 copy-start.2
  11.4 2.5 %collective-permute-start.4 = (bf16[160,128]{1,0:T(8,128)(2,1)S(1)}, bf16[160,128]{1,0:T(8,128)(2,1)S(1)}, u32[]{:S(2)}, u32[]{:S(2)}) collective-permute-start(bf16[160,128]{1,0:T(8,128)(2,1)S(1)} %get-tuple-element.13), channel_id=1, source_target_pairs={{1,2},{2,1},{3,4},{4,3},{5,6},{6,5},{0,7},{7,0},{9,10},{10,9},{11,... | collective-permute-start | bytes 122888 | tf_op jit(solution)/shard_map/ppermute | solution.py:419
  14.0 0.0 collective-permute-done.3.near
  14.0 3.1 %early.1.field_in = f32[1120,768]{1,0:T(8,128)S(1)} custom-call(bf16[320,128]{1,0:T(8,128)(2,1)S(1)} %get-tuple-element.12.own, bf16[320,128]{1,0:T(8,128)(2,1)S(1)} %collective-permute-done.3.near, bf16[768,2304]{1,0:T(8,128)(2,1)S(1)} %bands.1.refs_4_), custom_call_target="tpu_custom_call" | custom-call | flops 3500000000 | tf_op jit(solution)/shard_map/early/pallas_call | solution.py:506
  17.0 0.0 collective-permute-done.4.far
  17.0 0.0 copy-done.1
  17.1 0.0 copy-done.2
  17.1 10.4 %late.1 = (f32[40,128]{1,0:T(8,128)S(1)}, f32[8,128]{1,0:T(8,128)S(1)}, f32[1120,768]{1,0:T(8,128)S(1)}) custom-call(s32[2,8]{1,0:T(2,128)S(1)} %bitcast.4, f32[8]{0:T(128)S(1)} %copy-done.2, bf16[320,128]{1,0:T(8,128)(2,1)S(1)} %get-tuple-element.12.own, bf16[320,128]{1,0:T(8,128)(2,1)S(1)} %collective-permute-done.3.near, ...), custom_call_target="tpu_custom_call", output_to_operand_aliasing={{2}: (6, {})} | custom-call | flops 12000000000 | tf_op jit(solution)/shard_map/late/pallas_call | solution.py:520
  27.5 0.3 collective-permute-start.7
  27.8 0.5 %collective-permute-start.6 = (f32[8,128]{1,0:T(8,128)S(1)}, f32[8,128]{1,0:T(8,128)S(1)}, u32[]{:S(2)}, u32[]{:S(2)}) collective-permute-start(f32[8,128]{1,0:T(8,128)S(1)} %get-tuple-element.15), channel_id=1, source_target_pairs={{0,2},{1,3},{2,0},{3,1},{4,6},{5,7},{6,4},{7,5},{8,10},{9,11},{10,... | collective-permute-start | bytes 12296 | tf_op jit(solution)/shard_map/ppermute | solution.py:410
  28.4 1.1 %collective-permute-start.5 = (f32[8,128]{1,0:T(8,128)S(1)}, f32[8,128]{1,0:T(8,128)S(1)}, u32[]{:S(2)}, u32[]{:S(2)}) collective-permute-start(f32[8,128]{1,0:T(8,128)S(1)} %get-tuple-element.15), channel_id=1, source_target_pairs={{0,1},{1,0},{2,3},{3,2},{4,5},{5,4},{6,7},{7,6},{8,9},{9,8},{10,11... | collective-permute-start | bytes 12296 | tf_op jit(solution)/shard_map/ppermute | solution.py:410
  29.4 1.2 %collective-permute-done.7 = f32[8,128]{1,0:T(8,128)S(1)} collective-permute-done((f32[8,128]{1,0:T(8,128)S(1)}, f32[8,128]{1,0:T(8,128)S(1)}, u32[]{:S(2)}, u32[]{:S(2)}) %collective-permute-start.7) | collective-permute-done | bytes 4128 | tf_op jit(solution)/shard_map/ppermute | solution.py:410
  30.6 0.8 %collective-permute-done.6 = f32[8,128]{1,0:T(8,128)S(1)} collective-permute-done((f32[8,128]{1,0:T(8,128)S(1)}, f32[8,128]{1,0:T(8,128)S(1)}, u32[]{:S(2)}, u32[]{:S(2)}) %collective-permute-start.6) | collective-permute-done | bytes 4128 | tf_op jit(solution)/shard_map/ppermute | solution.py:410
  31.5 0.0 collective-permute-done.5
  31.5 1.6 %collective-permute-start.8 = (f32[8,128]{1,0:T(8,128)S(1)}, f32[8,128]{1,0:T(8,128)S(1)}, u32[]{:S(2)}, u32[]{:S(2)}) collective-permute-start(f32[8,128]{1,0:T(8,128)S(1)} %add_add_fusion.refs_0_), channel_id=1, source_target_pairs={{0,4},{1,5},{2,6},{3,7},{4,0},{5,1},{6,2},{7,3},{8,12},{9,13},{10,... | collective-permute-start | bytes 12296 | tf_op jit(solution)/shard_map/ppermute | solution.py:410
  33.0 2.1 %collective-permute-done.8.refs_1_ = f32[8,128]{1,0:T(8,128)S(1)} collective-permute-done((f32[8,128]{1,0:T(8,128)S(1)}, f32[8,128]{1,0:T(8,128)S(1)}, u32[]{:S(2)}, u32[]{:S(2)}) %collective-permute-start.8) | collective-permute-done | bytes 4128 | tf_op jit(solution)/shard_map/ppermute | solution.py:410
  35.1 0.6 %update.1 = (f32[40,128]{1,0:T(8,128)}, f32[1,1]{1,0:T(1,128)}) custom-call(f32[40,128]{1,0:T(8,128)S(1)} %get-tuple-element.10.mask, f32[40,128]{1,0:T(8,128)S(1)} %get-tuple-element.14.grad, f32[8,128]{1,0:T(8,128)S(1)} %add_add_fusion.refs_0_, f32[8,128]{1,0:T(8,128)S(1)} %collective-permute-done.8.refs_1_), custom_call_target="tpu_custom_call" | custom-call | tf_op jit(solution)/shard_map/update/pallas_call | solution.py:548
  (1 shorter events, 0.0 us)
Async XLA Ops:
  1.4 9.5 %collective-permute-start.2 = (bf16[80,128]{1,0:T(8,128)(2,1)S(1)}, bf16[80,128]{1,0:T(8,128)(2,1)S(1)}, u32[]{:S(2)}, u32[]{:S(2)}) collective-permute-start(bf16[80,128]{1,0:T(8,128)(2,1)S(1)} %get-tuple-element.11.refs_0_), channel_id=1, source_target_pairs={{0,24},{8,16},{16,8},{24,0},{1,25},{9,17},{17,9},{25,1},{2,26},{10... | collective-permute-start | bytes 61448 | tf_op jit(solution)/shard_map/ppermute | solution.py:410
  6.5 4.7 %collective-permute-start.1 = (bf16[80,128]{1,0:T(8,128)(2,1)S(1)}, bf16[80,128]{1,0:T(8,128)(2,1)S(1)}, u32[]{:S(2)}, u32[]{:S(2)}) collective-permute-start(bf16[80,128]{1,0:T(8,128)(2,1)S(1)} %get-tuple-element.11.refs_0_), channel_id=1, source_target_pairs={{0,16},{8,24},{16,0},{24,8},{1,17},{9,25},{17,1},{25,9},{2,18},{10... | collective-permute-start | bytes 61448 | tf_op jit(solution)/shard_map/ppermute | solution.py:410
  6.5 4.7 %collective-permute-start = (bf16[80,128]{1,0:T(8,128)(2,1)S(1)}, bf16[80,128]{1,0:T(8,128)(2,1)S(1)}, u32[]{:S(2)}, u32[]{:S(2)}) collective-permute-start(bf16[80,128]{1,0:T(8,128)(2,1)S(1)} %get-tuple-element.11.refs_0_), channel_id=1, source_target_pairs={{0,8},{8,0},{16,24},{24,16},{1,9},{9,1},{17,25},{25,17},{2,10},{10... | collective-permute-start | bytes 61448 | tf_op jit(solution)/shard_map/ppermute | solution.py:410
  7.2 0.9 %copy-start = (bf16[24,35,35]{2,0,1:T(8,128)(2,1)S(1)}, bf16[24,35,35]{2,0,1:T(8,128)(2,1)}, u32[]{:S(2)}) copy-start(bf16[24,35,35]{2,0,1:T(8,128)(2,1)} %param.7) | copy-start | bytes 176404
  11.3 2.6 %collective-permute-start.3 = (bf16[320,128]{1,0:T(8,128)(2,1)S(1)}, bf16[320,128]{1,0:T(8,128)(2,1)S(1)}, u32[]{:S(2)}, u32[]{:S(2)}) collective-permute-start(bf16[320,128]{1,0:T(8,128)(2,1)S(1)} %get-tuple-element.12.own), channel_id=1, source_target_pairs={{0,1},{1,0},{2,3},{3,2},{4,5},{5,4},{6,7},{7,6},{8,9},{9,8},{10,11... | collective-permute-start | bytes 245768 | tf_op jit(solution)/shard_map/ppermute | solution.py:419
  11.4 5.6 %copy-start.1 = (s32[8,2]{0,1:T(2,128)S(1)}, s32[8,2]{0,1:T(2,128)}, u32[]{:S(2)}) copy-start(s32[8,2]{0,1:T(2,128)} %param.8) | copy-start | bytes 196
  11.4 5.6 %copy-start.2 = (f32[8]{0:T(128)S(1)}, f32[8]{0:T(128)}, u32[]{:S(2)}) copy-start(f32[8]{0:T(128)} %load_weights.1) | copy-start | bytes 100
  11.4 5.6 %collective-permute-start.4 = (bf16[160,128]{1,0:T(8,128)(2,1)S(1)}, bf16[160,128]{1,0:T(8,128)(2,1)S(1)}, u32[]{:S(2)}, u32[]{:S(2)}) collective-permute-start(bf16[160,128]{1,0:T(8,128)(2,1)S(1)} %get-tuple-element.13), channel_id=1, source_target_pairs={{1,2},{2,1},{3,4},{4,3},{5,6},{6,5},{0,7},{7,0},{9,10},{10,9},{11,... | collective-permute-start | bytes 122888 | tf_op jit(solution)/shard_map/ppermute | solution.py:419
  27.5 3.1 %collective-permute-start.7 = (f32[8,128]{1,0:T(8,128)S(1)}, f32[8,128]{1,0:T(8,128)S(1)}, u32[]{:S(2)}, u32[]{:S(2)}) collective-permute-start(f32[8,128]{1,0:T(8,128)S(1)} %get-tuple-element.15), channel_id=1, source_target_pairs={{0,3},{1,2},{2,1},{3,0},{4,7},{5,6},{6,5},{7,4},{8,11},{9,10},{10,... | collective-permute-start | bytes 12296 | tf_op jit(solution)/shard_map/ppermute | solution.py:410
  27.8 3.6 %collective-permute-start.6 = (f32[8,128]{1,0:T(8,128)S(1)}, f32[8,128]{1,0:T(8,128)S(1)}, u32[]{:S(2)}, u32[]{:S(2)}) collective-permute-start(f32[8,128]{1,0:T(8,128)S(1)} %get-tuple-element.15), channel_id=1, source_target_pairs={{0,2},{1,3},{2,0},{3,1},{4,6},{5,7},{6,4},{7,5},{8,10},{9,11},{10,... | collective-permute-start | bytes 12296 | tf_op jit(solution)/shard_map/ppermute | solution.py:410
  28.4 3.1 %collective-permute-start.5 = (f32[8,128]{1,0:T(8,128)S(1)}, f32[8,128]{1,0:T(8,128)S(1)}, u32[]{:S(2)}, u32[]{:S(2)}) collective-permute-start(f32[8,128]{1,0:T(8,128)S(1)} %get-tuple-element.15), channel_id=1, source_target_pairs={{0,1},{1,0},{2,3},{3,2},{4,5},{5,4},{6,7},{7,6},{8,9},{9,8},{10,11... | collective-permute-start | bytes 12296 | tf_op jit(solution)/shard_map/ppermute | solution.py:410
  31.5 3.7 %collective-permute-start.8 = (f32[8,128]{1,0:T(8,128)S(1)}, f32[8,128]{1,0:T(8,128)S(1)}, u32[]{:S(2)}, u32[]{:S(2)}) collective-permute-start(f32[8,128]{1,0:T(8,128)S(1)} %add_add_fusion.refs_0_), channel_id=1, source_target_pairs={{0,4},{1,5},{2,6},{3,7},{4,0},{5,1},{6,2},{7,3},{8,12},{9,13},{10,... | collective-permute-start | bytes 12296 | tf_op jit(solution)/shard_map/ppermute | solution.py:410

commit v4 on v3

--- a/solution.py
+++ b/solution.py
@@ -20,12 +20,12 @@
 SLOT = 32
 WIDE = 256
 TOP = 24
+CHUNK = 32
 PAD = 8
 
 NT = (((1,), (1,)), ((), ()))
 NN = (((1,), (0,)), ((), ()))
 VMEM = pl.BlockSpec(memory_space=pltpu.VMEM)
-SMEM = pl.BlockSpec(memory_space=pltpu.SMEM)
 
 
 class Plan:
@@ -77,14 +77,13 @@
     return lax.broadcasted_iota(jnp.int32, (rows, lanes), 1)
 
 
-def shifted_image(ref, rows, down, right):
-    start = PAD + down
-    rest = lax.rem(start, 8)
-    base = pl.multiple_of(start - rest, 8)
-    tiles = ref[pl.ds(base, rows + 8), :].reshape(rows // 8 + 1, 8, WIDE)
+def shifted_chunk(ref, start, down, right):
+    rest = lax.rem(PAD + down, 8)
+    base = pl.multiple_of(start + PAD + down - rest, 8)
+    tiles = ref[pl.ds(base, CHUNK + 8), :].reshape(CHUNK // 8 + 1, 8, WIDE)
     tiles = pltpu.roll(tiles, lax.rem(8 - rest, 8), 1)
-    row = lax.broadcasted_iota(jnp.int32, (rows // 8, 8, WIDE), 1)
-    value = jnp.where(row < 8 - rest, tiles[:-1], tiles[1:]).reshape(rows, WIDE)
+    row = lax.broadcasted_iota(jnp.int32, (CHUNK // 8, 8, WIDE), 1)
+    value = jnp.where(row < 8 - rest, tiles[:-1], tiles[1:]).reshape(CHUNK, WIDE)
     return pltpu.roll(value, lax.rem(WIDE - right, WIDE), 1)
 
 
@@ -104,8 +103,13 @@
     both[rows : 2 * rows, 0:cols] = target_in[...].astype(jnp.float32).astype(jnp.bfloat16)
 
 
+def entries(row):
+    column = lane_index(1, row.shape[1])
+    return [jnp.sum(jnp.where(column == i, row, 0)) for i in range(row.shape[1])]
+
+
 def strip_kernel(plan, *refs):
-    pieces, (out, facing, hold) = refs[: plan.ny], refs[plan.ny + 1 :]
+    pieces, (out, to_near, to_far, hold) = refs[: plan.ny], refs[plan.ny + 1 :]
     here = lax.axis_index("gy")
     tile_rows, rows = plan.tile_rows, plan.rows
     for index, piece in enumerate(pieces):
@@ -118,9 +122,11 @@
     out[rows : 2 * rows, :] = hold[1].astype(jnp.bfloat16)
     even = lax.axis_index("gx") % 2 == 0
     cols = plan.tile_cols
-    first = jnp.where(even, hold[0], roll_lanes(hold[0], WINDOW - cols))
-    second = jnp.where(even, roll_lanes(hold[1], WINDOW), roll_lanes(hold[1], LANES - cols))
-    facing[...] = jnp.where(lane_index(rows, LANES) < WINDOW, first, second).astype(jnp.bfloat16)
+    first = lane_index(rows, LANES) < WINDOW
+    low = jnp.where(first, hold[0], roll_lanes(hold[1], WINDOW))
+    high = jnp.where(first, roll_lanes(hold[0], WINDOW - cols), roll_lanes(hold[1], LANES - cols))
+    to_near[...] = jnp.where(even, high, low).astype(jnp.bfloat16)
+    to_far[...] = jnp.where(even, low, high).astype(jnp.bfloat16)
 
 
 def bands_kernel(plan, kernels_ref, bands, row_ref, pairs_ref):
@@ -147,54 +153,72 @@
     lax.fori_loop(0, channels, channel, 0)
 
 
-def smooth_rows(ref, rows):
-    total = None
-    for a in range(5):
-        term = SMOOTH_TAPS[a] * ref[pl.ds(PAD + a - 2, rows), :]
-        total = term if total is None else total + term
-    return total
-
-
-def smooth_cols(value):
-    total = None
-    for b in range(5):
-        term = SMOOTH_TAPS[b] * (value if b == 2 else roll_lanes(value, 2 - b))
-        total = term if total is None else total + term
-    return total
+def smooth_chunk(ref, start):
+    rows = [chunk_at(ref, start, PAD + a) for a in (-2, -1, 0, 1, 2)]
+    total = SMOOTH_TAPS[2] * rows[2]
+    total = total + SMOOTH_TAPS[1] * (rows[1] + rows[3]) + SMOOTH_TAPS[0] * (rows[0] + rows[4])
+    cols = [total if b == 0 else roll_lanes(total, -b) for b in (-2, -1, 0, 1, 2)]
+    total = SMOOTH_TAPS[2] * cols[2]
+    return total + SMOOTH_TAPS[1] * (cols[1] + cols[3]) + SMOOTH_TAPS[0] * (cols[0] + cols[4])
 
 
 def widen(value):
     return jnp.concatenate([value, jnp.zeros_like(value)], axis=1)
 
 
-def join_columns(plan, own, near, far, part):
-    rows, tile_cols, halo = plan.rows, plan.tile_cols, plan.halo
+def each_chunk(rows, work):
+    count = rows // CHUNK
+    if count <= 8:
+        results = [work(i * CHUNK) for i in range(count)]
+        return None if results[0] is None else functools.reduce(jnp.add, results)
+    zero = jax.eval_shape(lambda: work(0))
+
+    def step(index, total):
+        result = work(pl.multiple_of(index * CHUNK, CHUNK))
+        return None if result is None else total + result
+
+    return lax.fori_loop(0, count, step, None if zero is None else jnp.zeros(zero.shape, zero.dtype))
+
+
+def chunk_at(ref, start, offset):
+    if isinstance(start, int):
+        return ref[start + offset : start + offset + CHUNK, :]
+    return ref[pl.ds(start, CHUNK + 2 * PAD), :][offset : offset + CHUNK]
+
+
+def join_columns(plan, own, near, far, part, start):
+    tile_cols, halo = plan.tile_cols, plan.halo
     here = lax.axis_index("gx")
     even = here % 2 == 0
-    lane = lane_index(rows, WIDE)
-    mine, close = (
-        widen(ref[part * rows : (part + 1) * rows, :].astype(jnp.float32)) for ref in (own, near)
-    )
-    mine = roll_lanes(mine, halo)
+    lane = lane_index(CHUNK, WIDE)
     to_right = halo + tile_cols
-    close = pltpu.roll(close, jnp.where(even, to_right, WIDE + halo - tile_cols) % WIDE, 1)
     on_left, on_right = lane < halo, (lane >= to_right) & (lane < to_right + halo)
-    joined = jnp.where((on_left & ~even) | (on_right & even), close, 0.0)
-    joined = jnp.where((lane >= halo) & (lane < to_right), mine, joined)
+
+    def side(ref, right):
+        shift = jnp.where(right, to_right, halo - WINDOW) + (WIDE - part * WINDOW)
+        value = widen(ref[pl.ds(start, CHUNK), :].astype(jnp.float32))
+        return pltpu.roll(value, shift % WIDE, 1), (on_left & ~right) | (on_right & right)
+
+    mine = widen(own[pl.ds(part * plan.rows + start, CHUNK), :].astype(jnp.float32))
+    value, there = side(near, even)
+    joined = jnp.where(there, value, 0.0)
+    joined = jnp.where((lane >= halo) & (lane < to_right), roll_lanes(mine, halo), joined)
     if far is not None:
+        value, there = side(far, ~even)
         exists = jnp.where(even, here > 0, here < plan.nx - 1)
-        shift = jnp.where(even, halo - WINDOW, to_right) + (WIDE - part * WINDOW)
-        remote = pltpu.roll(widen(far[...].astype(jnp.float32)), shift % WIDE, 1)
-        there = ((on_left & even) | (on_right & ~even)) & exists
-        joined = jnp.where(there, remote, joined)
+        joined = jnp.where(there & exists, value, joined)
     return joined
 
 
-def fill_extended(plan, value, extended):
+def fill_extended(plan, own, near, far, extended):
     rows, tall_rows = plan.rows, extended.shape[0]
     extended[0:TOP, :] = jnp.zeros((TOP, WIDE), jnp.float32)
-    extended[TOP : TOP + rows, :] = value
     extended[TOP + rows : tall_rows, :] = jnp.zeros((tall_rows - TOP - rows, WIDE), jnp.float32)
+
+    def fill(start):
+        extended[pl.ds(TOP + start, CHUNK), :] = join_columns(plan, own, near, far, 0, start)
+
+    each_chunk(rows, fill)
 
 
 def fill_patches(plan, block, index, extended, turned, pairs_ref, patches):
@@ -203,16 +227,20 @@
     window = pltpu.roll(extended[...], lax.rem(WIDE - block * plan.step, WIDE), 1)[:, :LANES]
     turned[...] = roll_lanes(window, WINDOW)
     pairs_ref[0:body_rows, :] = jnp.where(half, window[0:body_rows], turned[1 : body_rows + 1, :])
-    for q in range(plan.pairs):
+    for q in range(8):
         start = TOP - plan.radius + 2 * q
-        patches[index * rows : (index + 1) * rows, q * LANES : (q + 1) * LANES] = pairs_ref[
-            start : start + rows, :
-        ].astype(jnp.bfloat16)
+        uses = range(q, plan.pairs, 8)
+        height = rows + 16 * (len(uses) - 1)
+        value = pairs_ref[start : start + height, :].astype(jnp.bfloat16)
+        for tile, pair in enumerate(uses):
+            patches[index * rows : (index + 1) * rows, pair * LANES : (pair + 1) * LANES] = value[
+                16 * tile : 16 * tile + rows
+            ]
 
 
 def early_kernel(plan, own, near, bands, field, extended, turned, pairs_ref, patches):
     rows, late, blocks = plan.rows, plan.late, plan.blocks
-    fill_extended(plan, join_columns(plan, own, near, None, 0), extended)
+    fill_extended(plan, own, near, None, extended)
     first = jnp.where(lax.axis_index("gx") % 2 == 0, late, 0)
     for index in range(blocks - late):
         fill_patches(plan, first + index, index, extended, turned, pairs_ref, patches)
@@ -237,21 +265,24 @@
     turned,
     pairs_ref,
     patches,
-    image,
+    intensity,
+    develop,
+    resid,
+    dense_grad,
     products,
     low,
     high,
     tall,
 ):
     del field_in
+    downs, rights = (entries(offsets[axis : axis + 1, :]) for axis in range(2))
+    load_gains = entries(load_weights[...] * (LOADING_GAIN / LOAD_TAPS))
     rows, tile_cols, step = plan.rows, plan.tile_cols, plan.step
     late, blocks = plan.late, plan.blocks
     here = lax.axis_index("gx")
     is_even = here % 2 == 0
     first_col = here * tile_cols
-    lane = lane_index(rows, WIDE)
-    fill_extended(plan, join_columns(plan, own, near, far, 0), extended)
-    target = roll_lanes(join_columns(plan, own, near, far, 1), -plan.radius)
+    fill_extended(plan, own, near, far, extended)
     first = jnp.where(is_even, 0, blocks - late)
     for index in range(late):
         fill_patches(plan, first + index, index, extended, turned, pairs_ref, patches)
@@ -259,79 +290,98 @@
         patches[...], bands[...], NT, preferred_element_type=jnp.float32
     )
 
-    def field_piece(block, t):
+    def field_piece(block, t, start):
         slot = jnp.where(is_even, block, (block + late) % blocks)
-        start = pl.multiple_of(slot * rows, 8)
-        return field[pl.ds(start, rows), t * LANES : (t + 1) * LANES]
-
+        first = pl.multiple_of(slot * rows + start, 8)
+        return field[pl.ds(first, CHUNK), t * LANES : (t + 1) * LANES]
+
+    lane = lane_index(CHUNK, WIDE)
+    near_lane = lane_index(CHUNK, LANES)
     col = lane + (first_col - plan.field_halo)
     inside = (col >= 0) & (col < plan.cols)
-    total = jnp.zeros((rows, WIDE), jnp.float32)
-    for block in range(plan.blocks):
-        power = None
-        for t in range(plan.wide // LANES):
-            piece = field_piece(block, t)
-            power = piece * piece if power is None else power + piece * piece
-        power = power + roll_lanes(power, 2 * SLOT)
-        power = power + roll_lanes(power, SLOT)
-        power = roll_lanes(jnp.concatenate([power, power], axis=1), block * step)
-        total = jnp.where((lane >= block * step) & (lane < (block + 1) * step), power, total)
     kernels_count = plan.channels // 2
-    intensity = jnp.where(inside, total / kernels_count, 0.0)
-    zeros = jnp.zeros((PAD, WIDE), jnp.float32)
-    image[0:PAD, :] = zeros
-    image[PAD + rows : 3 * PAD + rows, :] = jnp.concatenate([zeros, zeros], axis=0)
-    image[PAD : PAD + rows, :] = intensity
-    dense = smooth_cols(smooth_rows(image, rows))
-    develop = jnp.where(inside, jax.nn.sigmoid(SHARPNESS * (dense - THRESHOLD)), 0.0)
-
-    image[PAD : PAD + rows, :] = develop
-    loading = jnp.zeros((rows, WIDE), jnp.float32)
-    for index in range(LOAD_TAPS):
-        shifted = shifted_image(image, rows, offsets[0, index], offsets[1, index])
-        loading = loading + load_weights[index] * shifted
-    printed = develop - LOADING_GAIN / LOAD_TAPS * loading
-    row_pos = lax.broadcasted_iota(jnp.int32, (rows, WIDE), 0).astype(jnp.float32)
-    weight = (1.0 + 2.0 * row_pos / rows) * (1.0 + 2.0 * col.astype(jnp.float32) / plan.cols)
-    diff = printed - target
-    weighted = weight * diff
-    mine = (lane >= plan.field_halo) & (lane < plan.field_halo + tile_cols)
-    loss = jnp.sum(jnp.where(mine, weighted * diff, 0.0))
-    resid = jnp.where(inside, 2.0 * weighted, 0.0)
-
-    image[PAD : PAD + rows, :] = resid
-    back = jnp.zeros((rows, WIDE), jnp.float32)
-    for index in range(LOAD_TAPS):
-        shifted = shifted_image(image, rows, -offsets[0, index], -offsets[1, index])
-        back = back + load_weights[index] * shifted
-    slope = resid - LOADING_GAIN / LOAD_TAPS * back
-    image[PAD : PAD + rows, :] = slope * SHARPNESS * develop * (1.0 - develop)
-    inten_grad = smooth_cols(smooth_rows(image, rows)) * (2.0 / kernels_count)
+    for image in (intensity, develop, resid, dense_grad):
+        image[0:PAD, :] = jnp.zeros((PAD, WIDE), jnp.float32)
+        image[PAD + rows : 3 * PAD + rows, :] = jnp.zeros((2 * PAD, WIDE), jnp.float32)
+
+    def find_intensity(start):
+        halves = [jnp.zeros((CHUNK, LANES), jnp.float32)] * (WIDE // LANES)
+        for block in range(blocks):
+            power = None
+            for t in range(plan.wide // LANES):
+                piece = field_piece(block, t, start)
+                power = piece * piece if power is None else power + piece * piece
+            power = power + roll_lanes(power, 2 * SLOT)
+            power = power + roll_lanes(power, SLOT)
+            power = roll_lanes(power, block * step)
+            for half in range(WIDE // LANES):
+                low_lane = block * step - half * LANES
+                if -step < low_lane < LANES:
+                    here_too = (near_lane >= low_lane) & (near_lane < low_lane + step)
+                    halves[half] = jnp.where(here_too, power, halves[half])
+        total = jnp.concatenate(halves, axis=1) / kernels_count
+        intensity[pl.ds(PAD + start, CHUNK), :] = jnp.where(inside, total, 0.0)
+
+    def find_develop(start):
+        dense = smooth_chunk(intensity, start)
+        value = jnp.where(inside, jax.nn.sigmoid(SHARPNESS * (dense - THRESHOLD)), 0.0)
+        develop[pl.ds(PAD + start, CHUNK), :] = value
+
+    def find_resid(start):
+        printed = develop[pl.ds(PAD + start, CHUNK), :]
+        for down, right, gain in zip(downs, rights, load_gains):
+            printed = printed - gain * shifted_chunk(develop, start, down, right)
+        target = roll_lanes(join_columns(plan, own, near, far, 1, start), -plan.radius)
+        row = lax.broadcasted_iota(jnp.int32, (CHUNK, WIDE), 0) + start
+        weight = (1.0 + 2.0 * row.astype(jnp.float32) / rows) * (
+            1.0 + 2.0 * col.astype(jnp.float32) / plan.cols
+        )
+        diff = printed - target
+        weighted = weight * diff
+        resid[pl.ds(PAD + start, CHUNK), :] = jnp.where(inside, 2.0 * weighted, 0.0)
+        mine = (lane >= plan.field_halo) & (lane < plan.field_halo + tile_cols)
+        part = jnp.where(mine, weighted * diff, 0.0)
+        return jnp.sum(part.reshape(CHUNK // 8, 8, WIDE), axis=0)
+
+    def find_dense_grad(start):
+        slope = resid[pl.ds(PAD + start, CHUNK), :]
+        for down, right, gain in zip(downs, rights, load_gains):
+            slope = slope - gain * shifted_chunk(resid, start, -down, -right)
+        value = develop[pl.ds(PAD + start, CHUNK), :]
+        dense_grad[pl.ds(PAD + start, CHUNK), :] = slope * SHARPNESS * value * (1.0 - value)
+
     used = inside & (lane >= plan.lo) & (lane < plan.hi)
-    inten_grad = jnp.where(used, inten_grad, 0.0)
-
-    narrow = lane_index(rows, LANES) < step
-    gains = {}
-    for block, operand, _, _, _ in plan.pieces:
-        begin, end = block * step // LANES, (block * step + step - 1) // LANES
-        if begin == end:
-            part = roll_lanes(
-                inten_grad[:, begin * LANES : (begin + 1) * LANES], begin * LANES - block * step
-            )
-        else:
-            part = roll_lanes(inten_grad, -block * step)[:, :LANES]
-        part = jnp.where(narrow, part, 0.0)
-        part = part + roll_lanes(part, SLOT)
-        gains[block] = part + roll_lanes(part, 2 * SLOT)
-    for operand in range(plan.operand_blocks):
-        sources = [p[0] for p in plan.pieces if p[1] == operand]
-        for t in range(plan.wide // LANES):
-            value = None
-            for block in sources:
-                piece = field_piece(block, t) * gains[block]
-                value = piece if value is None else value + piece
-            lanes = slice(t * LANES, (t + 1) * LANES)
-            products[operand * rows : (operand + 1) * rows, lanes] = value.astype(jnp.bfloat16)
+    narrow = near_lane < step
+
+    def find_products(start):
+        inten_grad = smooth_chunk(dense_grad, start) * (2.0 / kernels_count)
+        inten_grad = jnp.where(used, inten_grad, 0.0)
+        halves = [inten_grad[:, h * LANES : (h + 1) * LANES] for h in range(WIDE // LANES)]
+        gains = {}
+        for block in range(plan.pieces[0][0], plan.pieces[-1][0] + 1):
+            half, begin = divmod(block * step, LANES)
+            part = halves[half]
+            if begin + step > LANES:
+                part = jnp.where(near_lane >= begin, part, halves[half + 1])
+            part = jnp.where(narrow, roll_lanes(part, -begin), 0.0)
+            part = part + roll_lanes(part, SLOT)
+            gains[block] = part + roll_lanes(part, 2 * SLOT)
+        for operand in range(plan.operand_blocks):
+            sources = [p[0] for p in plan.pieces if p[1] == operand]
+            for t in range(plan.wide // LANES):
+                value = None
+                for block in sources:
+                    piece = field_piece(block, t, start) * gains[block]
+                    value = piece if value is None else value + piece
+                products[
+                    pl.ds(operand * rows + start, CHUNK), t * LANES : (t + 1) * LANES
+                ] = value.astype(jnp.bfloat16)
+
+    each_chunk(rows, find_intensity)
+    each_chunk(rows, find_develop)
+    loss = jnp.sum(each_chunk(rows, find_resid))
+    each_chunk(rows, find_dense_grad)
+    each_chunk(rows, find_products)
 
     acc_rows, group_lanes = plan.acc_rows, 2 * LANES
     low[...] = jnp.zeros_like(low)
@@ -425,7 +475,7 @@
     terms, bit = [value], 1
     while bit < count:
         value = functools.reduce(jnp.add, terms)
-        steps = (bit, 2 * bit, 3 * bit) if 2 * bit < count else (bit,)
+        steps = (bit, 2 * bit, 3 * bit) if 1 < bit and 2 * bit < count else (bit,)
         terms = [value] + [fetch(value, axis, s, count) for s in steps]
         bit *= 4 if len(steps) == 3 else 2
     return terms
@@ -478,22 +528,23 @@
         name="bands",
     )(in_vmem(jnp.transpose(kernels, (1, 0, 2))))
     bands = in_vmem(bands)
-    strip, facing = pl.pallas_call(
+    own, to_near, to_far = pl.pallas_call(
         functools.partial(strip_kernel, plan),
         out_shape=(
             pltpu.VMEM((2 * rows, LANES), jnp.bfloat16),
             pltpu.VMEM((rows, LANES), jnp.bfloat16),
+            pltpu.VMEM((rows, LANES), jnp.bfloat16),
         ),
         in_specs=[VMEM] * ny + [pl.BlockSpec(memory_space=pl.ANY)],
-        out_specs=(VMEM,) * 2,
+        out_specs=(VMEM,) * 3,
         scratch_shapes=[pltpu.VMEM((2, rows, LANES), jnp.float32)],
         compiler_params=params(0),
         cost_estimate=cost(300),
         name="strip",
     )(*[in_vmem(p) for p in pieces], bands)
-    near = in_vmem(swap_neighbours(strip, "gx", nx, 0))
-    far = in_vmem(swap_neighbours(facing, "gx", nx, 1))
-    own = in_vmem(strip)
+    near = in_vmem(swap_neighbours(to_near, "gx", nx, 0))
+    far = in_vmem(swap_neighbours(to_far, "gx", nx, 1))
+    own = in_vmem(own)
 
     tall_rows = TOP + rows + 32
     early = plan.blocks - plan.late
@@ -524,12 +575,12 @@
             pltpu.VMEM((8, LANES), jnp.float32),
             field_type,
         ),
-        in_specs=[SMEM, SMEM] + [VMEM] * 5,
+        in_specs=[VMEM] * 7,
         out_specs=(VMEM,) * 3,
         scratch_shapes=[
             *patch_scratch,
             pltpu.VMEM((plan.late * rows, plan.depth), jnp.bfloat16),
-            pltpu.VMEM((rows + 3 * PAD, WIDE), jnp.float32),
+            *[pltpu.VMEM((rows + 3 * PAD, WIDE), jnp.float32)] * 4,
             pltpu.VMEM((plan.operand_blocks * rows, plan.wide), jnp.bfloat16),
             pltpu.VMEM((plan.operand_blocks * plan.acc_rows, 2 * LANES), jnp.float32),
             pltpu.VMEM((plan.operand_blocks * plan.acc_rows, 2 * LANES), jnp.float32),
@@ -542,7 +593,7 @@
         ),
         cost_estimate=cost(12000),
         name="late",
-    )(jnp.transpose(offsets), load_weights, own, near, far, bands, in_vmem(field))
+    )(in_vmem(jnp.transpose(offsets)), in_vmem(load_weights[None]), own, near, far, bands, in_vmem(field))
 
     terms = [in_vmem(t) for t in sum_terms(sums, "gx", nx)]
     update, loss = pl.pallas_call(

time: 36 us -> 34.2 us (0.950)
  waiting for transfers between devices: 4.43 us -> 3.34 us
  Pallas kernels: 17.8 us -> 17.1 us
    ppermute x7, waiting for transfers between devices: 4.43 us -> 3.34 us  [fetch(): return lax.ppermute(value, axis, pairs)]
    pallas_call x1, Pallas kernels: 10.4 us -> 9.66 us  [body(): pl.pallas_call(functools.partial(late_kernel, plan), out_shape=(pltpu.VME...]
  transfers between devices with their start and end apart: 9 -> 9, of which waited for: 4 -> 5; matrix products, arithmetic and copies ran while one was open for 0% -> 0% of each run, Pallas kernels for 16% -> 17%
where the time goes in v4:
time: 34.2 us; the launch traced here: 34 us
  Pallas kernels  17.1 us (50%)
  starting transfers between devices  11.9 us (35%)
  waiting for transfers between devices  3.34 us (10%)
  local copies, waits for them, and re-layouts  0.94 us (3%)
  between operations  0.72 us (2%)
    pallas_call x1, Pallas kernels, body(): pl.pallas_call(functools.partial(late_kernel, plan), out_shape=(pltpu.VME...  9.66 us
    ppermute x7, starting transfers between devices, fetch(): return lax.ppermute(value, axis, pairs)  9.32 us
    ppermute x7, waiting for transfers between devices, fetch(): return lax.ppermute(value, axis, pairs)  3.34 us
    pallas_call x1, Pallas kernels, body(): pl.pallas_call(functools.partial(early_kernel, plan), out_shape=field_typ...  3.12 us
    pallas_call x1, Pallas kernels, body(): pl.pallas_call(functools.partial(bands_kernel, plan), out_shape=pltpu.VME...  2.76 us
    ppermute x2, starting transfers between devices, swap_neighbours(): return lax.ppermute(value, axis, pairs)  2.62 us
    unnamed x6, local copies, waits for them, and re-layouts  0.94 us
    pallas_call x1, Pallas kernels, body(): pl.pallas_call(functools.partial(pack_kernel, plan), out_shape=(pltpu.VME...  0.77 us
  transfers between devices with their start and end apart: 9, of which 5 were waited for; matrix products, arithmetic and copies ran while one was open for 0% of the time, Pallas kernels for 17%

profile of v4, /device:TPU:0, one launch (start us, length us, event | category | flops | bytes accessed | tf_op | source)
XLA Modules:
  0.0 34.0 jit_solution(1273686004855378636)
XLA Ops:
  0.6 0.8 %pack.1 = (bf16[80,128]{1,0:T(8,128)(2,1)S(1)}, f32[40,128]{1,0:T(8,128)S(1)}) custom-call(f32[40,128]{1,0:T(8,128)} %mask.1, s32[40,128]{1,0:T(8,128)} %target.1), custom_call_target="tpu_custom_call" | custom-call | tf_op jit(solution)/shard_map/pack/pallas_call | solution.py:500
  1.4 5.1 %collective-permute-start.2 = (bf16[80,128]{1,0:T(8,128)(2,1)S(1)}, bf16[80,128]{1,0:T(8,128)(2,1)S(1)}, u32[]{:S(2)}, u32[]{:S(2)}) collective-permute-start(bf16[80,128]{1,0:T(8,128)(2,1)S(1)} %get-tuple-element.12.refs_0_), channel_id=1, source_target_pairs={{0,24},{8,16},{16,8},{24,0},{1,25},{9,17},{17,9},{25,1},{2,26},{10... | collective-permute-start | bytes 61448 | tf_op jit(solution)/shard_map/ppermute | solution.py:460
  6.5 0.0 collective-permute-start.1
  6.5 0.6 %collective-permute-start = (bf16[80,128]{1,0:T(8,128)(2,1)S(1)}, bf16[80,128]{1,0:T(8,128)(2,1)S(1)}, u32[]{:S(2)}, u32[]{:S(2)}) collective-permute-start(bf16[80,128]{1,0:T(8,128)(2,1)S(1)} %get-tuple-element.12.refs_0_), channel_id=1, source_target_pairs={{0,8},{8,0},{16,24},{24,16},{1,9},{9,1},{17,25},{25,17},{2,10},{10... | collective-permute-start | bytes 61448 | tf_op jit(solution)/shard_map/ppermute | solution.py:460
  7.2 0.0 copy-start
  7.2 0.9 %copy-done = bf16[24,35,35]{2,0,1:T(8,128)(2,1)S(1)} copy-done((bf16[24,35,35]{2,0,1:T(8,128)(2,1)S(1)}, bf16[24,35,35]{2,0,1:T(8,128)(2,1)}, u32[]{:S(2)}) %copy-start) | copy-done | bytes 58824
  8.1 2.8 %bands.1.refs_4_ = bf16[768,2304]{1,0:T(8,128)(2,1)S(1)} custom-call(bf16[35,24,35]{2,1,0:T(8,128)(2,1)S(1)} %bitcast.4), custom_call_target="tpu_custom_call" | custom-call | flops 2000000000 | tf_op jit(solution)/shard_map/bands/pallas_call | solution.py:517
  10.9 0.0 collective-permute-done.2.refs_3_
  10.9 0.3 collective-permute-done.1.refs_2_
  11.2 0.0 collective-permute-done.refs_1_
  11.2 0.1 strip.1
  11.3 0.1 collective-permute-start.3
  11.4 2.5 %collective-permute-start.4 = (bf16[160,128]{1,0:T(8,128)(2,1)S(1)}, bf16[160,128]{1,0:T(8,128)(2,1)S(1)}, u32[]{:S(2)}, u32[]{:S(2)}) collective-permute-start(bf16[160,128]{1,0:T(8,128)(2,1)S(1)} %get-tuple-element.15), channel_id=1, source_target_pairs={{1,2},{2,1},{3,4},{4,3},{5,6},{6,5},{0,7},{7,0},{9,10},{10,9},{11,... | collective-permute-start | bytes 122888 | tf_op jit(solution)/shard_map/ppermute | solution.py:469
  14.0 0.0 collective-permute-done.3.near
  14.0 0.0 copy-start.1
  14.0 0.0 copy-start.2
  14.0 3.1 %early.1.field_in = f32[1120,768]{1,0:T(8,128)S(1)} custom-call(bf16[320,128]{1,0:T(8,128)(2,1)S(1)} %get-tuple-element.13.own, bf16[160,128]{1,0:T(8,128)(2,1)S(1)} %collective-permute-done.3.near, bf16[768,2304]{1,0:T(8,128)(2,1)S(1)} %bands.1.refs_4_), custom_call_target="tpu_custom_call" | custom-call | flops 3500000000 | tf_op jit(solution)/shard_map/early/pallas_call | solution.py:557
  17.1 0.0 collective-permute-done.4.far
  17.1 0.0 copy-done.1
  17.1 0.0 copy-done.2
  17.1 9.7 %late.1 = (f32[40,128]{1,0:T(8,128)S(1)}, f32[8,128]{1,0:T(8,128)S(1)}, f32[1120,768]{1,0:T(8,128)S(1)}) custom-call(s32[2,8]{1,0:T(2,128)S(1)} %bitcast.5, f32[1,8]{1,0:T(1,128)S(1)} %bitcast.6, bf16[320,128]{1,0:T(8,128)(2,1)S(1)} %get-tuple-element.13.own, bf16[160,128]{1,0:T(8,128)(2,1)S(1)} %collective-permute-done.3.near, ...), custom_call_target="tpu_custom_call", output_to_operand_aliasing={{2}: (6, {})} | custom-call | flops 12000000000 | tf_op jit(solution)/shard_map/late/pallas_call | solution.py:571
  26.8 0.1 collective-permute-start.5
  26.9 1.2 %collective-permute-done.5 = f32[8,128]{1,0:T(8,128)S(1)} collective-permute-done((f32[8,128]{1,0:T(8,128)S(1)}, f32[8,128]{1,0:T(8,128)S(1)}, u32[]{:S(2)}, u32[]{:S(2)}) %collective-permute-start.5) | collective-permute-done | bytes 4128 | tf_op jit(solution)/shard_map/ppermute | solution.py:460
  28.0 1.2 %collective-permute-start.8 = (f32[8,128]{1,0:T(8,128)S(1)}, f32[8,128]{1,0:T(8,128)S(1)}, u32[]{:S(2)}, u32[]{:S(2)}) collective-permute-start(f32[8,128]{1,0:T(8,128)S(1)} %add.3.refs_0_), channel_id=1, source_target_pairs={{0,6},{1,7},{2,4},{3,5},{4,2},{5,3},{6,0},{7,1},{8,14},{9,15},{10,... | collective-permute-start | bytes 12296 | tf_op jit(solution)/shard_map/ppermute | solution.py:460
  29.2 0.5 %collective-permute-start.7 = (f32[8,128]{1,0:T(8,128)S(1)}, f32[8,128]{1,0:T(8,128)S(1)}, u32[]{:S(2)}, u32[]{:S(2)}) collective-permute-start(f32[8,128]{1,0:T(8,128)S(1)} %add.3.refs_0_), channel_id=1, source_target_pairs={{0,4},{1,5},{2,6},{3,7},{4,0},{5,1},{6,2},{7,3},{8,12},{9,13},{10,... | collective-permute-start | bytes 12296 | tf_op jit(solution)/shard_map/ppermute | solution.py:460
  29.7 1.8 %collective-permute-start.6 = (f32[8,128]{1,0:T(8,128)S(1)}, f32[8,128]{1,0:T(8,128)S(1)}, u32[]{:S(2)}, u32[]{:S(2)}) collective-permute-start(f32[8,128]{1,0:T(8,128)S(1)} %add.3.refs_0_), channel_id=1, source_target_pairs={{0,2},{1,3},{2,0},{3,1},{4,6},{5,7},{6,4},{7,5},{8,10},{9,11},{10,... | collective-permute-start | bytes 12296 | tf_op jit(solution)/shard_map/ppermute | solution.py:460
  31.5 1.0 %collective-permute-done.8.refs_3_ = f32[8,128]{1,0:T(8,128)S(1)} collective-permute-done((f32[8,128]{1,0:T(8,128)S(1)}, f32[8,128]{1,0:T(8,128)S(1)}, u32[]{:S(2)}, u32[]{:S(2)}) %collective-permute-start.8) | collective-permute-done | bytes 4128 | tf_op jit(solution)/shard_map/ppermute | solution.py:460
  32.5 0.3 collective-permute-done.7.refs_2_
  32.8 0.5 %collective-permute-done.6.refs_1_ = f32[8,128]{1,0:T(8,128)S(1)} collective-permute-done((f32[8,128]{1,0:T(8,128)S(1)}, f32[8,128]{1,0:T(8,128)S(1)}, u32[]{:S(2)}, u32[]{:S(2)}) %collective-permute-start.6) | collective-permute-done | bytes 4128 | tf_op jit(solution)/shard_map/ppermute | solution.py:460
  33.4 0.6 %update.1 = (f32[40,128]{1,0:T(8,128)}, f32[1,1]{1,0:T(1,128)}) custom-call(f32[40,128]{1,0:T(8,128)S(1)} %get-tuple-element.11.mask, f32[40,128]{1,0:T(8,128)S(1)} %get-tuple-element.16.grad, f32[8,128]{1,0:T(8,128)S(1)} %add.3.refs_0_, f32[8,128]{1,0:T(8,128)S(1)} %collective-permute-done.6.refs_1_, f32[8,128]{1,0:T(8,128)S(1)} %collective-permute-done.7.refs_2_, ...), custom_call_target="tpu_custom_call" | custom-call | tf_op jit(solution)/shard_map/update/pallas_call | solution.py:599
  (1 shorter events, 0.0 us)
Async XLA Ops:
  1.4 9.5 %collective-permute-start.2 = (bf16[80,128]{1,0:T(8,128)(2,1)S(1)}, bf16[80,128]{1,0:T(8,128)(2,1)S(1)}, u32[]{:S(2)}, u32[]{:S(2)}) collective-permute-start(bf16[80,128]{1,0:T(8,128)(2,1)S(1)} %get-tuple-element.12.refs_0_), channel_id=1, source_target_pairs={{0,24},{8,16},{16,8},{24,0},{1,25},{9,17},{17,9},{25,1},{2,26},{10... | collective-permute-start | bytes 61448 | tf_op jit(solution)/shard_map/ppermute | solution.py:460
  6.5 4.7 %collective-permute-start.1 = (bf16[80,128]{1,0:T(8,128)(2,1)S(1)}, bf16[80,128]{1,0:T(8,128)(2,1)S(1)}, u32[]{:S(2)}, u32[]{:S(2)}) collective-permute-start(bf16[80,128]{1,0:T(8,128)(2,1)S(1)} %get-tuple-element.12.refs_0_), channel_id=1, source_target_pairs={{0,16},{8,24},{16,0},{24,8},{1,17},{9,25},{17,1},{25,9},{2,18},{10... | collective-permute-start | bytes 61448 | tf_op jit(solution)/shard_map/ppermute | solution.py:460
  6.5 4.7 %collective-permute-start = (bf16[80,128]{1,0:T(8,128)(2,1)S(1)}, bf16[80,128]{1,0:T(8,128)(2,1)S(1)}, u32[]{:S(2)}, u32[]{:S(2)}) collective-permute-start(bf16[80,128]{1,0:T(8,128)(2,1)S(1)} %get-tuple-element.12.refs_0_), channel_id=1, source_target_pairs={{0,8},{8,0},{16,24},{24,16},{1,9},{9,1},{17,25},{25,17},{2,10},{10... | collective-permute-start | bytes 61448 | tf_op jit(solution)/shard_map/ppermute | solution.py:460
  7.2 0.9 %copy-start = (bf16[24,35,35]{2,0,1:T(8,128)(2,1)S(1)}, bf16[24,35,35]{2,0,1:T(8,128)(2,1)}, u32[]{:S(2)}) copy-start(bf16[24,35,35]{2,0,1:T(8,128)(2,1)} %param.7) | copy-start | bytes 176404
  11.3 2.6 %collective-permute-start.3 = (bf16[160,128]{1,0:T(8,128)(2,1)S(1)}, bf16[160,128]{1,0:T(8,128)(2,1)S(1)}, u32[]{:S(2)}, u32[]{:S(2)}) collective-permute-start(bf16[160,128]{1,0:T(8,128)(2,1)S(1)} %get-tuple-element.14), channel_id=1, source_target_pairs={{0,1},{1,0},{2,3},{3,2},{4,5},{5,4},{6,7},{7,6},{8,9},{9,8},{10,11... | collective-permute-start | bytes 122888 | tf_op jit(solution)/shard_map/ppermute | solution.py:469
  11.4 5.7 %collective-permute-start.4 = (bf16[160,128]{1,0:T(8,128)(2,1)S(1)}, bf16[160,128]{1,0:T(8,128)(2,1)S(1)}, u32[]{:S(2)}, u32[]{:S(2)}) collective-permute-start(bf16[160,128]{1,0:T(8,128)(2,1)S(1)} %get-tuple-element.15), channel_id=1, source_target_pairs={{1,2},{2,1},{3,4},{4,3},{5,6},{6,5},{0,7},{7,0},{9,10},{10,9},{11,... | collective-permute-start | bytes 122888 | tf_op jit(solution)/shard_map/ppermute | solution.py:469
  14.0 3.1 %copy-start.1 = (s32[8,2]{0,1:T(2,128)S(1)}, s32[8,2]{0,1:T(2,128)}, u32[]{:S(2)}) copy-start(s32[8,2]{0,1:T(2,128)} %param.8) | copy-start | bytes 196
  14.0 3.1 %copy-start.2 = (f32[8]{0:T(128)S(1)}, f32[8]{0:T(128)}, u32[]{:S(2)}) copy-start(f32[8]{0:T(128)} %param.9) | copy-start | bytes 100
  26.8 1.2 %collective-permute-start.5 = (f32[8,128]{1,0:T(8,128)S(1)}, f32[8,128]{1,0:T(8,128)S(1)}, u32[]{:S(2)}, u32[]{:S(2)}) collective-permute-start(f32[8,128]{1,0:T(8,128)S(1)} %get-tuple-element.17), channel_id=1, source_target_pairs={{0,1},{1,0},{2,3},{3,2},{4,5},{5,4},{6,7},{7,6},{8,9},{9,8},{10,11... | collective-permute-start | bytes 12296 | tf_op jit(solution)/shard_map/ppermute | solution.py:460
  28.0 4.5 %collective-permute-start.8 = (f32[8,128]{1,0:T(8,128)S(1)}, f32[8,128]{1,0:T(8,128)S(1)}, u32[]{:S(2)}, u32[]{:S(2)}) collective-permute-start(f32[8,128]{1,0:T(8,128)S(1)} %add.3.refs_0_), channel_id=1, source_target_pairs={{0,6},{1,7},{2,4},{3,5},{4,2},{5,3},{6,0},{7,1},{8,14},{9,15},{10,... | collective-permute-start | bytes 12296 | tf_op jit(solution)/shard_map/ppermute | solution.py:460
  29.2 3.6 %collective-permute-start.7 = (f32[8,128]{1,0:T(8,128)S(1)}, f32[8,128]{1,0:T(8,128)S(1)}, u32[]{:S(2)}, u32[]{:S(2)}) collective-permute-start(f32[8,128]{1,0:T(8,128)S(1)} %add.3.refs_0_), channel_id=1, source_target_pairs={{0,4},{1,5},{2,6},{3,7},{4,0},{5,1},{6,2},{7,3},{8,12},{9,13},{10,... | collective-permute-start | bytes 12296 | tf_op jit(solution)/shard_map/ppermute | solution.py:460
  29.7 3.6 %collective-permute-start.6 = (f32[8,128]{1,0:T(8,128)S(1)}, f32[8,128]{1,0:T(8,128)S(1)}, u32[]{:S(2)}, u32[]{:S(2)}) collective-permute-start(f32[8,128]{1,0:T(8,128)S(1)} %add.3.refs_0_), channel_id=1, source_target_pairs={{0,2},{1,3},{2,0},{3,1},{4,6},{5,7},{6,4},{7,5},{8,10},{9,11},{10,... | collective-permute-start | bytes 12296 | tf_op jit(solution)/shard_map/ppermute | solution.py:460

commit v5 on v4

--- a/solution.py
+++ b/solution.py
@@ -61,6 +61,7 @@
         if self.merged:
             pieces[-1][1] = 0
         self.pieces = pieces
+        self.operand_half = (max(p[1] for p in pieces) + 1) // 2
         self.operand_blocks = max(p[1] for p in pieces) + 1
         low = sum(b * self.step < self.halo for b in range(self.blocks))
         end = self.halo + tile_cols
@@ -168,7 +169,7 @@
 
 def each_chunk(rows, work):
     count = rows // CHUNK
-    if count <= 8:
+    if count <= 24:
         results = [work(i * CHUNK) for i in range(count)]
         return None if results[0] is None else functools.reduce(jnp.add, results)
     zero = jax.eval_shape(lambda: work(0))
@@ -238,15 +239,48 @@
             ]
 
 
-def early_kernel(plan, own, near, bands, field, extended, turned, pairs_ref, patches):
-    rows, late, blocks = plan.rows, plan.late, plan.blocks
+def find_field(plan, slot, count, patches, bands, field, power, meanwhile=()):
+    rows = plan.rows
+    first = slot * rows
+
+    def add_squares(lanes, is_last):
+        def add(start):
+            held = pl.ds(first + start, CHUNK)
+            total = None if lanes.start == 0 else power[held, :]
+            for low in range(lanes.start, lanes.stop, LANES):
+                piece = field[held, low : low + LANES]
+                total = piece * piece if total is None else total + piece * piece
+            if is_last:
+                total = total + roll_lanes(total, 2 * SLOT)
+                total = total + roll_lanes(total, SLOT)
+            power[held, :] = total
+
+        each_chunk(count * rows, add)
+
+    last = None
+    for low in range(0, plan.wide, 2 * LANES):
+        lanes = slice(low, min(low + 2 * LANES, plan.wide))
+        field[first : first + count * rows, lanes] = lax.dot_general(
+            patches[...], bands[lanes, :], NT, preferred_element_type=jnp.float32
+        )
+        if last is not None:
+            add_squares(last, False)
+        if low == 2 * LANES:
+            for work in meanwhile:
+                work()
+        last = lanes
+    add_squares(last, True)
+
+
+def early_kernel(
+    plan, own, near, bands, field, power, extended, turned, pairs_ref, patches
+):
+    late, blocks = plan.late, plan.blocks
     fill_extended(plan, own, near, None, extended)
     first = jnp.where(lax.axis_index("gx") % 2 == 0, late, 0)
     for index in range(blocks - late):
         fill_patches(plan, first + index, index, extended, turned, pairs_ref, patches)
-    field[late * rows : blocks * rows, :] = lax.dot_general(
-        patches[...], bands[...], NT, preferred_element_type=jnp.float32
-    )
+    find_field(plan, late, blocks - late, patches, bands, field, power)
 
 
 def late_kernel(
@@ -258,9 +292,11 @@
     far,
     bands,
     field_in,
+    power_in,
     grad_out,
     sums_out,
     field,
+    power,
     extended,
     turned,
     pairs_ref,
@@ -269,12 +305,15 @@
     develop,
     resid,
     dense_grad,
+    inten_grad,
+    target,
     products,
+    products_two,
     low,
     high,
     tall,
 ):
-    del field_in
+    del field_in, power_in
     downs, rights = (entries(offsets[axis : axis + 1, :]) for axis in range(2))
     load_gains = entries(load_weights[...] * (LOADING_GAIN / LOAD_TAPS))
     rows, tile_cols, step = plan.rows, plan.tile_cols, plan.step
@@ -286,39 +325,41 @@
     first = jnp.where(is_even, 0, blocks - late)
     for index in range(late):
         fill_patches(plan, first + index, index, extended, turned, pairs_ref, patches)
-    field[0 : late * rows, :] = lax.dot_general(
-        patches[...], bands[...], NT, preferred_element_type=jnp.float32
-    )
-
-    def field_piece(block, t, start):
+
+    def find_target(start):
+        joined = join_columns(plan, own, near, far, 1, start)
+        target[pl.ds(start, CHUNK), :] = roll_lanes(joined, -plan.radius)
+
+    def clear():
+        low[...] = jnp.zeros_like(low)
+        high[...] = jnp.zeros_like(high)
+        for image in (intensity, develop, resid, dense_grad):
+            image[0:PAD, :] = jnp.zeros((PAD, WIDE), jnp.float32)
+            image[PAD + rows : 3 * PAD + rows, :] = jnp.zeros((2 * PAD, WIDE), jnp.float32)
+
+    meanwhile = (lambda: each_chunk(rows, find_target), clear)
+    find_field(plan, 0, late, patches, bands, field, power, meanwhile)
+
+    def slot_row(block, start):
         slot = jnp.where(is_even, block, (block + late) % blocks)
-        first = pl.multiple_of(slot * rows + start, 8)
-        return field[pl.ds(first, CHUNK), t * LANES : (t + 1) * LANES]
+        return pl.multiple_of(slot * rows + start, 8)
 
     lane = lane_index(CHUNK, WIDE)
     near_lane = lane_index(CHUNK, LANES)
     col = lane + (first_col - plan.field_halo)
     inside = (col >= 0) & (col < plan.cols)
     kernels_count = plan.channels // 2
-    for image in (intensity, develop, resid, dense_grad):
-        image[0:PAD, :] = jnp.zeros((PAD, WIDE), jnp.float32)
-        image[PAD + rows : 3 * PAD + rows, :] = jnp.zeros((2 * PAD, WIDE), jnp.float32)
 
     def find_intensity(start):
         halves = [jnp.zeros((CHUNK, LANES), jnp.float32)] * (WIDE // LANES)
         for block in range(blocks):
-            power = None
-            for t in range(plan.wide // LANES):
-                piece = field_piece(block, t, start)
-                power = piece * piece if power is None else power + piece * piece
-            power = power + roll_lanes(power, 2 * SLOT)
-            power = power + roll_lanes(power, SLOT)
-            power = roll_lanes(power, block * step)
+            total = power[pl.ds(slot_row(block, start), CHUNK), :]
+            total = roll_lanes(total, block * step)
             for half in range(WIDE // LANES):
                 low_lane = block * step - half * LANES
                 if -step < low_lane < LANES:
                     here_too = (near_lane >= low_lane) & (near_lane < low_lane + step)
-                    halves[half] = jnp.where(here_too, power, halves[half])
+                    halves[half] = jnp.where(here_too, total, halves[half])
         total = jnp.concatenate(halves, axis=1) / kernels_count
         intensity[pl.ds(PAD + start, CHUNK), :] = jnp.where(inside, total, 0.0)
 
@@ -331,12 +372,11 @@
         printed = develop[pl.ds(PAD + start, CHUNK), :]
         for down, right, gain in zip(downs, rights, load_gains):
             printed = printed - gain * shifted_chunk(develop, start, down, right)
-        target = roll_lanes(join_columns(plan, own, near, far, 1, start), -plan.radius)
         row = lax.broadcasted_iota(jnp.int32, (CHUNK, WIDE), 0) + start
         weight = (1.0 + 2.0 * row.astype(jnp.float32) / rows) * (
             1.0 + 2.0 * col.astype(jnp.float32) / plan.cols
         )
-        diff = printed - target
+        diff = printed - target[pl.ds(start, CHUNK), :]
         weighted = weight * diff
         resid[pl.ds(PAD + start, CHUNK), :] = jnp.where(inside, 2.0 * weighted, 0.0)
         mine = (lane >= plan.field_halo) & (lane < plan.field_halo + tile_cols)
@@ -353,85 +393,92 @@
     used = inside & (lane >= plan.lo) & (lane < plan.hi)
     narrow = near_lane < step
 
-    def find_products(start):
-        inten_grad = smooth_chunk(dense_grad, start) * (2.0 / kernels_count)
-        inten_grad = jnp.where(used, inten_grad, 0.0)
-        halves = [inten_grad[:, h * LANES : (h + 1) * LANES] for h in range(WIDE // LANES)]
-        gains = {}
-        for block in range(plan.pieces[0][0], plan.pieces[-1][0] + 1):
-            half, begin = divmod(block * step, LANES)
-            part = halves[half]
-            if begin + step > LANES:
-                part = jnp.where(near_lane >= begin, part, halves[half + 1])
-            part = jnp.where(narrow, roll_lanes(part, -begin), 0.0)
-            part = part + roll_lanes(part, SLOT)
-            gains[block] = part + roll_lanes(part, 2 * SLOT)
-        for operand in range(plan.operand_blocks):
-            sources = [p[0] for p in plan.pieces if p[1] == operand]
+    def find_inten_grad(start):
+        value = smooth_chunk(dense_grad, start) * (2.0 / kernels_count)
+        inten_grad[pl.ds(start, CHUNK), :] = jnp.where(used, value, 0.0)
+
+    def find_products(operands, ref, start):
+        wide = inten_grad[pl.ds(start, CHUNK), :]
+        halves = [wide[:, h * LANES : (h + 1) * LANES] for h in range(WIDE // LANES)]
+        for index, operand in enumerate(operands):
+            sources = []
+            for block in (p[0] for p in plan.pieces if p[1] == operand):
+                half, begin = divmod(block * step, LANES)
+                part = halves[half]
+                if begin + step > LANES:
+                    part = jnp.where(near_lane >= begin, part, halves[half + 1])
+                part = jnp.where(narrow, roll_lanes(part, -begin), 0.0)
+                part = part + roll_lanes(part, SLOT)
+                sources.append((slot_row(block, start), part + roll_lanes(part, 2 * SLOT)))
             for t in range(plan.wide // LANES):
-                value = None
-                for block in sources:
-                    piece = field_piece(block, t, start) * gains[block]
-                    value = piece if value is None else value + piece
-                products[
-                    pl.ds(operand * rows + start, CHUNK), t * LANES : (t + 1) * LANES
-                ] = value.astype(jnp.bfloat16)
+                lanes = slice(t * LANES, (t + 1) * LANES)
+                terms = [field[pl.ds(first, CHUNK), lanes] * gain for first, gain in sources]
+                ref[pl.ds(index * rows + start, CHUNK), lanes] = functools.reduce(
+                    jnp.add, terms
+                ).astype(jnp.bfloat16)
+
+    acc_rows, group_lanes = plan.acc_rows, 2 * LANES
+    groups = plan.pairs // 2
+
+    def add_group(operands, ref, group):
+        out = lax.dot_general(
+            ref[...],
+            bands[:, group * group_lanes : (group + 1) * group_lanes],
+            NN,
+            preferred_element_type=jnp.float32,
+        )
+        held = high if group % 2 else low
+        for index, operand in enumerate(operands):
+            first = operand * acc_rows + group // 2 * 8
+            held[first : first + rows, :] += out[index * rows : (index + 1) * rows, :]
 
     each_chunk(rows, find_intensity)
     each_chunk(rows, find_develop)
     loss = jnp.sum(each_chunk(rows, find_resid))
     each_chunk(rows, find_dense_grad)
-    each_chunk(rows, find_products)
-
-    acc_rows, group_lanes = plan.acc_rows, 2 * LANES
-    low[...] = jnp.zeros_like(low)
-    high[...] = jnp.zeros_like(high)
-
-    def add_groups(index, count):
-        lanes = pl.ds(pl.multiple_of(index * 2 * group_lanes, LANES), count * group_lanes)
-        out = lax.dot_general(
-            products[...], bands[:, lanes], NN, preferred_element_type=jnp.float32
-        )
-        for operand in range(plan.operand_blocks):
-            held = pl.ds(pl.multiple_of(operand * acc_rows + index * 8, 8), rows)
-            block = slice(operand * rows, (operand + 1) * rows)
-            low[held, :] += out[block, :group_lanes]
-            if count == 2:
-                high[held, :] += out[block, group_lanes:]
-
-    def both_groups(index, carry):
-        add_groups(index, 2)
-        return carry
-
-    groups = plan.pairs // 2
-    lax.fori_loop(0, groups // 2, both_groups, 0)
-    if groups % 2:
-        add_groups(groups // 2, 1)
+    each_chunk(rows, find_inten_grad)
+    halves_of = [range(plan.operand_half), range(plan.operand_half, plan.operand_blocks)]
+    each_chunk(rows, functools.partial(find_products, halves_of[0], products))
+    chunks = rows // CHUNK
+    if chunks > groups:
+        each_chunk(rows, functools.partial(find_products, halves_of[1], products_two))
+    for group in range(groups):
+        add_group(halves_of[0], products, group)
+        if group < chunks <= groups:
+            find_products(halves_of[1], products_two, group * CHUNK)
 
     start_row = plan.radius - 1
-    count = -(-(rows + 1) // 8) * 8
-    lane = lane_index(count, LANES)
-    total = [None, None]
-    for operand in range(plan.operand_blocks):
+    count = tall.shape[1]
+    gather_lane = lane_index(count, LANES)
+
+    def gather(operand):
         base = operand * acc_rows + start_row
         pair = None
         for out, tap in ((low, 0), (low, 2), (high, 4), (high, 6)):
             lanes = slice(LANES, 2 * LANES) if tap % 4 else slice(0, LANES)
             piece = out[base - tap : base - tap + count, lanes]
             pair = piece if pair is None else pair + piece
-        for _, index, shift, lowest, highest in plan.pieces:
-            if index != operand:
-                continue
-            keep = (lane >= lowest + shift) & (lane < highest + shift)
-            for a in range(2):
+        for a in range(2):
+            total = None if operand == 0 else tall[a]
+            for _, index, shift, lowest, highest in plan.pieces:
+                if index != operand:
+                    continue
+                keep = (gather_lane >= lowest + shift) & (gather_lane < highest + shift)
                 piece = jnp.where(keep, roll_lanes(pair, shift - a * WINDOW), 0.0)
-                total[a] = piece if total[a] is None else total[a] + piece
-    tall[...] = total[0]
-    gradient = tall[1 : 1 + rows, :] + total[1][:rows]
+                total = piece if total is None else total + piece
+            tall[a] = total
+
+    for group in range(groups):
+        add_group(halves_of[1], products_two, group)
+        if group < len(halves_of[0]):
+            gather(halves_of[0][group])
+    for operand in [*halves_of[0][groups:], *halves_of[1]]:
+        gather(operand)
+    gradient = tall[0, 1 : 1 + rows, :] + tall[1, 0:rows, :]
     square = jnp.sum(gradient * gradient)
-    tall[0:rows, :] = gradient
+    tall[0, 0:rows, :] = gradient
     start = pl.multiple_of(lax.axis_index("gy") * plan.tile_rows, 8)
-    grad_out[...] = tall[pl.ds(start, plan.tile_rows), :]
+    grad_out[...] = tall[0, pl.ds(start, plan.tile_rows), :]
     sums_out[0:4, :] = jnp.broadcast_to(loss, (4, LANES))
     sums_out[4:8, :] = jnp.broadcast_to(square, (4, LANES))
 
@@ -554,11 +601,12 @@
         pltpu.VMEM((tall_rows, LANES), jnp.float32),
     ]
     field_type = pltpu.VMEM((plan.blocks * rows, plan.wide), jnp.float32)
-    field = pl.pallas_call(
+    power_type = pltpu.VMEM((plan.blocks * rows, LANES), jnp.float32)
+    field, power = pl.pallas_call(
         functools.partial(early_kernel, plan),
-        out_shape=field_type,
+        out_shape=(field_type, power_type),
         in_specs=[VMEM] * 3,
-        out_specs=VMEM,
+        out_specs=(VMEM,) * 2,
         scratch_shapes=[
             *patch_scratch,
             pltpu.VMEM((early * rows, plan.depth), jnp.bfloat16),
@@ -568,32 +616,35 @@
         name="early",
     )(own, near, bands)
 
-    grad, sums, _ = pl.pallas_call(
+    grad, sums, _, _ = pl.pallas_call(
         functools.partial(late_kernel, plan),
         out_shape=(
             pltpu.VMEM((tile_rows, LANES), jnp.float32),
             pltpu.VMEM((8, LANES), jnp.float32),
             field_type,
+            power_type,
         ),
-        in_specs=[VMEM] * 7,
-        out_specs=(VMEM,) * 3,
+        in_specs=[VMEM] * 8,
+        out_specs=(VMEM,) * 4,
         scratch_shapes=[
             *patch_scratch,
             pltpu.VMEM((plan.late * rows, plan.depth), jnp.bfloat16),
             *[pltpu.VMEM((rows + 3 * PAD, WIDE), jnp.float32)] * 4,
-            pltpu.VMEM((plan.operand_blocks * rows, plan.wide), jnp.bfloat16),
+            *[pltpu.VMEM((rows, WIDE), jnp.float32)] * 2,
+            pltpu.VMEM((plan.operand_half * rows, plan.wide), jnp.bfloat16),
+            pltpu.VMEM(((plan.operand_blocks - plan.operand_half) * rows, plan.wide), jnp.bfloat16),
             pltpu.VMEM((plan.operand_blocks * plan.acc_rows, 2 * LANES), jnp.float32),
             pltpu.VMEM((plan.operand_blocks * plan.acc_rows, 2 * LANES), jnp.float32),
-            pltpu.VMEM((-(-(rows + 1) // 8) * 8, LANES), jnp.float32),
+            pltpu.VMEM((2, -(-(rows + 1) // 8) * 8, LANES), jnp.float32),
         ],
-        input_output_aliases={6: 2},
+        input_output_aliases={6: 2, 7: 3},
         compiler_params=params(
             plan.late * rows * plan.depth * 2
             + plan.operand_blocks * (rows * plan.wide * 2 + plan.acc_rows * 16 * LANES)
         ),
         cost_estimate=cost(12000),
         name="late",
-    )(in_vmem(jnp.transpose(offsets)), in_vmem(load_weights[None]), own, near, far, bands, in_vmem(field))
+    )(in_vmem(jnp.transpose(offsets)), in_vmem(load_weights[None]), own, near, far, bands, in_vmem(field), in_vmem(power))
 
     terms = [in_vmem(t) for t in sum_terms(sums, "gx", nx)]
     update, loss = pl.pallas_call(

time: 34.2 us -> 33.7 us (0.985)
  Pallas kernels: 17.1 us -> 16.6 us
    pallas_call x1, Pallas kernels: 9.66 us -> 9.06 us  [body(): pl.pallas_call(functools.partial(late_kernel, plan), out_shape=(pltpu.VME...]
  transfers between devices with their start and end apart: 9 -> 9, of which waited for: 5 -> 5; matrix products, arithmetic and copies ran while one was open for 0% -> 0% of each run, Pallas kernels for 17% -> 18%
where the time goes in v5:
time: 33.7 us; the launch traced here: 33.5 us
  Pallas kernels  16.6 us (49%)
  starting transfers between devices  11.9 us (35%)
  waiting for transfers between devices  3.33 us (10%)
  local copies, waits for them, and re-layouts  0.94 us (3%)
  between operations  0.72 us (2%)
    ppermute x7, starting transfers between devices, fetch(): return lax.ppermute(value, axis, pairs)  9.32 us
    pallas_call x1, Pallas kernels, body(): pl.pallas_call(functools.partial(late_kernel, plan), out_shape=(pltpu.VME...  9.06 us
    ppermute x7, waiting for transfers between devices, fetch(): return lax.ppermute(value, axis, pairs)  3.33 us
    pallas_call x1, Pallas kernels, body(): pl.pallas_call(functools.partial(early_kernel, plan), out_shape=(field_ty...  3.27 us
    pallas_call x1, Pallas kernels, body(): pl.pallas_call(functools.partial(bands_kernel, plan), out_shape=pltpu.VME...  2.76 us
    ppermute x2, starting transfers between devices, swap_neighbours(): return lax.ppermute(value, axis, pairs)  2.62 us
    unnamed x6, local copies, waits for them, and re-layouts  0.94 us
    pallas_call x1, Pallas kernels, body(): pl.pallas_call(functools.partial(pack_kernel, plan), out_shape=(pltpu.VME...  0.77 us
  transfers between devices with their start and end apart: 9, of which 5 were waited for; matrix products, arithmetic and copies ran while one was open for 0% of the time, Pallas kernels for 18%

profile of v5, /device:TPU:0, one launch (start us, length us, event | category | flops | bytes accessed | tf_op | source)
XLA Modules:
  0.0 33.5 jit_solution(11837078542364265013)
XLA Ops:
  0.6 0.8 %pack.1 = (bf16[80,128]{1,0:T(8,128)(2,1)S(1)}, f32[40,128]{1,0:T(8,128)S(1)}) custom-call(f32[40,128]{1,0:T(8,128)} %mask.1, s32[40,128]{1,0:T(8,128)} %target.1), custom_call_target="tpu_custom_call" | custom-call | tf_op jit(solution)/shard_map/pack/pallas_call | solution.py:547
  1.4 5.1 %collective-permute-start.2 = (bf16[80,128]{1,0:T(8,128)(2,1)S(1)}, bf16[80,128]{1,0:T(8,128)(2,1)S(1)}, u32[]{:S(2)}, u32[]{:S(2)}) collective-permute-start(bf16[80,128]{1,0:T(8,128)(2,1)S(1)} %get-tuple-element.14.refs_0_), channel_id=1, source_target_pairs={{0,24},{8,16},{16,8},{24,0},{1,25},{9,17},{17,9},{25,1},{2,26},{10... | collective-permute-start | bytes 61448 | tf_op jit(solution)/shard_map/ppermute | solution.py:507
  6.5 0.0 collective-permute-start.1
  6.5 0.6 %collective-permute-start = (bf16[80,128]{1,0:T(8,128)(2,1)S(1)}, bf16[80,128]{1,0:T(8,128)(2,1)S(1)}, u32[]{:S(2)}, u32[]{:S(2)}) collective-permute-start(bf16[80,128]{1,0:T(8,128)(2,1)S(1)} %get-tuple-element.14.refs_0_), channel_id=1, source_target_pairs={{0,8},{8,0},{16,24},{24,16},{1,9},{9,1},{17,25},{25,17},{2,10},{10... | collective-permute-start | bytes 61448 | tf_op jit(solution)/shard_map/ppermute | solution.py:507
  7.2 0.0 copy-start
  7.2 0.9 %copy-done = bf16[24,35,35]{2,0,1:T(8,128)(2,1)S(1)} copy-done((bf16[24,35,35]{2,0,1:T(8,128)(2,1)S(1)}, bf16[24,35,35]{2,0,1:T(8,128)(2,1)}, u32[]{:S(2)}) %copy-start) | copy-done | bytes 58824
  8.1 2.8 %bands.1.refs_4_ = bf16[768,2304]{1,0:T(8,128)(2,1)S(1)} custom-call(bf16[35,24,35]{2,1,0:T(8,128)(2,1)S(1)} %bitcast.4), custom_call_target="tpu_custom_call" | custom-call | flops 2000000000 | tf_op jit(solution)/shard_map/bands/pallas_call | solution.py:564
  10.9 0.0 collective-permute-done.2.refs_3_
  10.9 0.3 collective-permute-done.1.refs_2_
  11.2 0.0 collective-permute-done.refs_1_
  11.2 0.1 strip.1
  11.3 0.1 collective-permute-start.3
  11.4 2.5 %collective-permute-start.4 = (bf16[160,128]{1,0:T(8,128)(2,1)S(1)}, bf16[160,128]{1,0:T(8,128)(2,1)S(1)}, u32[]{:S(2)}, u32[]{:S(2)}) collective-permute-start(bf16[160,128]{1,0:T(8,128)(2,1)S(1)} %get-tuple-element.17), channel_id=1, source_target_pairs={{1,2},{2,1},{3,4},{4,3},{5,6},{6,5},{0,7},{7,0},{9,10},{10,9},{11,... | collective-permute-start | bytes 122888 | tf_op jit(solution)/shard_map/ppermute | solution.py:516
  14.0 0.0 collective-permute-done.3.near
  14.0 0.0 copy-start.1
  14.0 0.0 copy-start.2
  14.0 3.3 %early.1 = (f32[1120,768]{1,0:T(8,128)S(1)}, f32[1120,128]{1,0:T(8,128)S(1)}) custom-call(bf16[320,128]{1,0:T(8,128)(2,1)S(1)} %get-tuple-element.15.own, bf16[160,128]{1,0:T(8,128)(2,1)S(1)} %collective-permute-done.3.near, bf16[768,2304]{1,0:T(8,128)(2,1)S(1)} %bands.1.refs_4_), custom_call_target="tpu_custom_call" | custom-call | flops 3500000000 | tf_op jit(solution)/shard_map/early/pallas_call | solution.py:605
  17.2 0.0 collective-permute-done.4.far
  17.2 0.0 copy-done.1
  17.2 0.0 copy-done.2
  17.3 9.1 %late.1 = (f32[40,128]{1,0:T(8,128)S(1)}, f32[8,128]{1,0:T(8,128)S(1)}, f32[1120,768]{1,0:T(8,128)S(1)}, f32[1120,128]{1,0:T(8,128)S(1)}) custom-call(s32[2,8]{1,0:T(2,128)S(1)} %bitcast.5, f32[1,8]{1,0:T(1,128)S(1)} %bitcast.6, bf16[320,128]{1,0:T(8,128)(2,1)S(1)} %get-tuple-element.15.own, ...), custom_call_target="tpu_custom_call", output_to_operand_aliasing={{2}: (6, {}), {3}: (7, {})} | custom-call | flops 12000000000 | tf_op jit(solution)/shard_map/late/pallas_call | solution.py:619
  26.3 0.1 collective-permute-start.5
  26.4 1.2 %collective-permute-done.5 = f32[8,128]{1,0:T(8,128)S(1)} collective-permute-done((f32[8,128]{1,0:T(8,128)S(1)}, f32[8,128]{1,0:T(8,128)S(1)}, u32[]{:S(2)}, u32[]{:S(2)}) %collective-permute-start.5) | collective-permute-done | bytes 4128 | tf_op jit(solution)/shard_map/ppermute | solution.py:507
  27.6 1.1 %collective-permute-start.8 = (f32[8,128]{1,0:T(8,128)S(1)}, f32[8,128]{1,0:T(8,128)S(1)}, u32[]{:S(2)}, u32[]{:S(2)}) collective-permute-start(f32[8,128]{1,0:T(8,128)S(1)} %add.3.refs_0_), channel_id=1, source_target_pairs={{0,6},{1,7},{2,4},{3,5},{4,2},{5,3},{6,0},{7,1},{8,14},{9,15},{10,... | collective-permute-start | bytes 12296 | tf_op jit(solution)/shard_map/ppermute | solution.py:507
  28.7 0.6 %collective-permute-start.7 = (f32[8,128]{1,0:T(8,128)S(1)}, f32[8,128]{1,0:T(8,128)S(1)}, u32[]{:S(2)}, u32[]{:S(2)}) collective-permute-start(f32[8,128]{1,0:T(8,128)S(1)} %add.3.refs_0_), channel_id=1, source_target_pairs={{0,4},{1,5},{2,6},{3,7},{4,0},{5,1},{6,2},{7,3},{8,12},{9,13},{10,... | collective-permute-start | bytes 12296 | tf_op jit(solution)/shard_map/ppermute | solution.py:507
  29.3 1.8 %collective-permute-start.6 = (f32[8,128]{1,0:T(8,128)S(1)}, f32[8,128]{1,0:T(8,128)S(1)}, u32[]{:S(2)}, u32[]{:S(2)}) collective-permute-start(f32[8,128]{1,0:T(8,128)S(1)} %add.3.refs_0_), channel_id=1, source_target_pairs={{0,2},{1,3},{2,0},{3,1},{4,6},{5,7},{6,4},{7,5},{8,10},{9,11},{10,... | collective-permute-start | bytes 12296 | tf_op jit(solution)/shard_map/ppermute | solution.py:507
  31.1 1.0 %collective-permute-done.8.refs_3_ = f32[8,128]{1,0:T(8,128)S(1)} collective-permute-done((f32[8,128]{1,0:T(8,128)S(1)}, f32[8,128]{1,0:T(8,128)S(1)}, u32[]{:S(2)}, u32[]{:S(2)}) %collective-permute-start.8) | collective-permute-done | bytes 4128 | tf_op jit(solution)/shard_map/ppermute | solution.py:507
  32.1 0.2 collective-permute-done.7.refs_2_
  32.3 0.6 %collective-permute-done.6.refs_1_ = f32[8,128]{1,0:T(8,128)S(1)} collective-permute-done((f32[8,128]{1,0:T(8,128)S(1)}, f32[8,128]{1,0:T(8,128)S(1)}, u32[]{:S(2)}, u32[]{:S(2)}) %collective-permute-start.6) | collective-permute-done | bytes 4128 | tf_op jit(solution)/shard_map/ppermute | solution.py:507
  32.9 0.6 %update.1 = (f32[40,128]{1,0:T(8,128)}, f32[1,1]{1,0:T(1,128)}) custom-call(f32[40,128]{1,0:T(8,128)S(1)} %get-tuple-element.13.mask, f32[40,128]{1,0:T(8,128)S(1)} %get-tuple-element.20.grad, f32[8,128]{1,0:T(8,128)S(1)} %add.3.refs_0_, f32[8,128]{1,0:T(8,128)S(1)} %collective-permute-done.6.refs_1_, f32[8,128]{1,0:T(8,128)S(1)} %collective-permute-done.7.refs_2_, ...), custom_call_target="tpu_custom_call" | custom-call | tf_op jit(solution)/shard_map/update/pallas_call | solution.py:650
  (1 shorter events, 0.0 us)
Async XLA Ops:
  1.4 9.5 %collective-permute-start.2 = (bf16[80,128]{1,0:T(8,128)(2,1)S(1)}, bf16[80,128]{1,0:T(8,128)(2,1)S(1)}, u32[]{:S(2)}, u32[]{:S(2)}) collective-permute-start(bf16[80,128]{1,0:T(8,128)(2,1)S(1)} %get-tuple-element.14.refs_0_), channel_id=1, source_target_pairs={{0,24},{8,16},{16,8},{24,0},{1,25},{9,17},{17,9},{25,1},{2,26},{10... | collective-permute-start | bytes 61448 | tf_op jit(solution)/shard_map/ppermute | solution.py:507
  6.5 4.7 %collective-permute-start.1 = (bf16[80,128]{1,0:T(8,128)(2,1)S(1)}, bf16[80,128]{1,0:T(8,128)(2,1)S(1)}, u32[]{:S(2)}, u32[]{:S(2)}) collective-permute-start(bf16[80,128]{1,0:T(8,128)(2,1)S(1)} %get-tuple-element.14.refs_0_), channel_id=1, source_target_pairs={{0,16},{8,24},{16,0},{24,8},{1,17},{9,25},{17,1},{25,9},{2,18},{10... | collective-permute-start | bytes 61448 | tf_op jit(solution)/shard_map/ppermute | solution.py:507
  6.5 4.7 %collective-permute-start = (bf16[80,128]{1,0:T(8,128)(2,1)S(1)}, bf16[80,128]{1,0:T(8,128)(2,1)S(1)}, u32[]{:S(2)}, u32[]{:S(2)}) collective-permute-start(bf16[80,128]{1,0:T(8,128)(2,1)S(1)} %get-tuple-element.14.refs_0_), channel_id=1, source_target_pairs={{0,8},{8,0},{16,24},{24,16},{1,9},{9,1},{17,25},{25,17},{2,10},{10... | collective-permute-start | bytes 61448 | tf_op jit(solution)/shard_map/ppermute | solution.py:507
  7.2 0.9 %copy-start = (bf16[24,35,35]{2,0,1:T(8,128)(2,1)S(1)}, bf16[24,35,35]{2,0,1:T(8,128)(2,1)}, u32[]{:S(2)}) copy-start(bf16[24,35,35]{2,0,1:T(8,128)(2,1)} %param.7) | copy-start | bytes 176404
  11.3 2.6 %collective-permute-start.3 = (bf16[160,128]{1,0:T(8,128)(2,1)S(1)}, bf16[160,128]{1,0:T(8,128)(2,1)S(1)}, u32[]{:S(2)}, u32[]{:S(2)}) collective-permute-start(bf16[160,128]{1,0:T(8,128)(2,1)S(1)} %get-tuple-element.16), channel_id=1, source_target_pairs={{0,1},{1,0},{2,3},{3,2},{4,5},{5,4},{6,7},{7,6},{8,9},{9,8},{10,11... | collective-permute-start | bytes 122888 | tf_op jit(solution)/shard_map/ppermute | solution.py:516
  11.4 5.8 %collective-permute-start.4 = (bf16[160,128]{1,0:T(8,128)(2,1)S(1)}, bf16[160,128]{1,0:T(8,128)(2,1)S(1)}, u32[]{:S(2)}, u32[]{:S(2)}) collective-permute-start(bf16[160,128]{1,0:T(8,128)(2,1)S(1)} %get-tuple-element.17), channel_id=1, source_target_pairs={{1,2},{2,1},{3,4},{4,3},{5,6},{6,5},{0,7},{7,0},{9,10},{10,9},{11,... | collective-permute-start | bytes 122888 | tf_op jit(solution)/shard_map/ppermute | solution.py:516
  14.0 3.3 %copy-start.1 = (s32[8,2]{0,1:T(2,128)S(1)}, s32[8,2]{0,1:T(2,128)}, u32[]{:S(2)}) copy-start(s32[8,2]{0,1:T(2,128)} %param.8) | copy-start | bytes 196
  14.0 3.3 %copy-start.2 = (f32[8]{0:T(128)S(1)}, f32[8]{0:T(128)}, u32[]{:S(2)}) copy-start(f32[8]{0:T(128)} %param.9) | copy-start | bytes 100
  26.3 1.2 %collective-permute-start.5 = (f32[8,128]{1,0:T(8,128)S(1)}, f32[8,128]{1,0:T(8,128)S(1)}, u32[]{:S(2)}, u32[]{:S(2)}) collective-permute-start(f32[8,128]{1,0:T(8,128)S(1)} %get-tuple-element.21), channel_id=1, source_target_pairs={{0,1},{1,0},{2,3},{3,2},{4,5},{5,4},{6,7},{7,6},{8,9},{9,8},{10,11... | collective-permute-start | bytes 12296 | tf_op jit(solution)/shard_map/ppermute | solution.py:507
  27.6 4.5 %collective-permute-start.8 = (f32[8,128]{1,0:T(8,128)S(1)}, f32[8,128]{1,0:T(8,128)S(1)}, u32[]{:S(2)}, u32[]{:S(2)}) collective-permute-start(f32[8,128]{1,0:T(8,128)S(1)} %add.3.refs_0_), channel_id=1, source_target_pairs={{0,6},{1,7},{2,4},{3,5},{4,2},{5,3},{6,0},{7,1},{8,14},{9,15},{10,... | collective-permute-start | bytes 12296 | tf_op jit(solution)/shard_map/ppermute | solution.py:507
  28.7 3.6 %collective-permute-start.7 = (f32[8,128]{1,0:T(8,128)S(1)}, f32[8,128]{1,0:T(8,128)S(1)}, u32[]{:S(2)}, u32[]{:S(2)}) collective-permute-start(f32[8,128]{1,0:T(8,128)S(1)} %add.3.refs_0_), channel_id=1, source_target_pairs={{0,4},{1,5},{2,6},{3,7},{4,0},{5,1},{6,2},{7,3},{8,12},{9,13},{10,... | collective-permute-start | bytes 12296 | tf_op jit(solution)/shard_map/ppermute | solution.py:507
  29.3 3.6 %collective-permute-start.6 = (f32[8,128]{1,0:T(8,128)S(1)}, f32[8,128]{1,0:T(8,128)S(1)}, u32[]{:S(2)}, u32[]{:S(2)}) collective-permute-start(f32[8,128]{1,0:T(8,128)S(1)} %add.3.refs_0_), channel_id=1, source_target_pairs={{0,2},{1,3},{2,0},{3,1},{4,6},{5,7},{6,4},{7,5},{8,10},{9,11},{10,... | collective-permute-start | bytes 12296 | tf_op jit(solution)/shard_map/ppermute | solution.py:507

commit v6 on v5

--- a/solution.py
+++ b/solution.py
@@ -114,7 +114,7 @@
     here = lax.axis_index("gy")
     tile_rows, rows = plan.tile_rows, plan.rows
     for index, piece in enumerate(pieces):
-        source = partner(here, index, plan.ny)
+        source = lax.rem(here + index, plan.ny)
         value = piece[...].astype(jnp.float32)
         start = pl.multiple_of(source * tile_rows, 8)
         hold[0, pl.ds(start, tile_rows), :] = value[:tile_rows]
@@ -151,7 +151,7 @@
             )
         return 0
 
-    lax.fori_loop(0, channels, channel, 0)
+    lax.fori_loop(0, channels, channel, 0, unroll=4)
 
 
 def smooth_chunk(ref, start):
@@ -493,12 +493,6 @@
     loss[...] = total[0:1, 0:1]
 
 
-def partner(here, step, count):
-    if count & (count - 1) == 0:
-        return jnp.bitwise_xor(here, step)
-    return lax.rem(here + step, count)
-
-
 def fetch(value, axis, step, count):
     if count & (count - 1) == 0:
         pairs = [(i, i ^ step) for i in range(count)]
@@ -559,7 +553,7 @@
         compiler_params=params(0),
         name="pack",
     )(*[pltpu.with_memory_space_constraint(v, pltpu.HBM) for v in (mask, target)])
-    pieces = [both] + [fetch(both, "gy", s, ny) for s in range(1, ny)]
+    pieces = [both] + [lax.ppermute(both, "gy", [((i + s) % ny, i) for i in range(ny)]) for s in range(1, ny)]
 
     bands = pl.pallas_call(
         functools.partial(bands_kernel, plan),

time: 33.7 us -> 33.4 us (level)
  Pallas kernels: 16.6 us -> 15.3 us
  starting transfers between devices: 11.9 us -> 13.2 us
    ppermute x0 -> x3, starting transfers between devices: none -> 7.01 us  [body(): lax.ppermute(both, 'gy', [((i + s) % ny, i) for i in range(ny)])]
    ppermute x7 -> x4, starting transfers between devices: 9.32 us -> 3.56 us  [fetch(): return lax.ppermute(value, axis, pairs)]
    pallas_call x1, Pallas kernels: 2.76 us -> 1.5 us  [body(): pl.pallas_call(functools.partial(bands_kernel, plan), out_shape=pltpu.VME...]
    ppermute x7 -> x4, waiting for transfers between devices: 3.33 us -> 3 us  [fetch(): return lax.ppermute(value, axis, pairs)]
  transfers between devices with their start and end apart: 9 -> 9, of which waited for: 5 -> 4; matrix products, arithmetic and copies ran while one was open for 0% -> 0% of each run, Pallas kernels for 18% -> 14%
where the time goes in v6:
time: 33.4 us; the launch traced here: 33.2 us
  Pallas kernels  15.3 us (46%)
  starting transfers between devices  13.2 us (40%)
  waiting for transfers between devices  3.01 us (9%)
  local copies, waits for them, and re-layouts  0.94 us (3%)
  between operations  0.74 us (2%)
    pallas_call x1, Pallas kernels, body(): pl.pallas_call(functools.partial(late_kernel, plan), out_shape=(pltpu.VME...  9.04 us
    ppermute x3, starting transfers between devices, body(): lax.ppermute(both, 'gy', [((i + s) % ny, i) for i in range(ny)])  7.01 us
    ppermute x4, starting transfers between devices, fetch(): return lax.ppermute(value, axis, pairs)  3.56 us
    pallas_call x1, Pallas kernels, body(): pl.pallas_call(functools.partial(early_kernel, plan), out_shape=(field_ty...  3.27 us
    ppermute x4, waiting for transfers between devices, fetch(): return lax.ppermute(value, axis, pairs)  3 us
    ppermute x2, starting transfers between devices, swap_neighbours(): return lax.ppermute(value, axis, pairs)  2.62 us
    pallas_call x1, Pallas kernels, body(): pl.pallas_call(functools.partial(bands_kernel, plan), out_shape=pltpu.VME...  1.5 us
    unnamed x6, local copies, waits for them, and re-layouts  0.94 us
  transfers between devices with their start and end apart: 9, of which 4 were waited for; matrix products, arithmetic and copies ran while one was open for 0% of the time, Pallas kernels for 14%

profile of v6, /device:TPU:0, one launch (start us, length us, event | category | flops | bytes accessed | tf_op | source)
XLA Modules:
  0.0 33.2 jit_solution(9489071261046391085)
XLA Ops:
  0.6 0.8 %pack.1 = (bf16[80,128]{1,0:T(8,128)(2,1)S(1)}, f32[40,128]{1,0:T(8,128)S(1)}) custom-call(f32[40,128]{1,0:T(8,128)} %mask.1, s32[40,128]{1,0:T(8,128)} %target.1), custom_call_target="tpu_custom_call" | custom-call | tf_op jit(solution)/shard_map/pack/pallas_call | solution.py:541
  1.4 3.1 %collective-permute-start.2 = (bf16[80,128]{1,0:T(8,128)(2,1)S(1)}, bf16[80,128]{1,0:T(8,128)(2,1)S(1)}, u32[]{:S(2)}, u32[]{:S(2)}) collective-permute-start(bf16[80,128]{1,0:T(8,128)(2,1)S(1)} %get-tuple-element.14.refs_0_), channel_id=1, source_target_pairs={{24,0},{0,8},{8,16},{16,24},{25,1},{1,9},{9,17},{17,25},{26,2},{2,... | collective-permute-start | bytes 61448 | tf_op jit(solution)/shard_map/ppermute | solution.py:556
  4.5 2.6 %collective-permute-start.1 = (bf16[80,128]{1,0:T(8,128)(2,1)S(1)}, bf16[80,128]{1,0:T(8,128)(2,1)S(1)}, u32[]{:S(2)}, u32[]{:S(2)}) collective-permute-start(bf16[80,128]{1,0:T(8,128)(2,1)S(1)} %get-tuple-element.14.refs_0_), channel_id=1, source_target_pairs={{16,0},{24,8},{0,16},{8,24},{17,1},{25,9},{1,17},{9,25},{18,2},{26... | collective-permute-start | bytes 61448 | tf_op jit(solution)/shard_map/ppermute | solution.py:556
  7.1 1.3 %collective-permute-start = (bf16[80,128]{1,0:T(8,128)(2,1)S(1)}, bf16[80,128]{1,0:T(8,128)(2,1)S(1)}, u32[]{:S(2)}, u32[]{:S(2)}) collective-permute-start(bf16[80,128]{1,0:T(8,128)(2,1)S(1)} %get-tuple-element.14.refs_0_), channel_id=1, source_target_pairs={{8,0},{16,8},{24,16},{0,24},{9,1},{17,9},{25,17},{1,25},{10,2},{18... | collective-permute-start | bytes 61448 | tf_op jit(solution)/shard_map/ppermute | solution.py:556
  8.4 0.0 copy-start
  8.4 0.9 %copy-done = bf16[24,35,35]{2,0,1:T(8,128)(2,1)S(1)} copy-done((bf16[24,35,35]{2,0,1:T(8,128)(2,1)S(1)}, bf16[24,35,35]{2,0,1:T(8,128)(2,1)}, u32[]{:S(2)}) %copy-start) | copy-done | bytes 58824
  9.4 1.5 %bands.1.refs_4_ = bf16[768,2304]{1,0:T(8,128)(2,1)S(1)} custom-call(bf16[35,24,35]{2,1,0:T(8,128)(2,1)S(1)} %bitcast.4), custom_call_target="tpu_custom_call" | custom-call | flops 2000000000 | tf_op jit(solution)/shard_map/bands/pallas_call | solution.py:558
  10.9 0.0 collective-permute-done.2.refs_3_
  10.9 0.0 collective-permute-done.1.refs_2_
  10.9 0.0 collective-permute-done.refs_1_
  10.9 0.1 strip.1
  11.0 0.1 collective-permute-start.3
  11.1 2.5 %collective-permute-start.4 = (bf16[160,128]{1,0:T(8,128)(2,1)S(1)}, bf16[160,128]{1,0:T(8,128)(2,1)S(1)}, u32[]{:S(2)}, u32[]{:S(2)}) collective-permute-start(bf16[160,128]{1,0:T(8,128)(2,1)S(1)} %get-tuple-element.17), channel_id=1, source_target_pairs={{1,2},{2,1},{3,4},{4,3},{5,6},{6,5},{0,7},{7,0},{9,10},{10,9},{11,... | collective-permute-start | bytes 122888 | tf_op jit(solution)/shard_map/ppermute | solution.py:510
  13.7 0.0 collective-permute-done.3.near
  13.7 0.0 copy-start.1
  13.7 0.0 copy-start.2
  13.7 3.3 %early.1 = (f32[1120,768]{1,0:T(8,128)S(1)}, f32[1120,128]{1,0:T(8,128)S(1)}) custom-call(bf16[320,128]{1,0:T(8,128)(2,1)S(1)} %get-tuple-element.15.own, bf16[160,128]{1,0:T(8,128)(2,1)S(1)} %collective-permute-done.3.near, bf16[768,2304]{1,0:T(8,128)(2,1)S(1)} %bands.1.refs_4_), custom_call_target="tpu_custom_call" | custom-call | flops 3500000000 | tf_op jit(solution)/shard_map/early/pallas_call | solution.py:599
  16.9 0.0 collective-permute-done.4.far
  16.9 0.0 copy-done.1
  17.0 0.0 copy-done.2
  17.0 9.0 %late.1 = (f32[40,128]{1,0:T(8,128)S(1)}, f32[8,128]{1,0:T(8,128)S(1)}, f32[1120,768]{1,0:T(8,128)S(1)}, f32[1120,128]{1,0:T(8,128)S(1)}) custom-call(s32[2,8]{1,0:T(2,128)S(1)} %bitcast.5, f32[1,8]{1,0:T(1,128)S(1)} %bitcast.6, bf16[320,128]{1,0:T(8,128)(2,1)S(1)} %get-tuple-element.15.own, ...), custom_call_target="tpu_custom_call", output_to_operand_aliasing={{2}: (6, {}), {3}: (7, {})} | custom-call | flops 12000000000 | tf_op jit(solution)/shard_map/late/pallas_call | solution.py:613
  26.0 0.1 collective-permute-start.5
  26.1 1.2 %collective-permute-done.5 = f32[8,128]{1,0:T(8,128)S(1)} collective-permute-done((f32[8,128]{1,0:T(8,128)S(1)}, f32[8,128]{1,0:T(8,128)S(1)}, u32[]{:S(2)}, u32[]{:S(2)}) %collective-permute-start.5) | collective-permute-done | bytes 4128 | tf_op jit(solution)/shard_map/ppermute | solution.py:501
  27.2 1.1 %collective-permute-start.8 = (f32[8,128]{1,0:T(8,128)S(1)}, f32[8,128]{1,0:T(8,128)S(1)}, u32[]{:S(2)}, u32[]{:S(2)}) collective-permute-start(f32[8,128]{1,0:T(8,128)S(1)} %add.3.refs_0_), channel_id=1, source_target_pairs={{0,6},{1,7},{2,4},{3,5},{4,2},{5,3},{6,0},{7,1},{8,14},{9,15},{10,... | collective-permute-start | bytes 12296 | tf_op jit(solution)/shard_map/ppermute | solution.py:501
  28.3 0.6 %collective-permute-start.7 = (f32[8,128]{1,0:T(8,128)S(1)}, f32[8,128]{1,0:T(8,128)S(1)}, u32[]{:S(2)}, u32[]{:S(2)}) collective-permute-start(f32[8,128]{1,0:T(8,128)S(1)} %add.3.refs_0_), channel_id=1, source_target_pairs={{0,4},{1,5},{2,6},{3,7},{4,0},{5,1},{6,2},{7,3},{8,12},{9,13},{10,... | collective-permute-start | bytes 12296 | tf_op jit(solution)/shard_map/ppermute | solution.py:501
  29.0 1.8 %collective-permute-start.6 = (f32[8,128]{1,0:T(8,128)S(1)}, f32[8,128]{1,0:T(8,128)S(1)}, u32[]{:S(2)}, u32[]{:S(2)}) collective-permute-start(f32[8,128]{1,0:T(8,128)S(1)} %add.3.refs_0_), channel_id=1, source_target_pairs={{0,2},{1,3},{2,0},{3,1},{4,6},{5,7},{6,4},{7,5},{8,10},{9,11},{10,... | collective-permute-start | bytes 12296 | tf_op jit(solution)/shard_map/ppermute | solution.py:501
  30.7 1.0 %collective-permute-done.8.refs_3_ = f32[8,128]{1,0:T(8,128)S(1)} collective-permute-done((f32[8,128]{1,0:T(8,128)S(1)}, f32[8,128]{1,0:T(8,128)S(1)}, u32[]{:S(2)}, u32[]{:S(2)}) %collective-permute-start.8) | collective-permute-done | bytes 4128 | tf_op jit(solution)/shard_map/ppermute | solution.py:501
  31.7 0.2 collective-permute-done.7.refs_2_
  31.9 0.6 %collective-permute-done.6.refs_1_ = f32[8,128]{1,0:T(8,128)S(1)} collective-permute-done((f32[8,128]{1,0:T(8,128)S(1)}, f32[8,128]{1,0:T(8,128)S(1)}, u32[]{:S(2)}, u32[]{:S(2)}) %collective-permute-start.6) | collective-permute-done | bytes 4128 | tf_op jit(solution)/shard_map/ppermute | solution.py:501
  32.6 0.6 %update.1 = (f32[40,128]{1,0:T(8,128)}, f32[1,1]{1,0:T(1,128)}) custom-call(f32[40,128]{1,0:T(8,128)S(1)} %get-tuple-element.13.mask, f32[40,128]{1,0:T(8,128)S(1)} %get-tuple-element.20.grad, f32[8,128]{1,0:T(8,128)S(1)} %add.3.refs_0_, f32[8,128]{1,0:T(8,128)S(1)} %collective-permute-done.6.refs_1_, f32[8,128]{1,0:T(8,128)S(1)} %collective-permute-done.7.refs_2_, ...), custom_call_target="tpu_custom_call" | custom-call | tf_op jit(solution)/shard_map/update/pallas_call | solution.py:644
  (1 shorter events, 0.0 us)
Async XLA Ops:
  1.4 9.5 %collective-permute-start.2 = (bf16[80,128]{1,0:T(8,128)(2,1)S(1)}, bf16[80,128]{1,0:T(8,128)(2,1)S(1)}, u32[]{:S(2)}, u32[]{:S(2)}) collective-permute-start(bf16[80,128]{1,0:T(8,128)(2,1)S(1)} %get-tuple-element.14.refs_0_), channel_id=1, source_target_pairs={{24,0},{0,8},{8,16},{16,24},{25,1},{1,9},{9,17},{17,25},{26,2},{2,... | collective-permute-start | bytes 61448 | tf_op jit(solution)/shard_map/ppermute | solution.py:556
  4.5 6.4 %collective-permute-start.1 = (bf16[80,128]{1,0:T(8,128)(2,1)S(1)}, bf16[80,128]{1,0:T(8,128)(2,1)S(1)}, u32[]{:S(2)}, u32[]{:S(2)}) collective-permute-start(bf16[80,128]{1,0:T(8,128)(2,1)S(1)} %get-tuple-element.14.refs_0_), channel_id=1, source_target_pairs={{16,0},{24,8},{0,16},{8,24},{17,1},{25,9},{1,17},{9,25},{18,2},{26... | collective-permute-start | bytes 61448 | tf_op jit(solution)/shard_map/ppermute | solution.py:556
  7.1 3.8 %collective-permute-start = (bf16[80,128]{1,0:T(8,128)(2,1)S(1)}, bf16[80,128]{1,0:T(8,128)(2,1)S(1)}, u32[]{:S(2)}, u32[]{:S(2)}) collective-permute-start(bf16[80,128]{1,0:T(8,128)(2,1)S(1)} %get-tuple-element.14.refs_0_), channel_id=1, source_target_pairs={{8,0},{16,8},{24,16},{0,24},{9,1},{17,9},{25,17},{1,25},{10,2},{18... | collective-permute-start | bytes 61448 | tf_op jit(solution)/shard_map/ppermute | solution.py:556
  8.4 0.9 %copy-start = (bf16[24,35,35]{2,0,1:T(8,128)(2,1)S(1)}, bf16[24,35,35]{2,0,1:T(8,128)(2,1)}, u32[]{:S(2)}) copy-start(bf16[24,35,35]{2,0,1:T(8,128)(2,1)} %param.7) | copy-start | bytes 176404
  11.0 2.6 %collective-permute-start.3 = (bf16[160,128]{1,0:T(8,128)(2,1)S(1)}, bf16[160,128]{1,0:T(8,128)(2,1)S(1)}, u32[]{:S(2)}, u32[]{:S(2)}) collective-permute-start(bf16[160,128]{1,0:T(8,128)(2,1)S(1)} %get-tuple-element.16), channel_id=1, source_target_pairs={{0,1},{1,0},{2,3},{3,2},{4,5},{5,4},{6,7},{7,6},{8,9},{9,8},{10,11... | collective-permute-start | bytes 122888 | tf_op jit(solution)/shard_map/ppermute | solution.py:510
  11.1 5.8 %collective-permute-start.4 = (bf16[160,128]{1,0:T(8,128)(2,1)S(1)}, bf16[160,128]{1,0:T(8,128)(2,1)S(1)}, u32[]{:S(2)}, u32[]{:S(2)}) collective-permute-start(bf16[160,128]{1,0:T(8,128)(2,1)S(1)} %get-tuple-element.17), channel_id=1, source_target_pairs={{1,2},{2,1},{3,4},{4,3},{5,6},{6,5},{0,7},{7,0},{9,10},{10,9},{11,... | collective-permute-start | bytes 122888 | tf_op jit(solution)/shard_map/ppermute | solution.py:510
  13.7 3.3 %copy-start.1 = (s32[8,2]{0,1:T(2,128)S(1)}, s32[8,2]{0,1:T(2,128)}, u32[]{:S(2)}) copy-start(s32[8,2]{0,1:T(2,128)} %param.8) | copy-start | bytes 196
  13.7 3.3 %copy-start.2 = (f32[8]{0:T(128)S(1)}, f32[8]{0:T(128)}, u32[]{:S(2)}) copy-start(f32[8]{0:T(128)} %param.9) | copy-start | bytes 100
  26.0 1.2 %collective-permute-start.5 = (f32[8,128]{1,0:T(8,128)S(1)}, f32[8,128]{1,0:T(8,128)S(1)}, u32[]{:S(2)}, u32[]{:S(2)}) collective-permute-start(f32[8,128]{1,0:T(8,128)S(1)} %get-tuple-element.21), channel_id=1, source_target_pairs={{0,1},{1,0},{2,3},{3,2},{4,5},{5,4},{6,7},{7,6},{8,9},{9,8},{10,11... | collective-permute-start | bytes 12296 | tf_op jit(solution)/shard_map/ppermute | solution.py:501
  27.2 4.5 %collective-permute-start.8 = (f32[8,128]{1,0:T(8,128)S(1)}, f32[8,128]{1,0:T(8,128)S(1)}, u32[]{:S(2)}, u32[]{:S(2)}) collective-permute-start(f32[8,128]{1,0:T(8,128)S(1)} %add.3.refs_0_), channel_id=1, source_target_pairs={{0,6},{1,7},{2,4},{3,5},{4,2},{5,3},{6,0},{7,1},{8,14},{9,15},{10,... | collective-permute-start | bytes 12296 | tf_op jit(solution)/shard_map/ppermute | solution.py:501
  28.3 3.6 %collective-permute-start.7 = (f32[8,128]{1,0:T(8,128)S(1)}, f32[8,128]{1,0:T(8,128)S(1)}, u32[]{:S(2)}, u32[]{:S(2)}) collective-permute-start(f32[8,128]{1,0:T(8,128)S(1)} %add.3.refs_0_), channel_id=1, source_target_pairs={{0,4},{1,5},{2,6},{3,7},{4,0},{5,1},{6,2},{7,3},{8,12},{9,13},{10,... | collective-permute-start | bytes 12296 | tf_op jit(solution)/shard_map/ppermute | solution.py:501
  29.0 3.6 %collective-permute-start.6 = (f32[8,128]{1,0:T(8,128)S(1)}, f32[8,128]{1,0:T(8,128)S(1)}, u32[]{:S(2)}, u32[]{:S(2)}) collective-permute-start(f32[8,128]{1,0:T(8,128)S(1)} %add.3.refs_0_), channel_id=1, source_target_pairs={{0,2},{1,3},{2,0},{3,1},{4,6},{5,7},{6,4},{7,5},{8,10},{9,11},{10,... | collective-permute-start | bytes 12296 | tf_op jit(solution)/shard_map/ppermute | solution.py:501

commit v7 on v6

--- a/solution.py
+++ b/solution.py
@@ -20,7 +20,7 @@
 SLOT = 32
 WIDE = 256
 TOP = 24
-CHUNK = 32
+CHUNK = 80
 PAD = 8
 
 NT = (((1,), (1,)), ((), ()))
@@ -517,7 +517,13 @@
     while bit < count:
         value = functools.reduce(jnp.add, terms)
         steps = (bit, 2 * bit, 3 * bit) if 1 < bit and 2 * bit < count else (bit,)
-        terms = [value] + [fetch(value, axis, s, count) for s in steps]
+        if len(steps) == 3:
+            terms = [value]
+            for s in range(1, 4):
+                pairs = [(i // (4 * bit) * 4 * bit + (i + s * bit) % (4 * bit), i) for i in range(count)]
+                terms.append(lax.ppermute(value, axis, pairs))
+        else:
+            terms = [value] + [fetch(value, axis, s, count) for s in steps]
         bit *= 4 if len(steps) == 3 else 2
     return terms
 

time: 33.4 us -> 33.3 us (level)
    ppermute x4 -> x1, starting transfers between devices: 3.56 us -> 0.07 us  [fetch(): return lax.ppermute(value, axis, pairs)]
    ppermute x0 -> x3, starting transfers between devices: none -> 3.43 us  [sum_terms(): terms.append(lax.ppermute(value, axis, pairs))]
    ppermute x4 -> x1, waiting for transfers between devices: 3 us -> 1.15 us  [fetch(): return lax.ppermute(value, axis, pairs)]
    ppermute x0 -> x3, waiting for transfers between devices: none -> 1.84 us  [sum_terms(): terms.append(lax.ppermute(value, axis, pairs))]
  transfers between devices with their start and end apart: 9 -> 9, of which waited for: 4 -> 3; matrix products, arithmetic and copies ran while one was open for 0% -> 0% of each run, Pallas kernels for 14% -> 14%
where the time goes in v7:
time: 33.3 us; the launch traced here: 33.1 us
  Pallas kernels  15.3 us (46%)
  starting transfers between devices  13.1 us (39%)
  waiting for transfers between devices  3.01 us (9%)
  local copies, waits for them, and re-layouts  0.94 us (3%)
  between operations  0.74 us (2%)
    pallas_call x1, Pallas kernels, body(): pl.pallas_call(functools.partial(late_kernel, plan), out_shape=(pltpu.VME...  8.98 us
    ppermute x3, starting transfers between devices, body(): lax.ppermute(both, 'gy', [((i + s) % ny, i) for i in range(ny)])  7.01 us
    ppermute x3, starting transfers between devices, sum_terms(): terms.append(lax.ppermute(value, axis, pairs))  3.43 us
    pallas_call x1, Pallas kernels, body(): pl.pallas_call(functools.partial(early_kernel, plan), out_shape=(field_ty...  3.27 us
    ppermute x2, starting transfers between devices, swap_neighbours(): return lax.ppermute(value, axis, pairs)  2.62 us
    ppermute x3, waiting for transfers between devices, sum_terms(): terms.append(lax.ppermute(value, axis, pairs))  1.84 us
    pallas_call x1, Pallas kernels, body(): pl.pallas_call(functools.partial(bands_kernel, plan), out_shape=pltpu.VME...  1.5 us
    ppermute x1, waiting for transfers between devices, fetch(): return lax.ppermute(value, axis, pairs)  1.15 us
  transfers between devices with their start and end apart: 9, of which 3 were waited for; matrix products, arithmetic and copies ran while one was open for 0% of the time, Pallas kernels for 14%

profile of v7, /device:TPU:0, one launch (start us, length us, event | category | flops | bytes accessed | tf_op | source)
XLA Modules:
  0.0 33.1 jit_solution(2561105689065318284)
XLA Ops:
  0.6 0.8 %pack.1 = (bf16[80,128]{1,0:T(8,128)(2,1)S(1)}, f32[40,128]{1,0:T(8,128)S(1)}) custom-call(f32[40,128]{1,0:T(8,128)} %mask.1, s32[40,128]{1,0:T(8,128)} %target.1), custom_call_target="tpu_custom_call" | custom-call | tf_op jit(solution)/shard_map/pack/pallas_call | solution.py:547
  1.4 3.1 %collective-permute-start.2 = (bf16[80,128]{1,0:T(8,128)(2,1)S(1)}, bf16[80,128]{1,0:T(8,128)(2,1)S(1)}, u32[]{:S(2)}, u32[]{:S(2)}) collective-permute-start(bf16[80,128]{1,0:T(8,128)(2,1)S(1)} %get-tuple-element.14.refs_0_), channel_id=1, source_target_pairs={{24,0},{0,8},{8,16},{16,24},{25,1},{1,9},{9,17},{17,25},{26,2},{2,... | collective-permute-start | bytes 61448 | tf_op jit(solution)/shard_map/ppermute | solution.py:562
  4.5 2.6 %collective-permute-start.1 = (bf16[80,128]{1,0:T(8,128)(2,1)S(1)}, bf16[80,128]{1,0:T(8,128)(2,1)S(1)}, u32[]{:S(2)}, u32[]{:S(2)}) collective-permute-start(bf16[80,128]{1,0:T(8,128)(2,1)S(1)} %get-tuple-element.14.refs_0_), channel_id=1, source_target_pairs={{16,0},{24,8},{0,16},{8,24},{17,1},{25,9},{1,17},{9,25},{18,2},{26... | collective-permute-start | bytes 61448 | tf_op jit(solution)/shard_map/ppermute | solution.py:562
  7.1 1.3 %collective-permute-start = (bf16[80,128]{1,0:T(8,128)(2,1)S(1)}, bf16[80,128]{1,0:T(8,128)(2,1)S(1)}, u32[]{:S(2)}, u32[]{:S(2)}) collective-permute-start(bf16[80,128]{1,0:T(8,128)(2,1)S(1)} %get-tuple-element.14.refs_0_), channel_id=1, source_target_pairs={{8,0},{16,8},{24,16},{0,24},{9,1},{17,9},{25,17},{1,25},{10,2},{18... | collective-permute-start | bytes 61448 | tf_op jit(solution)/shard_map/ppermute | solution.py:562
  8.4 0.0 copy-start
  8.4 0.9 %copy-done = bf16[24,35,35]{2,0,1:T(8,128)(2,1)S(1)} copy-done((bf16[24,35,35]{2,0,1:T(8,128)(2,1)S(1)}, bf16[24,35,35]{2,0,1:T(8,128)(2,1)}, u32[]{:S(2)}) %copy-start) | copy-done | bytes 58824
  9.4 1.5 %bands.1.refs_4_ = bf16[768,2304]{1,0:T(8,128)(2,1)S(1)} custom-call(bf16[35,24,35]{2,1,0:T(8,128)(2,1)S(1)} %bitcast.4), custom_call_target="tpu_custom_call" | custom-call | flops 2000000000 | tf_op jit(solution)/shard_map/bands/pallas_call | solution.py:564
  10.9 0.0 collective-permute-done.2.refs_3_
  10.9 0.0 collective-permute-done.1.refs_2_
  10.9 0.0 collective-permute-done.refs_1_
  10.9 0.1 strip.1
  11.0 0.1 collective-permute-start.3
  11.1 2.5 %collective-permute-start.4 = (bf16[160,128]{1,0:T(8,128)(2,1)S(1)}, bf16[160,128]{1,0:T(8,128)(2,1)S(1)}, u32[]{:S(2)}, u32[]{:S(2)}) collective-permute-start(bf16[160,128]{1,0:T(8,128)(2,1)S(1)} %get-tuple-element.17), channel_id=1, source_target_pairs={{1,2},{2,1},{3,4},{4,3},{5,6},{6,5},{0,7},{7,0},{9,10},{10,9},{11,... | collective-permute-start | bytes 122888 | tf_op jit(solution)/shard_map/ppermute | solution.py:510
  13.7 0.0 collective-permute-done.3.near
  13.7 0.0 copy-start.1
  13.7 0.0 copy-start.2
  13.7 3.3 %early.1 = (f32[1120,768]{1,0:T(8,128)S(1)}, f32[1120,128]{1,0:T(8,128)S(1)}) custom-call(bf16[320,128]{1,0:T(8,128)(2,1)S(1)} %get-tuple-element.15.own, bf16[160,128]{1,0:T(8,128)(2,1)S(1)} %collective-permute-done.3.near, bf16[768,2304]{1,0:T(8,128)(2,1)S(1)} %bands.1.refs_4_), custom_call_target="tpu_custom_call" | custom-call | flops 3500000000 | tf_op jit(solution)/shard_map/early/pallas_call | solution.py:605
  16.9 0.0 collective-permute-done.4.far
  16.9 0.0 copy-done.1
  16.9 0.0 copy-done.2
  17.0 9.0 %late.1 = (f32[40,128]{1,0:T(8,128)S(1)}, f32[8,128]{1,0:T(8,128)S(1)}, f32[1120,768]{1,0:T(8,128)S(1)}, f32[1120,128]{1,0:T(8,128)S(1)}) custom-call(s32[2,8]{1,0:T(2,128)S(1)} %bitcast.5, f32[1,8]{1,0:T(1,128)S(1)} %bitcast.6, bf16[320,128]{1,0:T(8,128)(2,1)S(1)} %get-tuple-element.15.own, ...), custom_call_target="tpu_custom_call", output_to_operand_aliasing={{2}: (6, {}), {3}: (7, {})} | custom-call | flops 12000000000 | tf_op jit(solution)/shard_map/late/pallas_call | solution.py:619
  25.9 0.1 collective-permute-start.5
  26.0 1.2 %collective-permute-done.5 = f32[8,128]{1,0:T(8,128)S(1)} collective-permute-done((f32[8,128]{1,0:T(8,128)S(1)}, f32[8,128]{1,0:T(8,128)S(1)}, u32[]{:S(2)}, u32[]{:S(2)}) %collective-permute-start.5) | collective-permute-done | bytes 4128 | tf_op jit(solution)/shard_map/ppermute | solution.py:501
  27.2 0.3 collective-permute-start.8
  27.4 1.4 %collective-permute-start.7 = (f32[8,128]{1,0:T(8,128)S(1)}, f32[8,128]{1,0:T(8,128)S(1)}, u32[]{:S(2)}, u32[]{:S(2)}) collective-permute-start(f32[8,128]{1,0:T(8,128)S(1)} %add.3.refs_0_), channel_id=1, source_target_pairs={{4,0},{5,1},{6,2},{7,3},{0,4},{1,5},{2,6},{3,7},{12,8},{13,9},{14,... | collective-permute-start | bytes 12296 | tf_op jit(solution)/shard_map/ppermute | solution.py:524
  28.9 1.8 %collective-permute-start.6 = (f32[8,128]{1,0:T(8,128)S(1)}, f32[8,128]{1,0:T(8,128)S(1)}, u32[]{:S(2)}, u32[]{:S(2)}) collective-permute-start(f32[8,128]{1,0:T(8,128)S(1)} %add.3.refs_0_), channel_id=1, source_target_pairs={{2,0},{3,1},{4,2},{5,3},{6,4},{7,5},{0,6},{1,7},{10,8},{11,9},{12,... | collective-permute-start | bytes 12296 | tf_op jit(solution)/shard_map/ppermute | solution.py:524
  30.6 1.1 %collective-permute-done.8.refs_3_ = f32[8,128]{1,0:T(8,128)S(1)} collective-permute-done((f32[8,128]{1,0:T(8,128)S(1)}, f32[8,128]{1,0:T(8,128)S(1)}, u32[]{:S(2)}, u32[]{:S(2)}) %collective-permute-start.8) | collective-permute-done | bytes 4128 | tf_op jit(solution)/shard_map/ppermute | solution.py:524
  31.7 0.0 collective-permute-done.7.refs_2_
  31.7 0.8 %collective-permute-done.6.refs_1_ = f32[8,128]{1,0:T(8,128)S(1)} collective-permute-done((f32[8,128]{1,0:T(8,128)S(1)}, f32[8,128]{1,0:T(8,128)S(1)}, u32[]{:S(2)}, u32[]{:S(2)}) %collective-permute-start.6) | collective-permute-done | bytes 4128 | tf_op jit(solution)/shard_map/ppermute | solution.py:524
  32.5 0.6 %update.1 = (f32[40,128]{1,0:T(8,128)}, f32[1,1]{1,0:T(1,128)}) custom-call(f32[40,128]{1,0:T(8,128)S(1)} %get-tuple-element.13.mask, f32[40,128]{1,0:T(8,128)S(1)} %get-tuple-element.20.grad, f32[8,128]{1,0:T(8,128)S(1)} %add.3.refs_0_, f32[8,128]{1,0:T(8,128)S(1)} %collective-permute-done.6.refs_1_, f32[8,128]{1,0:T(8,128)S(1)} %collective-permute-done.7.refs_2_, ...), custom_call_target="tpu_custom_call" | custom-call | tf_op jit(solution)/shard_map/update/pallas_call | solution.py:650
  (1 shorter events, 0.0 us)
Async XLA Ops:
  1.4 9.5 %collective-permute-start.2 = (bf16[80,128]{1,0:T(8,128)(2,1)S(1)}, bf16[80,128]{1,0:T(8,128)(2,1)S(1)}, u32[]{:S(2)}, u32[]{:S(2)}) collective-permute-start(bf16[80,128]{1,0:T(8,128)(2,1)S(1)} %get-tuple-element.14.refs_0_), channel_id=1, source_target_pairs={{24,0},{0,8},{8,16},{16,24},{25,1},{1,9},{9,17},{17,25},{26,2},{2,... | collective-permute-start | bytes 61448 | tf_op jit(solution)/shard_map/ppermute | solution.py:562
  4.5 6.4 %collective-permute-start.1 = (bf16[80,128]{1,0:T(8,128)(2,1)S(1)}, bf16[80,128]{1,0:T(8,128)(2,1)S(1)}, u32[]{:S(2)}, u32[]{:S(2)}) collective-permute-start(bf16[80,128]{1,0:T(8,128)(2,1)S(1)} %get-tuple-element.14.refs_0_), channel_id=1, source_target_pairs={{16,0},{24,8},{0,16},{8,24},{17,1},{25,9},{1,17},{9,25},{18,2},{26... | collective-permute-start | bytes 61448 | tf_op jit(solution)/shard_map/ppermute | solution.py:562
  7.1 3.8 %collective-permute-start = (bf16[80,128]{1,0:T(8,128)(2,1)S(1)}, bf16[80,128]{1,0:T(8,128)(2,1)S(1)}, u32[]{:S(2)}, u32[]{:S(2)}) collective-permute-start(bf16[80,128]{1,0:T(8,128)(2,1)S(1)} %get-tuple-element.14.refs_0_), channel_id=1, source_target_pairs={{8,0},{16,8},{24,16},{0,24},{9,1},{17,9},{25,17},{1,25},{10,2},{18... | collective-permute-start | bytes 61448 | tf_op jit(solution)/shard_map/ppermute | solution.py:562
  8.4 0.9 %copy-start = (bf16[24,35,35]{2,0,1:T(8,128)(2,1)S(1)}, bf16[24,35,35]{2,0,1:T(8,128)(2,1)}, u32[]{:S(2)}) copy-start(bf16[24,35,35]{2,0,1:T(8,128)(2,1)} %param.7) | copy-start | bytes 176404
  11.0 2.6 %collective-permute-start.3 = (bf16[160,128]{1,0:T(8,128)(2,1)S(1)}, bf16[160,128]{1,0:T(8,128)(2,1)S(1)}, u32[]{:S(2)}, u32[]{:S(2)}) collective-permute-start(bf16[160,128]{1,0:T(8,128)(2,1)S(1)} %get-tuple-element.16), channel_id=1, source_target_pairs={{0,1},{1,0},{2,3},{3,2},{4,5},{5,4},{6,7},{7,6},{8,9},{9,8},{10,11... | collective-permute-start | bytes 122888 | tf_op jit(solution)/shard_map/ppermute | solution.py:510
  11.1 5.8 %collective-permute-start.4 = (bf16[160,128]{1,0:T(8,128)(2,1)S(1)}, bf16[160,128]{1,0:T(8,128)(2,1)S(1)}, u32[]{:S(2)}, u32[]{:S(2)}) collective-permute-start(bf16[160,128]{1,0:T(8,128)(2,1)S(1)} %get-tuple-element.17), channel_id=1, source_target_pairs={{1,2},{2,1},{3,4},{4,3},{5,6},{6,5},{0,7},{7,0},{9,10},{10,9},{11,... | collective-permute-start | bytes 122888 | tf_op jit(solution)/shard_map/ppermute | solution.py:510
  13.7 3.3 %copy-start.1 = (s32[8,2]{0,1:T(2,128)S(1)}, s32[8,2]{0,1:T(2,128)}, u32[]{:S(2)}) copy-start(s32[8,2]{0,1:T(2,128)} %param.8) | copy-start | bytes 196
  13.7 3.3 %copy-start.2 = (f32[8]{0:T(128)S(1)}, f32[8]{0:T(128)}, u32[]{:S(2)}) copy-start(f32[8]{0:T(128)} %param.9) | copy-start | bytes 100
  25.9 1.2 %collective-permute-start.5 = (f32[8,128]{1,0:T(8,128)S(1)}, f32[8,128]{1,0:T(8,128)S(1)}, u32[]{:S(2)}, u32[]{:S(2)}) collective-permute-start(f32[8,128]{1,0:T(8,128)S(1)} %get-tuple-element.21), channel_id=1, source_target_pairs={{0,1},{1,0},{2,3},{3,2},{4,5},{5,4},{6,7},{7,6},{8,9},{9,8},{10,11... | collective-permute-start | bytes 12296 | tf_op jit(solution)/shard_map/ppermute | solution.py:501
  27.2 4.5 %collective-permute-start.8 = (f32[8,128]{1,0:T(8,128)S(1)}, f32[8,128]{1,0:T(8,128)S(1)}, u32[]{:S(2)}, u32[]{:S(2)}) collective-permute-start(f32[8,128]{1,0:T(8,128)S(1)} %add.3.refs_0_), channel_id=1, source_target_pairs={{6,0},{7,1},{0,2},{1,3},{2,4},{3,5},{4,6},{5,7},{14,8},{15,9},{8,1... | collective-permute-start | bytes 12296 | tf_op jit(solution)/shard_map/ppermute | solution.py:524
  27.4 4.2 %collective-permute-start.7 = (f32[8,128]{1,0:T(8,128)S(1)}, f32[8,128]{1,0:T(8,128)S(1)}, u32[]{:S(2)}, u32[]{:S(2)}) collective-permute-start(f32[8,128]{1,0:T(8,128)S(1)} %add.3.refs_0_), channel_id=1, source_target_pairs={{4,0},{5,1},{6,2},{7,3},{0,4},{1,5},{2,6},{3,7},{12,8},{13,9},{14,... | collective-permute-start | bytes 12296 | tf_op jit(solution)/shard_map/ppermute | solution.py:524
  28.9 3.6 %collective-permute-start.6 = (f32[8,128]{1,0:T(8,128)S(1)}, f32[8,128]{1,0:T(8,128)S(1)}, u32[]{:S(2)}, u32[]{:S(2)}) collective-permute-start(f32[8,128]{1,0:T(8,128)S(1)} %add.3.refs_0_), channel_id=1, source_target_pairs={{2,0},{3,1},{4,2},{5,3},{6,4},{7,5},{0,6},{1,7},{10,8},{11,9},{12,... | collective-permute-start | bytes 12296 | tf_op jit(solution)/shard_map/ppermute | solution.py:524
